TPU v7x, 32 devices: a whole 2x2x4 slice. The times are simulated.
32 devices in a mesh: dp: 4 (over y, x), ctx: 8 (over z, core).
Axes of the slice: x: 2, y: 2, z: 4, core: 2. Of those that a mesh axis runs over, the one named last changes fastest.
Arguments:
- projected: bfloat16 [4, 1024, 12288], P('dp', 'ctx'), may hold values from -6 to 6
- doc_ids: int32 [4, 1024], P('dp'), may hold values from 0 to 15, never falling along the last dimension, each value on 1 to 128 neighbouring positions
- short_filter: float32 [3, 12288], replicated, may hold values from -3.5 to 3.5
- long_filter: bfloat16 [256, 128], replicated, may hold values from -0.5 to 0.5
- cotangent: bfloat16 [4, 1024, 4096], P('dp', 'ctx'), may hold values from -6 to 6
Outputs:
- block_out: bfloat16 [4, 1024, 4096], P('dp', 'ctx')
- grad_projected: bfloat16 [4, 1024, 12288], P('dp', 'ctx')
- grad_short: float32 [3, 12288], P(None, 'ctx')
- grad_long: float32 [256, 128], P('ctx')
Inputs may be any that keep to these rules, and one draw needn't show every extreme that they name: `doc_ids`: document numbers never fall along a row, each document spans 1 to 128 positions, and some document spans exactly 128.
All inputs are finite; a program needn't handle non-finite values.
Results may differ from a plain program's by a relative error of at most 0.0076.
Values may be sent and summed in bfloat16 or wider, within the bound.
No kernel may reach another device: no remote copies, remote signals or barrier semaphores. Data moves between devices by JAX's collectives and lax.ppermute only.
A program may use at most 256 MiB of HBM per device.

v0:
```python
import math

import jax
import jax.numpy as jnp
from jax import lax
from jax.sharding import PartitionSpec as P


def passed_along(value, axis, steps):
    count = lax.axis_size(axis)
    initial, last = (max(0, -steps), min(count, count - steps))
    return lax.ppermute(value, axis, [(source, source + steps) for source in range(initial, last)])


def doc_offsets(seg_row):
    length = seg_row.shape[0]
    places = jnp.arange(length, dtype=jnp.int32)
    starts_here = jnp.concatenate([jnp.ones((1,), bool), seg_row[1:] != seg_row[:-1]])
    return places - lax.cummax(jnp.where(starts_here, places, 0), axis=0)


def toeplitz(filters):
    groups, tap_count = filters.shape
    widened = jnp.concatenate(
        [
            jnp.zeros((groups, tap_count), filters.dtype),
            filters[:, ::-1],
            jnp.zeros((groups, tap_count - 1), filters.dtype),
        ],
        axis=1,
    )
    tiled_rows = jnp.tile(widened, (1, tap_count))
    span_len = 3 * tap_count - 2
    return tiled_rows[:, tap_count - 1 : tap_count - 1 + tap_count * span_len].reshape(
        groups, tap_count, span_len
    )[:, :, : 2 * tap_count]


def band_keep(offsets, tap_count):
    blocks = offsets.shape[0] // tap_count
    row_ids = jnp.arange(tap_count, dtype=jnp.int32)[:, None]
    col_ids = jnp.arange(2 * tap_count, dtype=jnp.int32)[None, :]
    return (row_ids + tap_count - col_ids)[None] <= offsets.reshape(blocks, tap_count)[:, :, None]


def group_tiles(values, group_step):
    blocks, rows, groups, width = values.shape
    tiled = values.reshape(blocks, rows, groups // group_step, group_step, width).transpose(
        0, 2, 1, 3, 4
    )
    return tiled.reshape(blocks * (groups // group_step), rows, group_step, width)


def group_untile(values, blocks):
    items, rows, group_step, width = values.shape
    tile_count = items // blocks
    placed = values.reshape(blocks, tile_count, rows, group_step, width).transpose(0, 2, 1, 3, 4)
    return placed.reshape(blocks, rows, tile_count * group_step, width)


def long_forward(source, offsets, kernel):
    groups, tap_count = (kernel.shape[0], kernel.shape[1])
    blocks = offsets.shape[0] // tap_count
    group_step = min(groups, 16)
    tile_count = groups // group_step
    shaped = source.reshape(blocks + 1, tap_count, groups, -1)
    windows = jnp.concatenate([shaped[:-1], shaped[1:]], axis=1)
    keep_all = band_keep(offsets, tap_count).astype(jnp.bfloat16)
    kernel_tiles = kernel.reshape(tile_count, group_step, tap_count, 2 * tap_count)
    window_tiles = group_tiles(windows, group_step)

    def one_tile(item):
        piece, index = item
        masked = kernel_tiles[index % tile_count] * keep_all[index // tile_count][None]
        return jnp.einsum("gis,sgc->igc", masked, piece, preferred_element_type=jnp.float32)

    mixed_tiles = lax.map(
        one_tile, (window_tiles, jnp.arange(blocks * tile_count, dtype=jnp.int32))
    )
    return (group_untile(mixed_tiles, blocks).reshape(blocks * tap_count, -1), window_tiles)


def long_backward(grads_ext, offsets_ext, kernel, window_tiles, filters):
    groups, tap_count = (kernel.shape[0], kernel.shape[1])
    out_blocks = offsets_ext.shape[0] // tap_count
    group_step = min(groups, 16)
    tile_count = groups // group_step
    keep_all = band_keep(offsets_ext, tap_count).astype(jnp.bfloat16)
    kernel_tiles = kernel.reshape(tile_count, group_step, tap_count, 2 * tap_count)
    filter_tiles = filters.reshape(tile_count, group_step, tap_count)
    grad_tiles = group_tiles(grads_ext.reshape(out_blocks, tap_count, groups, -1), group_step)
    padded_windows = jnp.concatenate(
        [window_tiles, jnp.zeros((tile_count,) + window_tiles.shape[1:], window_tiles.dtype)],
        axis=0,
    )

    def one_tile(carry, item):
        grad_piece, window_piece, index = item
        tile_id = index % tile_count
        keep_block = keep_all[index // tile_count]
        masked = kernel_tiles[tile_id] * keep_block[None]
        spread = jnp.einsum("gis,igc->sgc", masked, grad_piece, preferred_element_type=jnp.float32)
        inner_prod = jnp.einsum(
            "igc,sgc->gis", grad_piece, window_piece, preferred_element_type=jnp.float32
        )
        inner_prod = inner_prod * keep_block.astype(jnp.float32)[None]
        _, pull_back = jax.vjp(toeplitz, filter_tiles[tile_id])
        carry = carry.at[tile_id].add(pull_back(inner_prod)[0])
        return (carry, spread)

    start_grad = jnp.zeros((tile_count, group_step, tap_count), jnp.float32)
    kernel_grad, spread_tiles = lax.scan(
        one_tile,
        start_grad,
        (grad_tiles, padded_windows, jnp.arange(out_blocks * tile_count, dtype=jnp.int32)),
    )
    spread = group_untile(spread_tiles, out_blocks)
    back_grad = spread[:-1, tap_count:] + spread[1:, :tap_count]
    return (
        back_grad.reshape((out_blocks - 1) * tap_count, -1),
        kernel_grad.reshape(groups, tap_count),
    )


def short_forward(extended, weights, offsets):
    short_taps = weights.shape[0]
    tok_count = offsets.shape[0]
    running = jnp.zeros((tok_count, extended.shape[1]), jnp.float32)
    for tap_pos in range(short_taps):
        shifted = extended[short_taps - 1 - tap_pos : short_taps - 1 - tap_pos + tok_count].astype(
            jnp.float32
        )
        running = running + jnp.where(
            (offsets >= tap_pos)[:, None], weights[tap_pos][None, :] * shifted, 0.0
        )
    return running


def short_backward(grads_ext, offsets_ext, extended, weights, offsets):
    short_taps = weights.shape[0]
    tok_count = offsets.shape[0]
    running = jnp.zeros((tok_count, extended.shape[1]), jnp.float32)
    pieces = []
    for tap_pos in range(short_taps):
        ahead_part = grads_ext[tap_pos : tap_pos + tok_count].astype(jnp.float32)
        keep_mask = (offsets_ext[tap_pos : tap_pos + tok_count] >= tap_pos)[:, None]
        running = running + jnp.where(keep_mask, weights[tap_pos][None, :] * ahead_part, 0.0)
        shifted = extended[short_taps - 1 - tap_pos : short_taps - 1 - tap_pos + tok_count].astype(
            jnp.float32
        )
        local_grad = grads_ext[:tok_count].astype(jnp.float32)
        pieces.append(
            jnp.sum(jnp.where((offsets >= tap_pos)[:, None], local_grad * shifted, 0.0), axis=0)
        )
    return (running, jnp.stack(pieces, axis=0))


def local(projected, doc_ids, short_filter, long_filter, cotangent):
    inputs_row = projected[0]
    grad_row = cotangent[0]
    seg_row = doc_ids[0]
    tok_count = inputs_row.shape[0]
    model_width = grad_row.shape[1]
    groups_total, tap_count = long_filter.shape
    short_taps = short_filter.shape[0]
    length = seg_row.shape[0]
    my_index = lax.axis_index("ctx")
    ctx_parts = lax.axis_size("ctx")
    first_row = my_index * tok_count
    offs_all = doc_offsets(seg_row)
    offs_pad = jnp.concatenate([offs_all, jnp.zeros((tap_count,), jnp.int32)])
    offs_local = lax.dynamic_slice_in_dim(offs_pad, first_row, tok_count, 0)
    offs_after = lax.dynamic_slice_in_dim(offs_pad, first_row + tok_count, tap_count, 0)
    border = passed_along(inputs_row[tok_count - (short_taps - 1) :], "ctx", 1)
    extended = jnp.concatenate([border, inputs_row], axis=0)
    mixed_in = short_forward(extended, short_filter, offs_local).astype(jnp.bfloat16)
    queries = mixed_in[:, :model_width]
    key_part = mixed_in[:, model_width : 2 * model_width]
    value_part = mixed_in[:, 2 * model_width :]
    product = (key_part.astype(jnp.float32) * value_part.astype(jnp.float32)).astype(jnp.bfloat16)
    grad_mix = (grad_row.astype(jnp.float32) * queries.astype(jnp.float32)).astype(jnp.bfloat16)
    local_groups = groups_total // ctx_parts
    local_filters = lax.dynamic_slice_in_dim(long_filter, my_index * local_groups, local_groups, 0)
    kernel = toeplitz(local_filters)
    channels = lax.all_to_all(product, "ctx", split_axis=1, concat_axis=0, tiled=True)
    lead_zeros = jnp.zeros((tap_count, channels.shape[1]), jnp.bfloat16)
    mixed_ch, windows = long_forward(
        jnp.concatenate([lead_zeros, channels], axis=0), offs_all, kernel
    )
    long_mix = lax.all_to_all(
        mixed_ch.astype(jnp.bfloat16), "ctx", split_axis=0, concat_axis=1, tiled=True
    )
    grads_ch = lax.all_to_all(grad_mix, "ctx", split_axis=1, concat_axis=0, tiled=True)
    back_ch, kernel_grad = long_backward(
        jnp.concatenate([grads_ch, lead_zeros], axis=0),
        offs_pad,
        kernel,
        windows,
        local_filters.astype(jnp.float32),
    )
    grad_product = lax.all_to_all(
        back_ch.astype(jnp.bfloat16), "ctx", split_axis=0, concat_axis=1, tiled=True
    )
    block_out = (queries.astype(jnp.float32) * long_mix.astype(jnp.float32)).astype(jnp.bfloat16)
    grad_queries = (grad_row.astype(jnp.float32) * long_mix.astype(jnp.float32)).astype(
        jnp.bfloat16
    )
    grad_keys = (grad_product.astype(jnp.float32) * value_part.astype(jnp.float32)).astype(
        jnp.bfloat16
    )
    grad_values = (grad_product.astype(jnp.float32) * key_part.astype(jnp.float32)).astype(
        jnp.bfloat16
    )
    mixed_grad = jnp.concatenate([grad_queries, grad_keys, grad_values], axis=1)
    ahead_rows = passed_along(mixed_grad[: short_taps - 1], "ctx", -1)
    offs_short = jnp.concatenate([offs_local, offs_after[: short_taps - 1]], axis=0)
    grad_inputs, weight_grad = short_backward(
        jnp.concatenate([mixed_grad, ahead_rows], axis=0),
        offs_short,
        extended,
        short_filter,
        offs_local,
    )
    weight_part = lax.psum_scatter(weight_grad, "ctx", scatter_dimension=1, tiled=True)
    weight_total, filter_total = lax.psum((weight_part, kernel_grad), "dp")
    norm_scale = lax.axis_size("dp") * length
    group_size = model_width // groups_total
    grad_short = weight_total / math.sqrt(norm_scale)
    grad_long = filter_total / math.sqrt(norm_scale * group_size)
    return (block_out[None], grad_inputs.astype(jnp.bfloat16)[None], grad_short, grad_long)


def solution(mesh):
    return jax.shard_map(
        local,
        mesh=mesh,
        in_specs=(P("dp", "ctx", None), P("dp", None), P(), P(), P("dp", "ctx", None)),
        out_specs=(P("dp", "ctx", None), P("dp", "ctx", None), P(None, "ctx"), P("ctx", None)),
        check_vma=False,
    )
```

profile of v0, /device:TPU:0, one launch (start us, length us, event | category | flops | bytes accessed | tf_op | source)
XLA Modules:
  0.0 795.4 jit_solution(12384447954054302385)
XLA Ops:
  22.7 10.2 %fusion.21 = bf16[128,12288]{0,1:T(8,128)(2,1)S(1)} fusion(bf16[128,12288]{0,1:T(8,128)(2,1)S(1)} %bitcast.138, f32[12288]{0:T(1024)S(1)} %bitcast.155, f32[12288]{0:T(1024)S(1)} %bitcast.157, f32[12288]{0:T(1024)S(1)} %bitcast.153, pred[128]{0:T(512)(128)(4,1)S(1)} %get-tuple-element.305, pred[128]{0:T(512)(128)(4,1)S(1)} %get-tuple-element.304, ...), kind=kLoop, calls=%fused_computation.37 | loop fusion | flops 28311552 | bytes 6488448 | tf_op jit(solution)/shard_map/convert_element_type | solution.py:176
  35.0 32.6 %all_to_all.58 = bf16[128,8,512]{0,2,1:T(8,128)(2,1)} all-to-all(bf16[128,8,512]{0,2,1:T(8,128)(2,1)S(1)} %bitcast.150), channel_id=1, replica_groups=mesh['dp'=4,'ctx'=8] {'ctx'}, dimensions={1} | all-to-all | bytes 2097152 | tf_op jit(solution)/shard_map/all_to_all | solution.py:193
  72.5 4.7 tile.10
  80.0 9.0 %reshape.196 = bf16[32,128,382]{2,1,0:T(8,128)(2,1)} reshape(bf16[32,48896]{1,0:T(8,128)(2,1)S(1)} %slice.152) | data formatting | bytes 6258688 | tf_op jit(solution)/shard_map/reshape | solution.py:34
  110.3 99.2 %while.27 = (s32[]{:T(128)}, bf16[16,128,16,16]{1,3,2,0:T(8,128)(2,1)}, bf16[16,256,16,16]{1,3,2,0:T(8,128)(2,1)S(1)}, s32[16]{0:T(128)S(1)}, bf16[2,16,128,256]...) while((s32[]{:T(128)}, ...), condition=%wide.region_3.4_spmd, body=%wide.region_2.3_spmd.sunk | while | flops 17301532 | bytes 1509252 | solution.py:77
  214.1 395.2 %while.28 = (s32[]{:T(128)}, f32[2,16,128]{2,1,0:T(8,128)S(1)}, f32[18,256,16,16]{1,3,2,0:T(8,128)}, s32[18]{0:T(128)S(1)}, bf16[18,128,16,16]{1,3,2,0:T(8,128)(...) while((s32[]{:T(128)}, f32[2,16,128]{2,1,0:T(8,128)S(1)}, ...), condition=%wide.region_7.8_spmd, body=%wide.region_4.7_spmd.sunk | while | flops 35418172 | bytes 31378320 | solution.py:112
  223.6 4.5 pad.121
  228.1 4.7 reshape.212
  245.5 4.5 pad.121
  250.0 4.7 reshape.212
  267.5 4.5 pad.121
  272.0 4.7 reshape.212
  289.4 4.5 pad.121
  293.9 4.7 reshape.212
  311.4 4.5 pad.121
  315.9 4.7 reshape.212
  333.3 4.5 pad.121
  337.8 4.7 reshape.212
  355.3 4.5 pad.121
  359.8 4.7 reshape.212
  377.2 4.5 pad.121
  381.8 4.7 reshape.212
  399.2 4.5 pad.121
  403.7 4.7 reshape.212
  421.1 4.5 pad.121
  425.7 4.7 reshape.212
  443.1 4.5 pad.121
  447.6 4.7 reshape.212
  465.1 4.5 pad.121
  469.6 4.7 reshape.212
  487.0 4.5 pad.121
  491.5 4.7 reshape.212
  509.0 4.5 pad.121
  513.5 4.7 reshape.212
  535.4 4.7 reshape.212
  557.4 4.7 reshape.212
  579.3 4.7 reshape.212
  601.3 4.7 reshape.212
  612.7 5.1 all-to-all-start.3
  618.0 26.5 %all-to-all-done.3 = bf16[8,128,512]{1,2,0:T(8,128)(2,1)} async-done(((bf16[8,128,512]{1,2,0:T(8,128)(2,1)}), bf16[8,128,512]{1,2,0:T(8,128)(2,1)}, u32[]{:S(2)}, u32[]{:S(2)}) %all-to-all-start.3) | async-done | bytes 1048608 | tf_op jit(solution)/shard_map/all_to_all | solution.py:201
  644.5 4.9 fusion.39
  649.4 23.8 %fusion.31 = (f32[12288]{0:T(1024)S(1)}, f32[12288]{0:T(1024)S(1)}, f32[12288]{0:T(1024)S(1)}) fusion(pred[128]{0:T(512)(128)(4,1)S(1)} %get-tuple-element.304, bf16[128,12288]{0,1:T(8,128)(2,1)S(1)} %bitcast.139, bf16[2,12288]{0,1:T(8,128)(2,1)S(1)} %copy-done.4, bf16[128,4096]{0,1:T(8,128)(2,1)S(1)} %get-tuple-element.292, ...), kind=kLoop, calls=%fused_computation.47 | loop fusion | flops 37711872 | bytes 9634176 | tf_op jit(solution)/shard_map/reduce_sum | solution.py:153
  673.2 15.7 %pad_maximum_fusion.2 = bf16[128,12288]{0,1:T(8,128)(2,1)S(1)} fusion(bf16[128,4096]{0,1:T(8,128)(2,1)S(1)} %get-tuple-element.292, bf16[128,4096]{0,1:T(8,128)(2,1)S(1)} %get-tuple-element.291, bf16[128,4096]{0,1:T(8,128)(2,1)S(1)} %get-tuple-element.298), kind=kLoop, calls=%fused_computation.56 | loop fusion | flops 9437184 | bytes 6291456 | tf_op jit(solution)/shard_map/concatenate | solution.py:214
  702.6 23.7 %pad_maximum_fusion = bf16[130,12288]{0,1:T(8,128)(2,1)S(1)} fusion(bf16[2,12288]{0,1:T(8,128)(2,1)} %copy.47, bf16[128,4096]{0,1:T(8,128)(2,1)S(1)} %copy-done.9, bf16[128,4096]{0,1:T(8,128)(2,1)S(1)} %copy-done.7, bf16[128,4096]{0,1:T(8,128)(2,1)S(1)} %copy-done.11), kind=kLoop, calls=%fused_computation.52 | loop fusion | flops 12779520 | bytes 6389760 | tf_op jit(solution)/shard_map/concatenate | solution.py:218
  726.4 25.5 %fusion.35 = bf16[1,128,12288]{1,2,0:T(8,128)(2,1)} fusion(bf16[130,12288]{0,1:T(8,128)(2,1)S(1)} %pad_maximum_fusion, f32[12288]{0:T(1024)S(1)} %bitcast.156, f32[12288]{0:T(1024)S(1)} %bitcast.158, f32[12288]{0:T(1024)S(1)} %bitcast.154, pred[128]{0:T(512)(128)(4,1)S(1)} %get-tuple-element.303, pred[128]{0:T(512)(128)(4,1)S(1)} %get-tuple-element.302, ...), kind=kLoop, calls=%fused_computation.54 | loop fusion | flops 26738688 | bytes 12730752 | tf_op jit(solution)/shard_map/broadcast_in_dim | solution.py:230
  751.9 4.7 copy.49
  756.5 12.6 %reduce-scatter.4.cloned.1.call-done = f32[1536,3]{1,0:T(8,128)} async-done(((f32[12288,3]{1,0:T(8,128)}), f32[1536,3]{1,0:T(8,128)}) %reduce-scatter.4.cloned.1.call-update) | async-done | bytes 18448
  770.6 16.6 %all-reduce.6 = (f32[3,1536]{1,0:T(4,128)S(1)}, f32[32,128]{1,0:T(8,128)S(1)}) all-reduce(f32[3,1536]{1,0:T(4,128)S(1)} %copy.51, f32[32,128]{1,0:T(8,128)S(1)} %bitcast.159), channel_id=1, replica_groups=mesh['dp'=4,'ctx'=8] {'dp'}, use_global_device_ids=true, to_apply=%region_12.13 | all-reduce | flops 8704 | bytes 69632 | tf_op jit(solution)/shard_map/psum | solution.py:225
  (354 shorter events, 328.0 us)
Async XLA Ops:
  7.2 65.0 %copy-start = (bf16[256,128]{1,0:T(8,128)(2,1)S(1)}, bf16[256,128]{1,0:T(8,128)(2,1)}, u32[]{:S(2)}) copy-start(bf16[256,128]{1,0:T(8,128)(2,1)} %param.14) | copy-start | bytes 196612
  8.2 11.7 %collective-permute-start = (bf16[2,12288]{1,0:T(2,128)(2,1)S(1)}, bf16[2,12288]{1,0:T(2,128)(2,1)S(1)}, u32[]{:S(2)}, u32[]{:S(2)}) collective-permute-start(bf16[2,12288]{1,0:T(2,128)(2,1)S(1)} %slice_bitcast_fusion), channel_id=1, source_target_pairs={{0,1},{1,2},{2,3},{3,4},{4,5},{5,6},{6,7},{8,9},{9,10},{10,11},{11... | collective-permute-start | bytes 147464 | tf_op jit(solution)/shard_map/ppermute | solution.py:12
  16.9 15.9 %copy-start.2 = (bf16[1,128,12288]{1,2,0:T(8,128)(2,1)}, bf16[1,128,12288]{1,2,0:T(8,128)(2,1)S(1)}, u32[]{:S(2)}) copy-start(bf16[1,128,12288]{1,2,0:T(8,128)(2,1)S(1)} %copy.35) | copy-start | bytes 9437188
  22.7 10.2 %copy-start.12 = (bf16[1,128,4096]{1,2,0:T(8,128)(2,1)S(1)}, bf16[1,128,4096]{1,2,0:T(8,128)(2,1)}, u32[]{:S(2)}) copy-start(bf16[1,128,4096]{1,2,0:T(8,128)(2,1)} %copy.41) | copy-start | bytes 3145732
  32.9 2.1 copy-start.5
  67.6 31.0 %all-to-all-start = ((bf16[128,8,512]{0,2,1:T(8,128)(2,1)}), bf16[128,8,512]{0,2,1:T(8,128)(2,1)}, u32[]{:S(2)}, u32[]{:S(2)}) async-start(bf16[128,8,512]{0,2,1:T(8,128)(2,1)} %bitcast.149), calls=%async_computation | async-start | bytes 2097152 | tf_op jit(solution)/shard_map/all_to_all | solution.py:185
  89.0 5.5 copy-start.13
  110.3 103.7 %copy-start.14 = (s32[3]{0:T(128)S(1)}, s32[3]{0:T(128)}, u32[]{:S(2)}) copy-start(s32[3]{0:T(128)} %constant.173.clone.1) | copy-start | bytes 40
  209.6 403.2 %all-to-all-start.1 = ((bf16[8,128,512]{1,2,0:T(8,128)(2,1)}), bf16[8,128,512]{1,2,0:T(8,128)(2,1)}, u32[]{:S(2)}, u32[]{:S(2)}) async-start(bf16[8,128,512]{1,2,0:T(8,128)(2,1)} %bitcast.29), calls=%async_computation.1 | async-start | bytes 2097152 | tf_op jit(solution)/shard_map/all_to_all | solution.py:190
  612.7 31.8 %all-to-all-start.3 = ((bf16[8,128,512]{1,2,0:T(8,128)(2,1)}), bf16[8,128,512]{1,2,0:T(8,128)(2,1)}, u32[]{:S(2)}, u32[]{:S(2)}) async-start(bf16[8,128,512]{1,2,0:T(8,128)(2,1)} %bitcast.47), calls=%async_computation.3 | async-start | bytes 2097152 | tf_op jit(solution)/shard_map/all_to_all | solution.py:201
  617.8 151.4 %reduce-scatter.4.cloned.1.call-start = ((), (), s32[]{:S(2)}) async-start(), calls=%async_computation.5 | async-start | bytes 7077888
  618.0 31.4 %copy-start.3 = (bf16[1,128,12288]{1,2,0:T(8,128)(2,1)S(1)}, bf16[1,128,12288]{1,2,0:T(8,128)(2,1)}, u32[]{:S(2)}) copy-start(bf16[1,128,12288]{1,2,0:T(8,128)(2,1)} %copy-done.2) | copy-start | bytes 9437188
  644.5 4.9 copy-start.4
  649.4 23.8 %copy-start.6 = (bf16[128,4096]{0,1:T(8,128)(2,1)}, bf16[128,4096]{0,1:T(8,128)(2,1)S(1)}, u32[]{:S(2)}) copy-start(bf16[128,4096]{0,1:T(8,128)(2,1)S(1)} %get-tuple-element.291) | copy-start | bytes 3145732
  649.4 23.8 %copy-start.8 = (bf16[128,4096]{0,1:T(8,128)(2,1)}, bf16[128,4096]{0,1:T(8,128)(2,1)S(1)}, u32[]{:S(2)}) copy-start(bf16[128,4096]{0,1:T(8,128)(2,1)S(1)} %get-tuple-element.292) | copy-start | bytes 3145732
  649.4 23.8 %copy-start.10 = (bf16[128,4096]{0,1:T(8,128)(2,1)}, bf16[128,4096]{0,1:T(8,128)(2,1)S(1)}, u32[]{:S(2)}) copy-start(bf16[128,4096]{0,1:T(8,128)(2,1)S(1)} %get-tuple-element.298) | copy-start | bytes 3145732
  691.0 7.9 collective-permute-start.1
  698.9 3.7 copy-start.7
  698.9 3.7 copy-start.9
  698.9 3.7 copy-start.11
  726.3 62.1 %copy-start.1 = (bf16[256,128]{1,0:T(8,128)(2,1)S(1)}, bf16[256,128]{1,0:T(8,128)(2,1)}, u32[]{:S(2)}) copy-start(bf16[256,128]{1,0:T(8,128)(2,1)} %param.14) | copy-start | bytes 196612
Sparse Core Ops, SparseCore 0:
  699.0 70.1 reduce-scatter.3
where the time goes:
time: 805 us; the launch traced here: 795 us
  local copies, waits for them, and re-layouts  325 us (40%)
  other arithmetic  159 us (20%)
  matrix products  102 us (13%)
  loops' own time  88.4 us (11%)
  blocking collectives  49.3 us (6%)
  waiting for transfers between devices  40 us (5%)
  starting transfers between devices  17.6 us (2%)
  between operations  14.7 us (2%)
    pad x36, local copies, waits for them, and re-layouts, toeplitz(): tiled_rows[:, tap_count - 1:tap_count - 1 + tap_count * span_len]  87.4 us
    reshape x18, local copies, waits for them, and re-layouts, toeplitz(): tiled_rows = jnp.tile(widened, (1, tap_count))  85.5 us
    reshape x19, local copies, waits for them, and re-layouts, toeplitz(): tiled_rows[:, tap_count - 1:tap_count - 1 + tap_count * span_len]  61.3 us
    another operation x1, loops' own time, long_backward(): lax.scan(one_tile, start_grad, (grad_tiles, padded_windows, jnp.arange(ou...  48.1 us
    another operation x1, loops' own time, long_forward(): lax.map(one_tile, (window_tiles, jnp.arange(blocks * tile_count, dtype=jn...  40.3 us
    dot_general x18, matrix products, one_tile(): jnp.einsum('gis,igc->sgc', masked, grad_piece, preferred_element_type=jnp...  40.1 us
    dot_general x16, matrix products, one_tile(): jnp.einsum('gis,sgc->igc', masked, piece, preferred_element_type=jnp.floa...  35.9 us
    all_to_all x1, blocking collectives, local(): lax.all_to_all(grad_mix, 'ctx', split_axis=1, concat_axis=0, tiled=True)  32.6 us
  transfers between devices with their start and end apart: 6, of which 3 were waited for; matrix products, arithmetic and copies ran while one was open for 57% of the time, Pallas kernels for 0%

commit v1 on v0

v1 whole, which is shorter than its diff:
```python
import math

import jax
import jax.numpy as jnp
from jax import lax
from jax.experimental import pallas as pl
from jax.experimental.pallas import tpu as pltpu
from jax.sharding import PartitionSpec as P

BF = jnp.bfloat16
F32 = jnp.float32
LANES = 128
EDGE = 16
VMEM = 48 * 1024 * 1024


def passed_along(value, axis, steps):
    count = lax.axis_size(axis)
    initial, last = (max(0, -steps), min(count, count - steps))
    return lax.ppermute(value, axis, [(source, source + steps) for source in range(initial, last)])


def swapped(value, axis, bits):
    count = lax.axis_size(axis)
    return lax.ppermute(value, axis, [(source, source ^ bits) for source in range(count)])


def whole(shape):
    return pl.BlockSpec(shape, lambda *_: (0,) * len(shape))


def call(kernel, name, grid, in_specs, out_specs, out_shape, cost, scratch=()):
    return pl.pallas_call(
        kernel,
        name=name,
        grid=grid,
        in_specs=in_specs,
        out_specs=out_specs,
        out_shape=out_shape,
        scratch_shapes=list(scratch),
        compiler_params=pltpu.CompilerParams(vmem_limit_bytes=VMEM),
        cost_estimate=pl.CostEstimate(flops=cost[0], bytes_accessed=cost[1], transcendentals=0),
    )


def mask_kernel(ids_ref, long_ref, back_ref, ahead_ref):
    taps = ids_ref.shape[1]
    prev_row, here_row, next_row = [
        jnp.broadcast_to(ids_ref[i : i + 1, :].astype(F32), (taps, taps)) for i in range(3)
    ]
    here_col = jnp.transpose(here_row)
    rows = lax.broadcasted_iota(jnp.int32, (taps, taps), 0)
    cols = lax.broadcasted_iota(jnp.int32, (taps, taps), 1)

    def put(condition):
        return jnp.where(condition, 1.0, 0.0).astype(BF)

    same = here_col == here_row
    long_ref[0] = put((cols <= rows) & same)
    long_ref[1] = put((cols > rows) & (here_col == prev_row))
    long_ref[2] = put((cols >= rows) & same)
    long_ref[3] = put((cols < rows) & (here_col == next_row))
    last_prev = here_col == pltpu.roll(prev_row, 2, 1)
    first_next = here_col == next_row
    for j in (1, 2):
        at = slice((j - 1) * taps, j * taps)
        back_ref[at, :taps] = put((cols == rows - j) & same)
        back_ref[at, taps:] = put((cols < 2) & (cols == rows + 2 - j) & last_prev)[:, :EDGE]
        ahead_ref[at, :taps] = put((cols == rows + j) & same)
        ahead_ref[at, taps:] = put((cols < 2) & (cols == rows + j - taps) & first_next)[:, :EDGE]


def make_masks(ids3):
    taps = ids3.shape[1]
    return call(
        mask_kernel,
        "masks",
        (),
        [whole(ids3.shape)],
        [whole((4, taps, taps)), whole((2 * taps, taps + EDGE)), whole((2 * taps, taps + EDGE))],
        [
            jax.ShapeDtypeStruct((4, taps, taps), BF),
            jax.ShapeDtypeStruct((2 * taps, taps + EDGE), BF),
            jax.ShapeDtypeStruct((2 * taps, taps + EDGE), BF),
        ],
        (100000, 400000),
    )(ids3)


def turn_kernel(filter_ref, out_ref):
    group_step, taps = filter_ref.shape
    values = filter_ref[...].astype(F32)
    for g in range(group_step):
        spread = jnp.broadcast_to(values[g : g + 1], (taps, taps))
        out_ref[g] = pltpu.roll(spread, 0, 1, stride=1, stride_axis=0).astype(BF)


def make_turned(filters):
    groups, taps = filters.shape
    group_step = 32
    return call(
        turn_kernel,
        "circulants",
        (groups // group_step,),
        [pl.BlockSpec((group_step, taps), lambda i: (i, 0))],
        pl.BlockSpec((group_step, taps, taps), lambda i: (i, 0, 0)),
        jax.ShapeDtypeStruct((groups, taps, taps), BF),
        (groups * taps * taps * 40, groups * taps * taps * 2),
    )(filters)


def extended(values, edge):
    blank = jnp.zeros((EDGE - edge.shape[0], edge.shape[1]), BF)
    return jnp.concatenate([values, edge, blank], axis=0)


def shifted(mask_ref, values, edge):
    taps = values.shape[0]
    both = jnp.dot(mask_ref[...], extended(values, edge), preferred_element_type=F32)
    return both[:taps], both[taps:]


def short_sum(weights, values, one, two):
    return (weights[0:1] * values.astype(F32) + weights[1:2] * one) + weights[2:3] * two


def gate_kernel(
    xq, xk, xv, eq, ek, ev, wq, wk, wv, cot_ref, mask_ref, mixed_ref, product_ref, grad_ref
):
    mixed = []
    for x_ref, e_ref, w_ref in ((xq, eq, wq), (xk, ek, wk), (xv, ev, wv)):
        values = x_ref[...]
        one, two = shifted(mask_ref, values, e_ref[...])
        mixed.append(short_sum(w_ref[...], values, one, two).astype(BF))
    for i in range(3):
        mixed_ref[i] = mixed[i]
    product_ref[...] = mixed[1] * mixed[2]
    grad_ref[...] = cot_ref[...] * mixed[0]


def branch_specs(rows, width, steps):
    return [pl.BlockSpec((rows, width), lambda i, b=b: (0, i + b * steps)) for b in range(3)]


def make_gates(inputs, border, weights, cotangent, back_mask):
    rows, model_width = cotangent.shape
    width = 512
    steps = model_width // width
    plain = pl.BlockSpec((rows, width), lambda i: (0, i))
    return call(
        gate_kernel,
        "gates",
        (steps,),
        branch_specs(rows, width, steps)
        + branch_specs(border.shape[0], width, steps)
        + branch_specs(weights.shape[0], width, steps)
        + [plain, whole(back_mask.shape)],
        [pl.BlockSpec((3, rows, width), lambda i: (0, 0, i)), plain, plain],
        [
            jax.ShapeDtypeStruct((3, rows, model_width), BF),
            jax.ShapeDtypeStruct((rows, model_width), BF),
            jax.ShapeDtypeStruct((rows, model_width), BF),
        ],
        (2 * 256 * 144 * 3 * model_width, 9 * rows * model_width * 2),
    )(inputs, inputs, inputs, border, border, border, weights, weights, weights, cotangent, back_mask)


def long_kernel(
    here_ref, prev_ref, grad_ref, next_ref, fwd_ref, bwd_ref, long_ref, back_ref,
    mixed_ref, cot_ref, xq, xk, xv, eq, ek, ev,
    out_ref, mg_ref, gl_ref, gs_ref, diag,
):
    taps = here_ref.shape[0]
    subs = here_ref.shape[1] // LANES
    per = fwd_ref.shape[0] // subs
    share = LANES // per
    lane_group = lax.broadcasted_iota(jnp.int32, (1, LANES), 1) // share
    lane = [jnp.where(lane_group == g, 1.0, 0.0).astype(BF) for g in range(per)]
    rows = lax.broadcasted_iota(jnp.int32, (8, taps), 0)
    cols = lax.broadcasted_iota(jnp.int32, (8, taps), 1)
    keep = (long_ref[2] + long_ref[3]).astype(F32)

    def long_conv(turned, first, second, stacked):
        left = jnp.concatenate(
            [turned[g] * mask for g in range(per) for mask in (first, second)], axis=1
        )
        right = jnp.concatenate([stacked * lane[g] for g in range(per)], axis=0)
        return jnp.dot(left, right, preferred_element_type=F32)

    for u in range(subs):
        ls = slice(u * LANES, (u + 1) * LANES)
        gs = slice(u * per, (u + 1) * per)
        here, grad = here_ref[:, ls], grad_ref[:, ls]
        sources = jnp.concatenate([here, prev_ref[:, ls]], axis=0)
        grads = jnp.concatenate([grad, next_ref[:, ls]], axis=0)
        long_mix = long_conv(fwd_ref[gs], long_ref[0], long_ref[1], sources).astype(BF)
        grad_product = long_conv(bwd_ref[gs], long_ref[2], long_ref[3], grads).astype(BF)
        out_ref[:, ls] = mixed_ref[0, :, ls] * long_mix
        mg_ref[0, :, ls] = cot_ref[:, ls] * long_mix
        mg_ref[1, :, ls] = grad_product * mixed_ref[2, :, ls]
        mg_ref[2, :, ls] = grad_product * mixed_ref[1, :, ls]

        spread = jnp.concatenate([here * lane[g] for g in range(per)], axis=0)
        inner = lax.dot_general(
            spread, grads, (((1,), (1,)), ((), ())), preferred_element_type=F32
        ).reshape(per, taps // 8, 8, 2 * taps)
        total = None
        for k in range(taps // 8):
            nearer = (cols >= rows + 8 * k)[None]
            term = jnp.where(nearer, inner[:, k, :, :taps], inner[:, k, :, taps:])
            term = (term * keep[8 * k : 8 * k + 8][None]).reshape(per * 8, taps)
            if k:
                term = pltpu.roll(term, taps - 8 * k, 1)
            total = term if total is None else total + term
        diag[u] = total.reshape(per, 8, taps)
        lined = diag[u, :, 0, :]
        for r in range(1, 8):
            lined = lined + pltpu.roll(diag[u, :, r, :], taps - r, 1)
        gl_ref[gs, :] = lined

    for b, (x_ref, e_ref) in enumerate(((xq, eq), (xk, ek), (xv, ev))):
        values = x_ref[...]
        one, two = shifted(back_ref, values, e_ref[...])
        local_grad = mg_ref[b].astype(F32)
        for j, part in enumerate((values.astype(F32), one, two)):
            summed = jnp.sum(local_grad * part, axis=0, keepdims=True)
            for u in range(subs):
                gs_ref[b, 0, j * subs + u : j * subs + u + 1, :] = summed[
                    :, u * LANES : (u + 1) * LANES
                ]


def make_long(product, before, grad_mix, after, fwd, bwd, long_masks, back_mask, mixed, cotangent,
              inputs, border):
    rows, model_width = product.shape
    groups, taps, _ = fwd.shape
    width = 512
    steps = model_width // width
    subs = width // LANES
    step_groups = groups // steps
    plain = pl.BlockSpec((rows, width), lambda i: (0, i))
    tiles = pl.BlockSpec((step_groups, taps, taps), lambda i: (i, 0, 0))
    triple = pl.BlockSpec((3, rows, width), lambda i: (0, 0, i))
    return call(
        long_kernel,
        "long_parts",
        (steps,),
        [plain] * 4
        + [tiles] * 2
        + [whole(long_masks.shape), whole(back_mask.shape), triple, plain]
        + branch_specs(rows, width, steps)
        + branch_specs(border.shape[0], width, steps),
        [
            plain,
            triple,
            pl.BlockSpec((step_groups, taps), lambda i: (i, 0)),
            pl.BlockSpec((3, 1, 3 * subs, LANES), lambda i: (0, i, 0, 0)),
        ],
        [
            jax.ShapeDtypeStruct((rows, model_width), BF),
            jax.ShapeDtypeStruct((3, rows, model_width), BF),
            jax.ShapeDtypeStruct((groups, taps), F32),
            jax.ShapeDtypeStruct((3, steps, 3 * subs, LANES), F32),
        ],
        (3 * groups * 2 * 128 * 256 * 256, 40 * 1024 * 1024),
        [pltpu.VMEM((subs, step_groups // subs, 8, taps), F32)],
    )(product, before, grad_mix, after, fwd, bwd, long_masks, back_mask, mixed, cotangent,
      inputs, inputs, inputs, border, border, border)


def input_grad_kernel(mg_ref, edge_ref, w_ref, mask_ref, out_ref):
    values = mg_ref[0]
    one, two = shifted(mask_ref, values, edge_ref[0])
    out_ref[...] = short_sum(w_ref[...], values, one, two).astype(BF)


def make_input_grad(mixed_grad, edge, weights, ahead_mask):
    _, rows, model_width = mixed_grad.shape
    width = 1024
    steps = model_width // width
    return call(
        input_grad_kernel,
        "input_grads",
        (3, steps),
        [
            pl.BlockSpec((1, rows, width), lambda b, i: (b, 0, i)),
            pl.BlockSpec((1, edge.shape[1], width), lambda b, i: (b, 0, i)),
            pl.BlockSpec((weights.shape[0], width), lambda b, i: (0, b * steps + i)),
            whole(ahead_mask.shape),
        ],
        pl.BlockSpec((rows, width), lambda b, i: (0, b * steps + i)),
        jax.ShapeDtypeStruct((rows, 3 * model_width), BF),
        (2 * 256 * 144 * 3 * model_width, 6 * rows * model_width * 2),
    )(mixed_grad, edge, weights, ahead_mask)


def summed_over_windows(value):
    count = lax.axis_size("dp")
    if count & (count - 1):
        return lax.psum(value, "dp")
    parts = [value] + [swapped(value, "dp", bits) for bits in range(1, count)]
    while len(parts) > 1:
        parts = [parts[i] + parts[i + 1] for i in range(0, len(parts), 2)]
    return parts[0]


def owned_sums(short_parts, long_parts):
    branches, steps, short_rows, lanes = short_parts.shape
    groups, taps = long_parts.shape
    subs = short_rows // 3
    ctx_parts = lax.axis_size("ctx")
    pieces = branches * steps
    if ctx_parts != 8 or pieces % ctx_parts or lanes != taps:
        weight_grad = short_parts.reshape(branches, steps, 3, subs, lanes).transpose(2, 0, 1, 3, 4)
        weight_part = lax.psum_scatter(
            weight_grad.reshape(3, -1), "ctx", scatter_dimension=1, tiled=True
        )
        filter_part = lax.psum_scatter(long_parts, "ctx", scatter_dimension=0, tiled=True)
        return lax.psum((weight_part, filter_part), "dp")
    held = pieces // ctx_parts
    short_owned = short_parts.reshape(ctx_parts, held * short_rows, lanes)
    long_owned = long_parts.reshape(ctx_parts, groups // ctx_parts, taps)
    joined = jnp.concatenate([short_owned, long_owned], axis=1)
    height = joined.shape[1]
    my_index = lax.axis_index("ctx")
    core, chip = my_index % 2, my_index // 2
    by_core = joined.reshape(ctx_parts // 2, 2, height, lanes)
    kept = lax.dynamic_index_in_dim(by_core, core, 1, keepdims=False)
    given = lax.dynamic_index_in_dim(by_core, 1 - core, 1, keepdims=False)
    paired = kept + swapped(given, "ctx", 1)
    mine = lax.dynamic_index_in_dim(paired, chip, 0, keepdims=False)
    others = [
        swapped(lax.dynamic_index_in_dim(paired, chip ^ d, 0, keepdims=False), "ctx", 2 * d)
        for d in range(1, ctx_parts // 2)
    ]
    total = (mine + others[0]) + (others[1] + others[2])
    total = summed_over_windows(total)
    short_total = total[: held * short_rows].reshape(held, 3, subs, lanes).transpose(1, 0, 2, 3)
    return short_total.reshape(3, held * subs * lanes), total[held * short_rows :]


def local(projected, doc_ids, short_filter, long_filter, cotangent):
    inputs_row = projected[0]
    grad_row = cotangent[0]
    seg_row = doc_ids[0]
    rows, model_width = grad_row.shape
    groups, taps = long_filter.shape
    short_taps = short_filter.shape[0]
    length = seg_row.shape[0]
    my_index = lax.axis_index("ctx")
    edge = short_taps - 1
    border = passed_along(inputs_row[rows - edge :], "ctx", 1)
    blank = jnp.full((rows,), -1, jnp.int32)
    ids_pad = jnp.concatenate([blank, seg_row, blank])
    ids3 = lax.dynamic_slice_in_dim(ids_pad, my_index * rows, 3 * rows, 0).reshape(3, rows)
    long_masks, back_mask, ahead_mask = make_masks(ids3)
    fwd = make_turned(jnp.roll(long_filter[:, ::-1], 1, axis=1))
    mixed, product, grad_mix = make_gates(inputs_row, border, short_filter, grad_row, back_mask)
    before = passed_along(product, "ctx", 1)
    after = passed_along(grad_mix, "ctx", -1)
    bwd = make_turned(long_filter)
    block_out, mixed_grad, long_parts, short_parts = make_long(
        product, before, grad_mix, after, fwd, bwd, long_masks, back_mask, mixed, grad_row,
        inputs_row, border,
    )
    ahead_rows = passed_along(mixed_grad[:, :edge], "ctx", -1)
    grad_inputs = make_input_grad(mixed_grad, ahead_rows, short_filter, ahead_mask)
    weight_total, filter_total = owned_sums(short_parts, long_parts)
    norm_scale = lax.axis_size("dp") * length
    group_size = model_width // groups
    grad_short = weight_total / math.sqrt(norm_scale)
    grad_long = filter_total / math.sqrt(norm_scale * group_size)
    return (block_out[None], grad_inputs[None], grad_short, grad_long)


def solution(mesh):
    return jax.shard_map(
        local,
        mesh=mesh,
        in_specs=(P("dp", "ctx", None), P("dp", None), P(), P(), P("dp", "ctx", None)),
        out_specs=(P("dp", "ctx", None), P("dp", "ctx", None), P(None, "ctx"), P("ctx", None)),
        check_vma=False,
    )
```

time: 805 us -> 82 us (0.10); the launches traced: 795 us -> 81.5 us
  local copies, waits for them, and re-layouts: 325 us -> 6.98 us
  other arithmetic: 159 us -> 1.55 us
  matrix products: 102 us -> 0 us
  loops' own time: 88.4 us -> 0 us
  blocking collectives: 49.3 us -> 0 us
  Pallas kernels: 0 us -> 46.3 us
  waiting for transfers between devices: 40 us -> 2.8 us
  between operations: 14.7 us -> 0.83 us
    reshape x38 -> x0, local copies, waits for them, and re-layouts: 149 us -> none  [the longest x18 85.5 us: toeplitz(): tiled_rows = jnp.tile(widened, (1, tap_count))]
    dot_general x52 -> x0, matrix products: 102 us -> none  [the longest x18 40.1 us: one_tile(): jnp.einsum('gis,igc->sgc', masked, grad_piece, preferred_element_type=jnp...]
    another operation x2 -> x0, loops' own time: 88.4 us -> none  [the longest x1 48.1 us: long_backward(): lax.scan(one_tile, start_grad, (grad_tiles, padded_windows, jnp.arange(ou...]
    pad x36 -> x0, local copies, waits for them, and re-layouts: 87.4 us -> none  [toeplitz(): tiled_rows[:, tap_count - 1:tap_count - 1 + tap_count * span_len]]
    pallas_call x0 -> x6, Pallas kernels: none -> 46.3 us  [the longest x1 20.7 us: make_long(): call(long_kernel, 'long_parts', (steps,), [plain] * 4 + [tiles] * 2 + [wh...]
    concatenate x4 -> x1, other arithmetic: 39.5 us -> 0.09 us  [local(): fwd = make_turned(jnp.roll(long_filter[:, ::-1], 1, axis=1))]
    all_to_all x1 -> x0, blocking collectives: 32.6 us -> none  [local(): lax.all_to_all(grad_mix, 'ctx', split_axis=1, concat_axis=0, tiled=True)]
    reduce_sum x19 -> x0, other arithmetic: 27.8 us -> none  [the longest x1 23.8 us: short_backward(): jnp.sum(jnp.where((offsets >= tap_pos)[:, None], local_grad * shifted, 0....]
  transfers between devices with their start and end apart: 6 -> 11, of which waited for: 3 -> 3; matrix products, arithmetic and copies ran while one was open for 57% -> 3% of each run, Pallas kernels for 0% -> 22%
where the time goes in v1:
time: 82 us; the launch traced here: 81.5 us
  Pallas kernels  46.3 us (56%)
  starting transfers between devices  23 us (28%)
  local copies, waits for them, and re-layouts  6.98 us (9%)
  waiting for transfers between devices  2.8 us (3%)
  other arithmetic  1.55 us (2%)
  between operations  0.83 us (1%)
    pallas_call x1, Pallas kernels, make_long(): call(long_kernel, 'long_parts', (steps,), [plain] * 4 + [tiles] * 2 + [wh...  20.7 us
    ppermute x7, starting transfers between devices, swapped(): lax.ppermute(value, axis, [(source, source ^ bits) for source in range(co...  12.3 us
    pallas_call x2, Pallas kernels, make_turned(): call(turn_kernel, 'circulants', (groups // group_step,), [pl.BlockSpec((g...  11.6 us
    ppermute x4, starting transfers between devices, passed_along(): lax.ppermute(value, axis, [(source, source + steps) for source in range(i...  10.7 us
    pallas_call x1, Pallas kernels, make_gates(): call(gate_kernel, 'gates', (steps,), branch_specs(rows, width, steps) + b...  7.5 us
    pallas_call x1, Pallas kernels, make_input_grad(): call(input_grad_kernel, 'input_grads', (3, steps), [pl.BlockSpec((1, rows...  6.42 us
    unnamed x12, local copies, waits for them, and re-layouts  4.05 us
    ppermute x7, waiting for transfers between devices, swapped(): lax.ppermute(value, axis, [(source, source ^ bits) for source in range(co...  2.79 us
  transfers between devices with their start and end apart: 11, of which 3 were waited for; matrix products, arithmetic and copies ran while one was open for 3% of the time, Pallas kernels for 22%

profile of v1, /device:TPU:0, one launch (start us, length us, event | category | flops | bytes accessed | tf_op | source)
XLA Modules:
  0.0 81.5 jit_solution(197528827296165450)
XLA Ops:
  0.6 1.0 %slice_bitcast_fusion = bf16[2,12288]{1,0:T(2,128)(2,1)S(1)} fusion(bf16[1,128,12288]{2,1,0:T(8,128)(2,1)} %param.5), kind=kLoop, calls=%fused_computation.10 | loop fusion | bytes 98304 | tf_op jit(solution)/shard_map/slice | solution.py:352
  1.6 2.4 %collective-permute-start = (bf16[2,12288]{1,0:T(2,128)(2,1)S(1)}, bf16[2,12288]{1,0:T(2,128)(2,1)S(1)}, u32[]{:S(2)}, u32[]{:S(2)}) collective-permute-start(bf16[2,12288]{1,0:T(2,128)(2,1)S(1)} %slice_bitcast_fusion), channel_id=1, source_target_pairs={{0,1},{1,2},{2,3},{3,4},{4,5},{5,6},{6,7},{8,9},{9,10},{10,11},{11... | collective-permute-start | bytes 147464 | tf_op jit(solution)/shard_map/ppermute | solution.py:20
  4.0 0.8 fusion.8.ids_ref
  4.8 0.2 masks.1
  4.9 0.0 collective-permute-done.eq.ek.ev
  4.9 0.0 copy-start.1
  5.0 0.9 %copy-done.1 = f32[3,12288]{1,0:T(4,128)S(1)} copy-done((f32[3,12288]{1,0:T(4,128)S(1)}, f32[3,12288]{1,0:T(4,128)}, u32[]{:S(2)}) %copy-start.1) | copy-done | bytes 147480
  5.9 0.0 copy-start.3
  5.9 1.2 %copy-done.3 = bf16[1,128,4096]{2,1,0:T(8,128)(2,1)S(1)} copy-done((bf16[1,128,4096]{2,1,0:T(8,128)(2,1)S(1)}, bf16[1,128,4096]{2,1,0:T(8,128)(2,1)}, u32[]{:S(2)}) %copy-start.3) | copy-done | bytes 1048600
  7.1 0.0 copy-start.5
  7.1 7.5 %gates.1 = (bf16[3,128,4096]{2,1,0:T(8,128)(2,1)}, bf16[128,4096]{1,0:T(8,128)(2,1)S(1)}, bf16[128,4096]{1,0:T(8,128)(2,1)S(1)}) custom-call(bf16[128,12288]{1,0:T(8,128)(2,1)} %bitcast.33, bf16[128,12288]{1,0:T(8,128)(2,1)} %bitcast.34, bf16[128,12288]{1,0:T(8,128)(2,1)} %bitcast.35, bf16[2,12288]{1,0:T(2,128)(2,1)S(1)} %collective-permute-done.eq.ek.ev, ...), custom_call_target="tpu_custom_call" | custom-call | flops 905969664 | bytes 9437184 | tf_op jit(solution)/shard_map/gates/pallas_call | solution.py:150
  14.6 5.8 %collective-permute-start.1 = (bf16[128,4096]{1,0:T(8,128)(2,1)S(1)}, bf16[128,4096]{1,0:T(8,128)(2,1)}, u32[]{:S(2)}, u32[]{:S(2)}) collective-permute-start(bf16[128,4096]{1,0:T(8,128)(2,1)S(1)} %get-tuple-element.15.here_ref), channel_id=1, source_target_pairs={{0,1},{1,2},{2,3},{3,4},{4,5},{5,6},{6,7},{8,9},{9,10},{10,11},{11... | collective-permute-start | bytes 3145736 | tf_op jit(solution)/shard_map/ppermute | solution.py:20
  20.4 1.3 %collective-permute-start.2 = (bf16[128,4096]{1,0:T(8,128)(2,1)S(1)}, bf16[128,4096]{1,0:T(8,128)(2,1)}, u32[]{:S(2)}, u32[]{:S(2)}) collective-permute-start(bf16[128,4096]{1,0:T(8,128)(2,1)S(1)} %get-tuple-element.16.grad_ref), channel_id=1, source_target_pairs={{1,0},{2,1},{3,2},{4,3},{5,4},{6,5},{7,6},{9,8},{10,9},{11,10},{12... | collective-permute-start | bytes 3145736 | tf_op jit(solution)/shard_map/ppermute | solution.py:20
  21.7 0.0 copy-done.5
  21.7 0.1 slice.30
  21.8 0.2 slice.31
  22.0 5.8 %circulants.3.bwd_ref = bf16[256,128,128]{2,1,0:T(8,128)(2,1)} custom-call(bf16[256,128]{1,0:T(8,128)(2,1)S(1)} %copy-done.5), custom_call_target="tpu_custom_call" | custom-call | flops 167772160 | bytes 8388608 | tf_op jit(solution)/shard_map/circulants/pallas_call | solution.py:101
  27.8 0.1 pad_maximum_fusion.filter_ref
  27.9 0.0 copy-start.4
  27.9 5.8 %circulants.2.fwd_ref = bf16[256,128,128]{2,1,0:T(8,128)(2,1)} custom-call(bf16[256,128]{1,0:T(8,128)(2,1)S(1)} %pad_maximum_fusion.filter_ref), custom_call_target="tpu_custom_call" | custom-call | flops 167772160 | bytes 8388608 | tf_op jit(solution)/shard_map/circulants/pallas_call | solution.py:101
  33.7 0.0 collective-permute-done.1.prev_ref
  33.7 0.0 collective-permute-done.2.next_ref
  33.7 0.0 copy-done.4
  33.7 0.0 copy-start.2
  33.7 20.7 %long_parts.1 = (bf16[128,4096]{1,0:T(8,128)(2,1)}, bf16[3,128,4096]{2,1,0:T(8,128)(2,1)}, f32[256,128]{1,0:T(8,128)S(1)}, f32[3,8,12,128]{3,2,1,0:T(8,128)S(1)}) custom-call(bf16[128,4096]{1,0:T(8,128)(2,1)S(1)} %get-tuple-element.15.here_ref, bf16[128,4096]{1,0:T(8,128)(2,1)} %collective-permute-done.1.prev_ref, ...), custom_call_target="tpu_custom_call" | custom-call | flops 12884901888 | bytes 41943040 | tf_op jit(solution)/shard_map/long_parts/pallas_call | solution.py:244
  54.4 4.3 %collective-permute-start.4 = (f32[4,68,128]{2,1,0:T(8,128)S(1)}, f32[4,68,128]{2,1,0:T(8,128)S(1)}, u32[]{:S(2)}, u32[]{:S(2)}) collective-permute-start(f32[4,68,128]{2,1,0:T(8,128)S(1)} %fusion.1), channel_id=1, source_target_pairs={{0,1},{1,0},{2,3},{3,2},{4,5},{5,4},{6,7},{7,6},{8,9},{9,8},{10,11... | collective-permute-start | bytes 417800 | tf_op jit(solution)/shard_map/ppermute | solution.py:25
  58.7 1.0 %collective-permute-done.4 = f32[4,68,128]{2,1,0:T(8,128)S(1)} collective-permute-done((f32[4,68,128]{2,1,0:T(8,128)S(1)}, f32[4,68,128]{2,1,0:T(8,128)S(1)}, u32[]{:S(2)}, u32[]{:S(2)}) %collective-permute-start.4) | collective-permute-done | bytes 139296 | tf_op jit(solution)/shard_map/ppermute | solution.py:25
  59.8 1.7 %collective-permute-start.5 = (f32[68,128]{1,0:T(8,128)S(1)}, f32[68,128]{1,0:T(8,128)S(1)}, u32[]{:S(2)}, u32[]{:S(2)}) collective-permute-start(f32[68,128]{1,0:T(8,128)S(1)} %get-tuple-element.26), channel_id=1, source_target_pairs={{0,2},{1,3},{2,0},{3,1},{4,6},{5,7},{6,4},{7,5},{8,10},{9,11},{10,... | collective-permute-start | bytes 104456 | tf_op jit(solution)/shard_map/ppermute | solution.py:25
  61.4 1.1 %collective-permute-start.6 = (f32[68,128]{1,0:T(8,128)S(1)}, f32[68,128]{1,0:T(8,128)S(1)}, u32[]{:S(2)}, u32[]{:S(2)}) collective-permute-start(f32[68,128]{1,0:T(8,128)S(1)} %get-tuple-element.25), channel_id=1, source_target_pairs={{0,4},{1,5},{2,6},{3,7},{4,0},{5,1},{6,2},{7,3},{8,12},{9,13},{10,... | collective-permute-start | bytes 104456 | tf_op jit(solution)/shard_map/ppermute | solution.py:25
  62.5 1.7 %collective-permute-start.7 = (f32[68,128]{1,0:T(8,128)S(1)}, f32[68,128]{1,0:T(8,128)S(1)}, u32[]{:S(2)}, u32[]{:S(2)}) collective-permute-start(f32[68,128]{1,0:T(8,128)S(1)} %get-tuple-element.24), channel_id=1, source_target_pairs={{0,6},{1,7},{2,4},{3,5},{4,2},{5,3},{6,0},{7,1},{8,14},{9,15},{10,... | collective-permute-start | bytes 104456 | tf_op jit(solution)/shard_map/ppermute | solution.py:25
  64.3 1.0 %slice.32 = bf16[3,2,4096]{2,1,0:T(2,128)(2,1)S(1)} slice(bf16[3,128,4096]{2,1,0:T(8,128)(2,1)} %get-tuple-element.20.mg_ref), slice={[0:3], [0:2], [0:4096]} | slice | bytes 98304 | tf_op jit(solution)/shard_map/slice | solution.py:366
  65.2 1.3 %collective-permute-start.3 = (bf16[3,2,4096]{2,1,0:T(2,128)(2,1)S(1)}, bf16[3,2,4096]{2,1,0:T(2,128)(2,1)S(1)}, u32[]{:S(2)}, u32[]{:S(2)}) collective-permute-start(bf16[3,2,4096]{2,1,0:T(2,128)(2,1)S(1)} %slice.32), channel_id=1, source_target_pairs={{1,0},{2,1},{3,2},{4,3},{5,4},{6,5},{7,6},{9,8},{10,9},{11,10},{12... | collective-permute-start | bytes 147464 | tf_op jit(solution)/shard_map/ppermute | solution.py:20
  66.5 0.0 collective-permute-done.5
  66.5 0.4 collective-permute-done.6
  67.0 1.3 %collective-permute-done.7 = f32[68,128]{1,0:T(8,128)S(1)} collective-permute-done((f32[68,128]{1,0:T(8,128)S(1)}, f32[68,128]{1,0:T(8,128)S(1)}, u32[]{:S(2)}, u32[]{:S(2)}) %collective-permute-start.7) | collective-permute-done | bytes 34848 | tf_op jit(solution)/shard_map/ppermute | solution.py:25
  68.3 2.5 %collective-permute-start.10 = (f32[68,128]{1,0:T(8,128)S(1)}, f32[68,128]{1,0:T(8,128)S(1)}, u32[]{:S(2)}, u32[]{:S(2)}) collective-permute-start(f32[68,128]{1,0:T(8,128)S(1)} %fusion.5), channel_id=1, source_target_pairs={{0,24},{8,16},{16,8},{24,0},{1,25},{9,17},{17,9},{25,1},{2,26},{10... | collective-permute-start | bytes 104456 | tf_op jit(solution)/shard_map/ppermute | solution.py:25
  70.8 0.5 collective-permute-start.8
  71.4 0.5 collective-permute-start.9
  71.9 0.0 collective-permute-done.3.edge_ref
  71.9 0.0 copy-done.2
  71.9 0.0 copy-start
  71.9 1.9 %copy-done = bf16[3,128,4096]{2,1,0:T(8,128)(2,1)S(1)} copy-done((bf16[3,128,4096]{2,1,0:T(8,128)(2,1)S(1)}, bf16[3,128,4096]{2,1,0:T(8,128)(2,1)}, u32[]{:S(2)}) %copy-start) | copy-done | bytes 3145752
  73.8 6.4 %input_grads.1 = bf16[128,12288]{1,0:T(8,128)(2,1)} custom-call(bf16[3,128,4096]{2,1,0:T(8,128)(2,1)S(1)} %copy-done, bf16[3,2,4096]{2,1,0:T(2,128)(2,1)S(1)} %collective-permute-done.3.edge_ref, f32[3,12288]{1,0:T(4,128)S(1)} %copy-done.2, bf16[256,144]{1,0:T(8,128)(2,1)S(1)} %get-tuple-element.21.mask_ref), custom_call_target="tpu_custom_call" | custom-call | flops 905969664 | bytes 6291456 | tf_op jit(solution)/shard_map/input_grads/pallas_call | solution.py:281
  80.2 0.0 collective-permute-done.10
  80.2 0.0 collective-permute-done.8
  80.2 0.0 collective-permute-done.9
  80.2 0.6 slice_multiply_fusion.1
  80.8 0.6 div.33
  (10 shorter events, 0.1 us)
Async XLA Ops:
  1.6 3.3 %collective-permute-start = (bf16[2,12288]{1,0:T(2,128)(2,1)S(1)}, bf16[2,12288]{1,0:T(2,128)(2,1)S(1)}, u32[]{:S(2)}, u32[]{:S(2)}) collective-permute-start(bf16[2,12288]{1,0:T(2,128)(2,1)S(1)} %slice_bitcast_fusion), channel_id=1, source_target_pairs={{0,1},{1,2},{2,3},{3,4},{4,5},{5,6},{6,7},{8,9},{9,10},{10,11},{11... | collective-permute-start | bytes 147464 | tf_op jit(solution)/shard_map/ppermute | solution.py:20
  4.9 0.9 %copy-start.1 = (f32[3,12288]{1,0:T(4,128)S(1)}, f32[3,12288]{1,0:T(4,128)}, u32[]{:S(2)}) copy-start(f32[3,12288]{1,0:T(4,128)} %w_ref.1) | copy-start | bytes 442372
  5.9 1.2 %copy-start.3 = (bf16[1,128,4096]{2,1,0:T(8,128)(2,1)S(1)}, bf16[1,128,4096]{2,1,0:T(8,128)(2,1)}, u32[]{:S(2)}) copy-start(bf16[1,128,4096]{2,1,0:T(8,128)(2,1)} %param.9) | copy-start | bytes 3145732
  7.1 14.6 %copy-start.5 = (bf16[256,128]{1,0:T(8,128)(2,1)S(1)}, bf16[256,128]{1,0:T(8,128)(2,1)}, u32[]{:S(2)}) copy-start(bf16[256,128]{1,0:T(8,128)(2,1)} %filter_ref.1) | copy-start | bytes 196612
  14.6 19.1 %collective-permute-start.1 = (bf16[128,4096]{1,0:T(8,128)(2,1)S(1)}, bf16[128,4096]{1,0:T(8,128)(2,1)}, u32[]{:S(2)}, u32[]{:S(2)}) collective-permute-start(bf16[128,4096]{1,0:T(8,128)(2,1)S(1)} %get-tuple-element.15.here_ref), channel_id=1, source_target_pairs={{0,1},{1,2},{2,3},{3,4},{4,5},{5,6},{6,7},{8,9},{9,10},{10,11},{11... | collective-permute-start | bytes 3145736 | tf_op jit(solution)/shard_map/ppermute | solution.py:20
  20.4 13.3 %collective-permute-start.2 = (bf16[128,4096]{1,0:T(8,128)(2,1)S(1)}, bf16[128,4096]{1,0:T(8,128)(2,1)}, u32[]{:S(2)}, u32[]{:S(2)}) collective-permute-start(bf16[128,4096]{1,0:T(8,128)(2,1)S(1)} %get-tuple-element.16.grad_ref), channel_id=1, source_target_pairs={{1,0},{2,1},{3,2},{4,3},{5,4},{6,5},{7,6},{9,8},{10,9},{11,10},{12... | collective-permute-start | bytes 3145736 | tf_op jit(solution)/shard_map/ppermute | solution.py:20
  27.9 5.8 %copy-start.4 = (bf16[1,128,4096]{2,1,0:T(8,128)(2,1)S(1)}, bf16[1,128,4096]{2,1,0:T(8,128)(2,1)}, u32[]{:S(2)}) copy-start(bf16[1,128,4096]{2,1,0:T(8,128)(2,1)} %param.9) | copy-start | bytes 3145732
  33.7 38.2 %copy-start.2 = (f32[3,12288]{1,0:T(4,128)S(1)}, f32[3,12288]{1,0:T(4,128)}, u32[]{:S(2)}) copy-start(f32[3,12288]{1,0:T(4,128)} %w_ref.1) | copy-start | bytes 442372
  54.4 5.3 %collective-permute-start.4 = (f32[4,68,128]{2,1,0:T(8,128)S(1)}, f32[4,68,128]{2,1,0:T(8,128)S(1)}, u32[]{:S(2)}, u32[]{:S(2)}) collective-permute-start(f32[4,68,128]{2,1,0:T(8,128)S(1)} %fusion.1), channel_id=1, source_target_pairs={{0,1},{1,0},{2,3},{3,2},{4,5},{5,4},{6,7},{7,6},{8,9},{9,8},{10,11... | collective-permute-start | bytes 417800 | tf_op jit(solution)/shard_map/ppermute | solution.py:25
  59.8 6.7 %collective-permute-start.5 = (f32[68,128]{1,0:T(8,128)S(1)}, f32[68,128]{1,0:T(8,128)S(1)}, u32[]{:S(2)}, u32[]{:S(2)}) collective-permute-start(f32[68,128]{1,0:T(8,128)S(1)} %get-tuple-element.26), channel_id=1, source_target_pairs={{0,2},{1,3},{2,0},{3,1},{4,6},{5,7},{6,4},{7,5},{8,10},{9,11},{10,... | collective-permute-start | bytes 104456 | tf_op jit(solution)/shard_map/ppermute | solution.py:25
  61.4 5.5 %collective-permute-start.6 = (f32[68,128]{1,0:T(8,128)S(1)}, f32[68,128]{1,0:T(8,128)S(1)}, u32[]{:S(2)}, u32[]{:S(2)}) collective-permute-start(f32[68,128]{1,0:T(8,128)S(1)} %get-tuple-element.25), channel_id=1, source_target_pairs={{0,4},{1,5},{2,6},{3,7},{4,0},{5,1},{6,2},{7,3},{8,12},{9,13},{10,... | collective-permute-start | bytes 104456 | tf_op jit(solution)/shard_map/ppermute | solution.py:25
  62.5 5.8 %collective-permute-start.7 = (f32[68,128]{1,0:T(8,128)S(1)}, f32[68,128]{1,0:T(8,128)S(1)}, u32[]{:S(2)}, u32[]{:S(2)}) collective-permute-start(f32[68,128]{1,0:T(8,128)S(1)} %get-tuple-element.24), channel_id=1, source_target_pairs={{0,6},{1,7},{2,4},{3,5},{4,2},{5,3},{6,0},{7,1},{8,14},{9,15},{10,... | collective-permute-start | bytes 104456 | tf_op jit(solution)/shard_map/ppermute | solution.py:25
  65.2 6.7 %collective-permute-start.3 = (bf16[3,2,4096]{2,1,0:T(2,128)(2,1)S(1)}, bf16[3,2,4096]{2,1,0:T(2,128)(2,1)S(1)}, u32[]{:S(2)}, u32[]{:S(2)}) collective-permute-start(bf16[3,2,4096]{2,1,0:T(2,128)(2,1)S(1)} %slice.32), channel_id=1, source_target_pairs={{1,0},{2,1},{3,2},{4,3},{5,4},{6,5},{7,6},{9,8},{10,9},{11,10},{12... | collective-permute-start | bytes 147464 | tf_op jit(solution)/shard_map/ppermute | solution.py:20
  68.3 11.9 %collective-permute-start.10 = (f32[68,128]{1,0:T(8,128)S(1)}, f32[68,128]{1,0:T(8,128)S(1)}, u32[]{:S(2)}, u32[]{:S(2)}) collective-permute-start(f32[68,128]{1,0:T(8,128)S(1)} %fusion.5), channel_id=1, source_target_pairs={{0,24},{8,16},{16,8},{24,0},{1,25},{9,17},{17,9},{25,1},{2,26},{10... | collective-permute-start | bytes 104456 | tf_op jit(solution)/shard_map/ppermute | solution.py:25
  70.8 9.4 %collective-permute-start.8 = (f32[68,128]{1,0:T(8,128)S(1)}, f32[68,128]{1,0:T(8,128)S(1)}, u32[]{:S(2)}, u32[]{:S(2)}) collective-permute-start(f32[68,128]{1,0:T(8,128)S(1)} %fusion.5), channel_id=1, source_target_pairs={{0,8},{8,0},{16,24},{24,16},{1,9},{9,1},{17,25},{25,17},{2,10},{10... | collective-permute-start | bytes 104456 | tf_op jit(solution)/shard_map/ppermute | solution.py:25
  71.4 8.8 %collective-permute-start.9 = (f32[68,128]{1,0:T(8,128)S(1)}, f32[68,128]{1,0:T(8,128)S(1)}, u32[]{:S(2)}, u32[]{:S(2)}) collective-permute-start(f32[68,128]{1,0:T(8,128)S(1)} %fusion.5), channel_id=1, source_target_pairs={{0,16},{8,24},{16,0},{24,8},{1,17},{9,25},{17,1},{25,9},{2,18},{10... | collective-permute-start | bytes 104456 | tf_op jit(solution)/shard_map/ppermute | solution.py:25
  71.9 1.9 %copy-start = (bf16[3,128,4096]{2,1,0:T(8,128)(2,1)S(1)}, bf16[3,128,4096]{2,1,0:T(8,128)(2,1)}, u32[]{:S(2)}) copy-start(bf16[3,128,4096]{2,1,0:T(8,128)(2,1)} %get-tuple-element.20.mg_ref) | copy-start | bytes 9437188

commit v2 on v1

v2 whole, which is shorter than its diff:
```python
import functools
import math

import jax
import jax.numpy as jnp
from jax import lax
from jax.experimental import pallas as pl
from jax.experimental.pallas import tpu as pltpu
from jax.sharding import PartitionSpec as P

BF = jnp.bfloat16
F32 = jnp.float32
LANES = 128
EDGE = 16
WIDTH = 512
PARTS = 2
VMEM = 32 * 1024 * 1024


def passed_along(value, axis, steps):
    count = lax.axis_size(axis)
    initial, last = (max(0, -steps), min(count, count - steps))
    return lax.ppermute(value, axis, [(source, source + steps) for source in range(initial, last)])


def swapped(value, axis, bits):
    count = lax.axis_size(axis)
    return lax.ppermute(value, axis, [(source, source ^ bits) for source in range(count)])


def linked(value, axis):
    count = lax.axis_size(axis)
    pairs = [(i, i + 1) for i in range(1, count - 1, 2)]
    return lax.ppermute(value, axis, pairs + [(b, a) for a, b in pairs])


def whole(shape):
    return pl.BlockSpec(shape, lambda *_: (0,) * len(shape))


def call(kernel, name, grid, in_specs, out_specs, out_shape, cost, scratch=(), aliases=None):
    return pl.pallas_call(
        kernel,
        name=name,
        grid=grid,
        in_specs=in_specs,
        out_specs=out_specs,
        out_shape=out_shape,
        scratch_shapes=list(scratch),
        input_output_aliases=aliases or {},
        compiler_params=pltpu.CompilerParams(vmem_limit_bytes=VMEM),
        cost_estimate=pl.CostEstimate(flops=cost[0], bytes_accessed=cost[1], transcendentals=0),
    )


def in_hbm(value):
    return pltpu.with_memory_space_constraint(value, pltpu.HBM)


def prepare_kernel(
    ids_ref, long_ref, back_ref, ahead_ref, late_ref
):
    taps = long_ref.shape[1]
    here = lax.axis_index("ctx")
    last = ids_ref.shape[1] // taps - 1

    def id_row(block, present):
        held = jnp.clip(block, 0, last) * taps
        row = ids_ref[:, pl.ds(pl.multiple_of(held, taps), taps)].astype(F32)
        return jnp.broadcast_to(jnp.where(present, row, -1.0), (taps, taps))

    prev_row = id_row(here - 1, here > 0)
    here_row = id_row(here, here >= 0)
    next_row = id_row(here + 1, here < last)
    here_col = jnp.transpose(here_row)
    rows = lax.broadcasted_iota(jnp.int32, (taps, taps), 0)
    cols = lax.broadcasted_iota(jnp.int32, (taps, taps), 1)

    def put(condition):
        return jnp.where(condition, 1.0, 0.0).astype(BF)

    same = here_col == here_row
    long_ref[0] = put((cols <= rows) & same)
    long_ref[1] = put((cols > rows) & (here_col == prev_row))
    long_ref[2] = put((cols >= rows) & same)
    long_ref[3] = put((cols < rows) & (here_col == next_row))
    long_ref[4] = put(((cols >= rows) & same) | ((cols < rows) & (here_col == next_row)))
    last_prev = here_col == pltpu.roll(prev_row, 2, 1)
    first_next = here_col == next_row
    for j in (1, 2):
        at = slice((j - 1) * taps, j * taps)
        back_ref[at, :taps] = put((cols == rows - j) & same)
        back_ref[at, taps:] = put((cols < 2) & (cols == rows + 2 - j) & last_prev)[:, :EDGE]
        ahead_ref[at, :] = put((cols == rows + j) & same)
        late = jnp.where((cols == rows + j - taps) & first_next, 1.0, 0.0)
        late_ref[j - 1] = late[taps - 8 :]


def prepare(doc_ids, taps):
    shapes = [
        ((5, taps, taps), BF),
        ((2 * taps, taps + EDGE), BF),
        ((2 * taps, taps), BF),
        ((2, 8, taps), F32),
    ]
    return call(
        prepare_kernel,
        "prepare",
        (),
        [whole(doc_ids.shape)],
        [whole(shape) for shape, _ in shapes],
        [jax.ShapeDtypeStruct(*entry) for entry in shapes],
        (1000000, 1000000),
    )(in_hbm(doc_ids))


def short_sum(weights, values, one, two):
    return (weights[0:1] * values.astype(F32) + weights[1:2] * one) + weights[2:3] * two


def gate_kernel(xq, xk, xv, edge_ref, w_ref, cot_ref, mask_ref, mixed_ref, chip_ref, link_ref,
                *, first, steps):
    rows, width = cot_ref.shape
    step = pl.program_id(0) + first
    mixed = []
    for b, x_ref in enumerate((xq, xk, xv)):
        values = x_ref[...]
        at = pl.ds(pl.multiple_of((step + b * steps) * width, width), width)
        edge = edge_ref[:, at]
        blank = jnp.zeros((EDGE - edge.shape[0], width), BF)
        both = jnp.dot(
            mask_ref[...],
            jnp.concatenate([values, edge, blank], axis=0),
            preferred_element_type=F32,
        )
        mixed.append(short_sum(w_ref[:, at], values, both[:rows], both[rows:]).astype(BF))
    for b in range(3):
        mixed_ref[b] = mixed[b]
    product = mixed[1] * mixed[2]
    grad_mix = cot_ref[...] * mixed[0]
    first_core = lax.axis_index("ctx") % 2 == 0
    chip_ref[...] = jnp.where(first_core, product, grad_mix)
    link_ref[...] = jnp.where(first_core, grad_mix, product)


def branch_specs(rows, width, first, steps):
    return [
        pl.BlockSpec((rows, width), lambda i, b=b: (0, first + i + b * steps)) for b in range(3)
    ]


def make_gates(inputs, border, weights, cotangent, back_mask, part, parts):
    rows, model_width = cotangent.shape
    width = WIDTH
    steps = model_width // width
    held = steps // parts
    first = part * held
    plain = pl.BlockSpec((rows, width), lambda i: (0, i))
    return call(
        functools.partial(gate_kernel, first=first, steps=steps),
        "gates",
        (held,),
        branch_specs(rows, width, first, steps)
        + [
            whole(border.shape),
            whole(weights.shape),
            pl.BlockSpec((rows, width), lambda i: (0, first + i)),
            whole(back_mask.shape),
        ],
        [pl.BlockSpec((3, rows, width), lambda i: (0, 0, i)), plain, plain],
        [
            pltpu.VMEM((3, rows, held * width), BF),
            pltpu.VMEM((rows, held * width), BF),
            pltpu.VMEM((rows, held * width), BF),
        ],
        (2 * 256 * 256 * 3 * held * width, 9 * rows * held * width * 2),
    )(inputs, inputs, inputs, border, weights, cotangent, back_mask)


def long_kernel(
    chip_ref, chip_in_ref, link_ref, link_in_ref, filter_ref, long_ref, back_ref, ahead_ref,
    mixed_ref, cot_ref, xq, xk, xv, edge_ref, w_ref, *rest, first, steps, held,
):
    out_ref, head_ref, tail_ref, gl_ref, gs_ref, inputs_ref, diag, staged, sems = rest[-9:]
    rows_here, width = chip_ref.shape
    first_core = lax.axis_index("ctx") % 2 == 0
    taps = filter_ref.shape[1]
    subs = width // LANES
    per = filter_ref.shape[0] // subs
    share = LANES // per
    i = pl.program_id(0)
    slot = lax.rem(i, 2)
    lane_group = lax.broadcasted_iota(jnp.int32, (1, LANES), 1) // share
    lane = [jnp.where(lane_group == g, 1.0, 0.0).astype(BF) for g in range(per)]
    rows = lax.broadcasted_iota(jnp.int32, (8, taps), 0)
    cols = lax.broadcasted_iota(jnp.int32, (8, taps), 1)

    def column(step, b):
        return pl.ds(pl.multiple_of((step + first + b * steps) * width, width), width)

    def leaving(step, b):
        at = lax.rem(step, 2)
        return pltpu.make_async_copy(
            staged.at[at, b], inputs_ref.at[:, column(step, b)], sems.at[at, b]
        )

    @pl.when(i >= 2)
    def _():
        for b in range(3):
            leaving(i - 2, b).wait()

    mixed_grads = [[], [], []]
    for u in range(subs):
        ls = slice(u * LANES, (u + 1) * LANES)
        gs = slice(u * per, (u + 1) * per)
        one_side = jnp.concatenate([chip_ref[:, ls], link_in_ref[:, ls]], axis=0)
        other_side = jnp.concatenate([link_ref[:, ls], chip_in_ref[:, ls]], axis=0)
        sources = jnp.where(first_core, one_side, other_side)
        grads = jnp.where(first_core, other_side, one_side)
        here = sources[:rows_here]
        filters = filter_ref[gs].astype(F32)
        turned = [
            pltpu.roll(
                jnp.broadcast_to(filters[g : g + 1], (taps, taps)), 0, 1, stride=1, stride_axis=0
            ).astype(BF)
            for g in range(per)
        ]
        upright = [jnp.transpose(turned[g]) for g in range(per)]

        def long_conv(circulants, first_mask, stacked):
            left = jnp.concatenate(
                [part * long_ref[first_mask + n] for part in circulants for n in range(2)], axis=1
            )
            right = jnp.concatenate([stacked * lane[g] for g in range(per)], axis=0)
            return jnp.dot(left, right, preferred_element_type=F32).astype(BF)

        long_mix = long_conv(upright, 0, sources)
        grad_product = long_conv(turned, 2, grads)
        out_ref[:, ls] = mixed_ref[0, :, ls] * long_mix
        mixed_grads[0].append(cot_ref[:, ls] * long_mix)
        mixed_grads[1].append(grad_product * mixed_ref[2, :, ls])
        mixed_grads[2].append(grad_product * mixed_ref[1, :, ls])

        spread = jnp.concatenate([here * lane[g] for g in range(per)], axis=0)
        inner = lax.dot_general(
            spread, grads, (((1,), (1,)), ((), ())), preferred_element_type=F32
        ).reshape(per, taps // 8, 8, 2 * taps)
        keep = long_ref[4].astype(F32)
        total = None
        for k in range(taps // 8):
            nearer = (cols >= rows + 8 * k)[None]
            term = jnp.where(nearer, inner[:, k, :, :taps], inner[:, k, :, taps:])
            term = (term * keep[8 * k : 8 * k + 8][None]).reshape(per * 8, taps)
            if k:
                term = pltpu.roll(term, taps - 8 * k, 1)
            total = term if total is None else total + term
        diag[u] = total.reshape(per, 8, taps)
        lined = diag[u, :, 0, :]
        for r in range(1, 8):
            lined = lined + pltpu.roll(diag[u, :, r, :], taps - r, 1)
        gl_ref[gs, :] = lined

    edge_keep = back_ref[:, taps : taps + 2].astype(F32)
    for b, x_ref in enumerate((xq, xk, xv)):
        mixed_grad = jnp.concatenate(mixed_grads[b], axis=1)
        head_ref[b] = mixed_grad[:2]
        both = jnp.dot(ahead_ref[...], mixed_grad, preferred_element_type=F32)
        one, two = both[:rows_here], both[rows_here:]
        at = column(i, b)
        total = short_sum(w_ref[:, at], mixed_grad, one, two)
        tail_ref[b] = total[rows_here - 8 :]
        staged[slot, b] = total.astype(BF)
        leaving(i, b).start()
        values = x_ref[...].astype(F32)
        edge = edge_ref[:, at].astype(F32)
        first_rows = mixed_grad[:16].astype(F32)
        over_edge = (
            None,
            edge_keep[0:1, 1:2] * first_rows[0:1] * edge[1:2],
            edge_keep[taps : taps + 1, 0:1] * first_rows[0:1] * edge[0:1]
            + edge_keep[taps + 1 : taps + 2, 1:2] * first_rows[1:2] * edge[1:2],
        )
        for j, part in enumerate((mixed_grad.astype(F32), one, two)):
            summed = jnp.sum(values * part, axis=0, keepdims=True)
            if j:
                summed = summed + over_edge[j]
            for u in range(subs):
                gs_ref[b, 0, j * subs + u : j * subs + u + 1, :] = summed[
                    :, u * LANES : (u + 1) * LANES
                ]

    @pl.when(i == held - 1)
    def _():
        for b in range(3):
            if held > 1:
                leaving(i - 1, b).wait()
            leaving(i, b).wait()


def make_long(chip, chip_in, link, link_in, filters, masks, mixed, cotangent, inputs, border,
              weights, part, parts, so_far):
    rows, model_width = cotangent.shape
    groups, taps = filters.shape
    width = WIDTH
    steps = model_width // width
    held = steps // parts
    first = part * held
    subs = width // LANES
    step_groups = groups // steps
    long_masks, back_mask, ahead_mask, _ = masks
    plain = pl.BlockSpec((rows, width), lambda i: (0, i))
    placed = pl.BlockSpec((rows, width), lambda i: (0, first + i))
    anywhere = pl.BlockSpec(memory_space=pl.ANY)
    operands = [chip, chip_in, link, link_in, filters, long_masks, back_mask, ahead_mask, mixed,
                cotangent, inputs, inputs, inputs, border, weights]
    in_specs = (
        [plain] * 4
        + [pl.BlockSpec((step_groups, taps), lambda i: (first + i, 0))]
        + [whole(mask.shape) for mask in (long_masks, back_mask, ahead_mask)]
        + [pl.BlockSpec((3, rows, width), lambda i: (0, 0, i)), placed]
        + branch_specs(rows, width, first, steps)
        + [whole(border.shape), whole(weights.shape)]
    )
    aliases = {}
    if so_far is not None:
        aliases = {len(operands) + n: n for n in range(len(so_far))}
        operands = operands + list(so_far)
        in_specs = in_specs + [anywhere] * len(so_far)
    return call(
        functools.partial(long_kernel, first=first, steps=steps, held=held),
        "long_parts",
        (held,),
        in_specs,
        [
            placed,
            pl.BlockSpec((3, 2, width), lambda i: (0, 0, first + i)),
            pl.BlockSpec((3, 8, width), lambda i: (0, 0, first + i)),
            pl.BlockSpec((step_groups, taps), lambda i: (first + i, 0)),
            pl.BlockSpec((3, 1, 3 * subs, LANES), lambda i: (0, first + i, 0, 0)),
            anywhere,
        ],
        [
            jax.ShapeDtypeStruct((rows, model_width), BF),
            jax.ShapeDtypeStruct((3, 2, model_width), BF),
            jax.ShapeDtypeStruct((3, 8, model_width), F32),
            jax.ShapeDtypeStruct((groups, taps), F32),
            jax.ShapeDtypeStruct((3, steps, 3 * subs, LANES), F32),
            jax.ShapeDtypeStruct((rows, 3 * model_width), BF),
        ],
        (3 * groups * 2 * 128 * 256 * 256 // parts, 24 * 1024 * 1024 // parts),
        [
            pltpu.VMEM((subs, step_groups // subs, 8, taps), F32),
            pltpu.VMEM((2, 3, rows, width), BF),
            pltpu.SemaphoreType.DMA((2, 3)),
        ],
        aliases,
    )(*operands)


def last_rows_kernel(tail_ref, ahead_ref, w_ref, late_ref, old_ref, out_ref):
    lines = old_ref.shape[0]
    width = tail_ref.shape[2]
    first_keep, second_keep = late_ref[0, :, 0:1], late_ref[1, :, 0:1]
    next_keep = late_ref[1, :, 1:2]
    for b in range(3):
        at = slice(b * width, (b + 1) * width)
        ahead = ahead_ref[b].astype(F32)
        first, second = ahead[0:1], ahead[1:2]
        extra = w_ref[1:2, at] * (first_keep * first)
        extra = extra + w_ref[2:3, at] * (second_keep * first + next_keep * second)
        ending = (tail_ref[b] + extra).astype(BF)
        out_ref[:, at] = jnp.concatenate([old_ref[: lines // 2, at], ending], axis=0)


def finish_last_rows(grad_inputs, tail, ahead_rows, weights, late_mask):
    rows, total_width = grad_inputs.shape
    lines = 16
    held = pl.BlockSpec((lines, total_width), lambda i: (rows // lines - 1, 0))
    return call(
        last_rows_kernel,
        "last_rows",
        (1,),
        [whole(value.shape) for value in (tail, ahead_rows, weights, late_mask)] + [held],
        held,
        jax.ShapeDtypeStruct(grad_inputs.shape, BF),
        (1000000, 2000000),
        aliases={4: 0},
    )(tail, ahead_rows, weights, late_mask, grad_inputs)


def summed_over_windows(value):
    count = lax.axis_size("dp")
    if count & (count - 1):
        return lax.psum(value, "dp")
    parts = [value] + [swapped(value, "dp", bits) for bits in range(1, count)]
    while len(parts) > 1:
        parts = [parts[i] + parts[i + 1] for i in range(0, len(parts), 2)]
    return parts[0]


def owned_sums(short_parts, long_parts):
    branches, steps, short_rows, lanes = short_parts.shape
    groups, taps = long_parts.shape
    subs = short_rows // 3
    ctx_parts = lax.axis_size("ctx")
    pieces = branches * steps
    if ctx_parts != 8 or pieces % ctx_parts or lanes != taps:
        weight_grad = short_parts.reshape(branches, steps, 3, subs, lanes).transpose(2, 0, 1, 3, 4)
        weight_part = lax.psum_scatter(
            weight_grad.reshape(3, -1), "ctx", scatter_dimension=1, tiled=True
        )
        filter_part = lax.psum_scatter(long_parts, "ctx", scatter_dimension=0, tiled=True)
        return lax.psum((weight_part, filter_part), "dp")
    held = pieces // ctx_parts
    short_owned = short_parts.reshape(ctx_parts, held * short_rows, lanes)
    long_owned = long_parts.reshape(ctx_parts, groups // ctx_parts, taps)
    joined = jnp.concatenate([short_owned, long_owned], axis=1)
    height = joined.shape[1]
    my_index = lax.axis_index("ctx")
    core, chip = my_index % 2, my_index // 2
    by_core = joined.reshape(ctx_parts // 2, 2, height, lanes)
    kept = lax.dynamic_index_in_dim(by_core, core, 1, keepdims=False)
    given = lax.dynamic_index_in_dim(by_core, 1 - core, 1, keepdims=False)
    paired = kept + swapped(given, "ctx", 1)
    mine = lax.dynamic_index_in_dim(paired, chip, 0, keepdims=False)
    others = [
        swapped(lax.dynamic_index_in_dim(paired, chip ^ d, 0, keepdims=False), "ctx", 2 * d)
        for d in range(1, ctx_parts // 2)
    ]
    total = (mine + others[0]) + (others[1] + others[2])
    total = summed_over_windows(total)
    short_total = total[: held * short_rows].reshape(held, 3, subs, lanes).transpose(1, 0, 2, 3)
    return short_total.reshape(3, held * subs * lanes), total[held * short_rows :]


def local(projected, doc_ids, short_filter, long_filter, cotangent):
    grad_row = cotangent[0]
    seg_row = doc_ids[0]
    rows, model_width = grad_row.shape
    groups = long_filter.shape[0]
    short_taps = short_filter.shape[0]
    length = seg_row.shape[0]
    edge = short_taps - 1
    border = passed_along(projected[0, rows - edge :], "ctx", 1)
    filters = in_hbm(long_filter)
    masks = prepare(doc_ids, long_filter.shape[1])
    inputs_row, grad_row, short_filter = [
        in_hbm(value) for value in (projected[0], grad_row, short_filter)
    ]
    gated = []
    for part in range(PARTS):
        mixed, chip, link = make_gates(
            inputs_row, border, short_filter, grad_row, masks[1], part, PARTS
        )
        chip_in = swapped(chip, "ctx", 1)
        link_in = linked(link, "ctx")
        gated.append((mixed, chip, chip_in, link, link_in))
    done = None
    for part, (mixed, chip, chip_in, link, link_in) in enumerate(gated):
        done = make_long(
            chip, chip_in, link, link_in, filters, masks, mixed, grad_row, inputs_row, border,
            short_filter, part, PARTS, done,
        )
    block_out, head, tail, long_parts, short_parts, grad_inputs = done
    ahead_rows = passed_along(head, "ctx", -1)
    grad_inputs = finish_last_rows(grad_inputs, tail, ahead_rows, short_filter, masks[3])
    weight_total, filter_total = owned_sums(short_parts, long_parts)
    norm_scale = lax.axis_size("dp") * length
    group_size = model_width // groups
    grad_short = weight_total / math.sqrt(norm_scale)
    grad_long = filter_total / math.sqrt(norm_scale * group_size)
    return (block_out[None], grad_inputs[None], grad_short, grad_long)


def solution(mesh):
    return jax.shard_map(
        local,
        mesh=mesh,
        in_specs=(P("dp", "ctx", None), P("dp", None), P(), P(), P("dp", "ctx", None)),
        out_specs=(P("dp", "ctx", None), P("dp", "ctx", None), P(None, "ctx"), P("ctx", None)),
        check_vma=False,
    )
```

time: 82 us -> 71.5 us (0.87)
  Pallas kernels: 46.3 us -> 36.2 us
  waiting for transfers between devices: 2.8 us -> 6.46 us
  local copies, waits for them, and re-layouts: 6.98 us -> 4.11 us
  other arithmetic: 1.55 us -> 0.68 us
    pallas_call x6, Pallas kernels: 46.3 us -> 36.2 us  [the longest x2 25.5 us: make_long(): call(functools.partial(long_kernel, first=first, steps=steps, held=held),...]
    ppermute x4 -> x2, starting transfers between devices: 10.7 us -> 3.64 us  [passed_along(): lax.ppermute(value, axis, [(source, source + steps) for source in range(i...]
    ppermute x7 -> x9, starting transfers between devices: 12.3 us -> 16.9 us  [swapped(): lax.ppermute(value, axis, [(source, source ^ bits) for source in range(co...]
    ppermute x7 -> x9, waiting for transfers between devices: 2.79 us -> 6.44 us  [swapped(): lax.ppermute(value, axis, [(source, source ^ bits) for source in range(co...]
    slice x4 -> x0, local copies, waits for them, and re-layouts: 2.24 us -> none  [the longest x1 0.98 us: local(): border = passed_along(inputs_row[rows - edge:], 'ctx', 1)]
    ppermute x0 -> x2, starting transfers between devices: none -> 2.14 us  [linked(): return lax.ppermute(value, axis, pairs + [(b, a) for a, b in pairs])]
    unnamed x12 -> x14, local copies, waits for them, and re-layouts: 4.05 us -> 2.45 us
    squeeze x0 -> x1, local copies, waits for them, and re-layouts: none -> 0.98 us  [local(): border = passed_along(projected[0, rows - edge:], 'ctx', 1)]
  transfers between devices with their start and end apart: 11 -> 13, of which waited for: 3 -> 4; matrix products, arithmetic and copies ran while one was open for 3% -> 0% of each run, Pallas kernels for 22% -> 28%
where the time goes in v2:
time: 71.5 us; the launch traced here: 71 us
  Pallas kernels  36.2 us (51%)
  starting transfers between devices  22.7 us (32%)
  waiting for transfers between devices  6.46 us (9%)
  local copies, waits for them, and re-layouts  4.11 us (6%)
  between operations  0.84 us (1%)
    pallas_call x2, Pallas kernels, make_long(): call(functools.partial(long_kernel, first=first, steps=steps, held=held),...  25.5 us
    ppermute x9, starting transfers between devices, swapped(): lax.ppermute(value, axis, [(source, source ^ bits) for source in range(co...  16.9 us
    pallas_call x2, Pallas kernels, make_gates(): call(functools.partial(gate_kernel, first=first, steps=steps), 'gates', (...  7.69 us
    ppermute x9, waiting for transfers between devices, swapped(): lax.ppermute(value, axis, [(source, source ^ bits) for source in range(co...  6.44 us
    ppermute x2, starting transfers between devices, passed_along(): lax.ppermute(value, axis, [(source, source + steps) for source in range(i...  3.64 us
    unnamed x14, local copies, waits for them, and re-layouts  2.45 us
    pallas_call x1, Pallas kernels, finish_last_rows(): call(last_rows_kernel, 'last_rows', (1,), [whole(value.shape) for value i...  2.14 us
    ppermute x2, starting transfers between devices, linked(): return lax.ppermute(value, axis, pairs + [(b, a) for a, b in pairs])  2.14 us
  transfers between devices with their start and end apart: 13, of which 4 were waited for; matrix products, arithmetic and copies ran while one was open for 0% of the time, Pallas kernels for 28%

profile of v2, /device:TPU:0, one launch (start us, length us, event | category | flops | bytes accessed | tf_op | source)
XLA Modules:
  0.0 71.0 jit_solution(11399839496268601153)
XLA Ops:
  0.6 1.0 %slice_bitcast_fusion = bf16[2,12288]{1,0:T(2,128)(2,1)S(1)} fusion(bf16[1,128,12288]{2,1,0:T(8,128)(2,1)} %param.5), kind=kLoop, calls=%fused_computation.9 | loop fusion | bytes 98304 | tf_op jit(solution)/shard_map/squeeze | solution.py:444
  1.6 2.4 %collective-permute-start = (bf16[2,12288]{1,0:T(2,128)(2,1)S(1)}, bf16[2,12288]{1,0:T(2,128)(2,1)S(1)}, u32[]{:S(2)}, u32[]{:S(2)}) collective-permute-start(bf16[2,12288]{1,0:T(2,128)(2,1)S(1)} %slice_bitcast_fusion), channel_id=1, source_target_pairs={{0,1},{1,2},{2,3},{3,4},{4,5},{5,6},{6,7},{8,9},{9,10},{10,11},{11... | collective-permute-start | bytes 147464 | tf_op jit(solution)/shard_map/ppermute | solution.py:23
  4.0 0.8 %prepare.1 = (bf16[5,128,128]{2,1,0:T(8,128)(2,1)S(1)}, bf16[256,144]{1,0:T(8,128)(2,1)S(1)}, bf16[256,128]{1,0:T(8,128)(2,1)S(1)}, f32[2,8,128]{2,1,0:T(8,128)S(1)}) custom-call(s32[1,1024]{1,0:T(1,128)} %ids_ref.1), custom_call_target="tpu_custom_call" | custom-call | flops 1000000 | bytes 1000000 | tf_op jit(solution)/shard_map/prepare/pallas_call | solution.py:106
  4.8 0.0 copy-start.2
  4.8 0.0 copy-start.4
  4.9 0.0 collective-permute-done.edge_ref
  4.9 3.9 %gates.3 = (bf16[3,128,2048]{2,1,0:T(8,128)(2,1)S(1)}, bf16[128,2048]{1,0:T(8,128)(2,1)S(1)}, bf16[128,2048]{1,0:T(8,128)(2,1)S(1)}) custom-call(bf16[128,12288]{1,0:T(8,128)(2,1)} %bitcast.26, bf16[128,12288]{1,0:T(8,128)(2,1)} %bitcast.27, bf16[128,12288]{1,0:T(8,128)(2,1)} %bitcast.28, bf16[2,12288]{1,0:T(2,128)(2,1)S(1)} %collective-permute-done.edge_ref, ...), custom_call_target="tpu_custom_call" | custom-call | flops 805306368 | bytes 4718592 | tf_op jit(solution)/shard_map/gates/pallas_call | solution.py:159
  8.8 0.0 copy-done.2
  8.8 0.0 copy-done.4
  8.8 3.0 %collective-permute-start.3 = (bf16[128,2048]{1,0:T(8,128)(2,1)S(1)}, bf16[128,2048]{1,0:T(8,128)(2,1)S(1)}, u32[]{:S(2)}, u32[]{:S(2)}) collective-permute-start(bf16[128,2048]{1,0:T(8,128)(2,1)S(1)} %get-tuple-element.32.chip_ref), channel_id=1, source_target_pairs={{0,1},{1,0},{2,3},{3,2},{4,5},{5,4},{6,7},{7,6},{8,9},{9,8},{10,11... | collective-permute-start | bytes 1572872 | tf_op jit(solution)/shard_map/ppermute | solution.py:28
  11.7 1.5 %collective-permute-start.4 = (bf16[128,2048]{1,0:T(8,128)(2,1)S(1)}, bf16[128,2048]{1,0:T(8,128)(2,1)}, u32[]{:S(2)}, u32[]{:S(2)}) collective-permute-start(bf16[128,2048]{1,0:T(8,128)(2,1)S(1)} %get-tuple-element.33.link_ref), channel_id=1, source_target_pairs={{1,2},{3,4},{5,6},{2,1},{4,3},{6,5},{9,10},{11,12},{13,14},{10,9},... | collective-permute-start | bytes 1572872 | tf_op jit(solution)/shard_map/ppermute | solution.py:34
  13.2 0.0 copy-start.3
  13.2 3.8 %gates.2 = (bf16[3,128,2048]{2,1,0:T(8,128)(2,1)S(1)}, bf16[128,2048]{1,0:T(8,128)(2,1)S(1)}, bf16[128,2048]{1,0:T(8,128)(2,1)S(1)}) custom-call(bf16[128,12288]{1,0:T(8,128)(2,1)} %bitcast.29, bf16[128,12288]{1,0:T(8,128)(2,1)} %bitcast.30, bf16[128,12288]{1,0:T(8,128)(2,1)} %bitcast.31, bf16[2,12288]{1,0:T(2,128)(2,1)S(1)} %collective-permute-done.edge_ref, ...), custom_call_target="tpu_custom_call" | custom-call | flops 805306368 | bytes 4718592 | tf_op jit(solution)/shard_map/gates/pallas_call | solution.py:159
  17.0 3.0 %collective-permute-start.1 = (bf16[128,2048]{1,0:T(8,128)(2,1)S(1)}, bf16[128,2048]{1,0:T(8,128)(2,1)S(1)}, u32[]{:S(2)}, u32[]{:S(2)}) collective-permute-start(bf16[128,2048]{1,0:T(8,128)(2,1)S(1)} %get-tuple-element.27.chip_ref), channel_id=1, source_target_pairs={{0,1},{1,0},{2,3},{3,2},{4,5},{5,4},{6,7},{7,6},{8,9},{9,8},{10,11... | collective-permute-start | bytes 1572872 | tf_op jit(solution)/shard_map/ppermute | solution.py:28
  20.0 0.7 collective-permute-start.2
  20.7 0.0 collective-permute-done.3.chip_in_ref
  20.7 0.0 copy-start
  20.7 0.8 %copy-done = bf16[128,2048]{1,0:T(8,128)(2,1)} copy-done((bf16[128,2048]{1,0:T(8,128)(2,1)}, bf16[128,2048]{1,0:T(8,128)(2,1)S(1)}, u32[]{:S(2)}) %copy-start) | copy-done | bytes 524312
  21.5 0.0 collective-permute-done.4.link_in_ref
  21.5 0.0 copy-done.3
  21.5 0.0 copy-done.5
  21.5 0.0 copy-start.1
  21.5 1.0 %copy-done.1 = bf16[128,2048]{1,0:T(8,128)(2,1)S(1)} copy-done((bf16[128,2048]{1,0:T(8,128)(2,1)S(1)}, bf16[128,2048]{1,0:T(8,128)(2,1)}, u32[]{:S(2)}) %copy-start.1) | copy-done | bytes 524312
  22.5 12.7 %long_parts.2 = (bf16[128,4096]{1,0:T(8,128)(2,1)}, bf16[3,2,4096]{2,1,0:T(2,128)(2,1)S(1)}, f32[3,8,4096]{2,1,0:T(8,128)S(1)}, f32[256,128]{1,0:T(8,128)S(1)}, ...) custom-call(bf16[128,2048]{1,0:T(8,128)(2,1)S(1)} %get-tuple-element.32.chip_ref, ...), custom_call_target="tpu_custom_call" | custom-call | flops 6442450944 | bytes 12582912 | tf_op jit(solution)/shard_map/long_parts/pallas_call | solution.py:329
  35.3 0.0 collective-permute-done.1.chip_in_ref
  35.3 0.0 collective-permute-done.2.link_in_ref
  35.3 12.8 %long_parts.3 = (bf16[128,4096]{1,0:T(8,128)(2,1)}, bf16[3,2,4096]{2,1,0:T(2,128)(2,1)S(1)}, f32[3,8,4096]{2,1,0:T(8,128)S(1)}, f32[256,128]{1,0:T(8,128)S(1)}, ...) custom-call(bf16[128,2048]{1,0:T(8,128)(2,1)S(1)} %get-tuple-element, ...), custom_call_target="tpu_custom_call", output_to_operand_aliasing={{0}: (15, {}), {1}: (16, {}), {2}: (17, {}), {3}: (18, {}),... | custom-call | flops 6442450944 | bytes 12582912 | tf_op jit(solution)/shard_map/long_parts/pallas_call | solution.py:329
  48.1 0.0 copy-start.6
  48.1 0.6 copy-done.6
  48.8 3.0 %collective-permute-start.6 = (f32[4,68,128]{2,1,0:T(8,128)S(1)}, f32[4,68,128]{2,1,0:T(8,128)S(1)}, u32[]{:S(2)}, u32[]{:S(2)}) collective-permute-start(f32[4,68,128]{2,1,0:T(8,128)S(1)} %fusion.1), channel_id=1, source_target_pairs={{0,1},{1,0},{2,3},{3,2},{4,5},{5,4},{6,7},{7,6},{8,9},{9,8},{10,11... | collective-permute-start | bytes 417800 | tf_op jit(solution)/shard_map/ppermute | solution.py:28
  51.7 1.0 %collective-permute-done.6 = f32[4,68,128]{2,1,0:T(8,128)S(1)} collective-permute-done((f32[4,68,128]{2,1,0:T(8,128)S(1)}, f32[4,68,128]{2,1,0:T(8,128)S(1)}, u32[]{:S(2)}, u32[]{:S(2)}) %collective-permute-start.6) | collective-permute-done | bytes 139296 | tf_op jit(solution)/shard_map/ppermute | solution.py:28
  52.8 1.7 %collective-permute-start.7 = (f32[68,128]{1,0:T(8,128)S(1)}, f32[68,128]{1,0:T(8,128)S(1)}, u32[]{:S(2)}, u32[]{:S(2)}) collective-permute-start(f32[68,128]{1,0:T(8,128)S(1)} %get-tuple-element.50), channel_id=1, source_target_pairs={{0,2},{1,3},{2,0},{3,1},{4,6},{5,7},{6,4},{7,5},{8,10},{9,11},{10,... | collective-permute-start | bytes 104456 | tf_op jit(solution)/shard_map/ppermute | solution.py:28
  54.4 1.6 %collective-permute-start.8 = (f32[68,128]{1,0:T(8,128)S(1)}, f32[68,128]{1,0:T(8,128)S(1)}, u32[]{:S(2)}, u32[]{:S(2)}) collective-permute-start(f32[68,128]{1,0:T(8,128)S(1)} %get-tuple-element.49), channel_id=1, source_target_pairs={{0,4},{1,5},{2,6},{3,7},{4,0},{5,1},{6,2},{7,3},{8,12},{9,13},{10,... | collective-permute-start | bytes 104456 | tf_op jit(solution)/shard_map/ppermute | solution.py:28
  56.0 1.3 %collective-permute-start.9 = (f32[68,128]{1,0:T(8,128)S(1)}, f32[68,128]{1,0:T(8,128)S(1)}, u32[]{:S(2)}, u32[]{:S(2)}) collective-permute-start(f32[68,128]{1,0:T(8,128)S(1)} %get-tuple-element.48), channel_id=1, source_target_pairs={{0,6},{1,7},{2,4},{3,5},{4,2},{5,3},{6,0},{7,1},{8,14},{9,15},{10,... | collective-permute-start | bytes 104456 | tf_op jit(solution)/shard_map/ppermute | solution.py:28
  57.2 1.3 %collective-permute-start.5 = (bf16[3,2,4096]{2,1,0:T(2,128)(2,1)}, bf16[3,2,4096]{2,1,0:T(2,128)(2,1)S(1)}, u32[]{:S(2)}, u32[]{:S(2)}) collective-permute-start(bf16[3,2,4096]{2,1,0:T(2,128)(2,1)} %copy-done.6), channel_id=1, source_target_pairs={{1,0},{2,1},{3,2},{4,3},{5,4},{6,5},{7,6},{9,8},{10,9},{11,10},{12... | collective-permute-start | bytes 147464 | tf_op jit(solution)/shard_map/ppermute | solution.py:23
  58.5 0.0 collective-permute-done.7
  58.5 1.4 %collective-permute-done.8 = f32[68,128]{1,0:T(8,128)S(1)} collective-permute-done((f32[68,128]{1,0:T(8,128)S(1)}, f32[68,128]{1,0:T(8,128)S(1)}, u32[]{:S(2)}, u32[]{:S(2)}) %collective-permute-start.8) | collective-permute-done | bytes 34848 | tf_op jit(solution)/shard_map/ppermute | solution.py:28
  59.9 1.8 %collective-permute-done.9 = f32[68,128]{1,0:T(8,128)S(1)} collective-permute-done((f32[68,128]{1,0:T(8,128)S(1)}, f32[68,128]{1,0:T(8,128)S(1)}, u32[]{:S(2)}, u32[]{:S(2)}) %collective-permute-start.9) | collective-permute-done | bytes 34848 | tf_op jit(solution)/shard_map/ppermute | solution.py:28
  61.8 1.6 %collective-permute-start.10 = (f32[68,128]{1,0:T(8,128)S(1)}, f32[68,128]{1,0:T(8,128)S(1)}, u32[]{:S(2)}, u32[]{:S(2)}) collective-permute-start(f32[68,128]{1,0:T(8,128)S(1)} %fusion.5), channel_id=1, source_target_pairs={{0,8},{8,0},{16,24},{24,16},{1,9},{9,1},{17,25},{25,17},{2,10},{10... | collective-permute-start | bytes 104456 | tf_op jit(solution)/shard_map/ppermute | solution.py:28
  63.3 1.5 %collective-permute-start.11 = (f32[68,128]{1,0:T(8,128)S(1)}, f32[68,128]{1,0:T(8,128)S(1)}, u32[]{:S(2)}, u32[]{:S(2)}) collective-permute-start(f32[68,128]{1,0:T(8,128)S(1)} %fusion.5), channel_id=1, source_target_pairs={{0,16},{8,24},{16,0},{24,8},{1,17},{9,25},{17,1},{25,9},{2,18},{10... | collective-permute-start | bytes 104456 | tf_op jit(solution)/shard_map/ppermute | solution.py:28
  64.8 0.5 collective-permute-start.12
  65.3 0.0 collective-permute-done.5.ahead_ref
  65.3 2.1 %last_rows.1 = bf16[128,12288]{1,0:T(8,128)(2,1)} custom-call(f32[3,8,4096]{2,1,0:T(8,128)S(1)} %get-tuple-element.42.tail_ref, bf16[3,2,4096]{2,1,0:T(2,128)(2,1)S(1)} %collective-permute-done.5.ahead_ref, f32[3,12288]{1,0:T(4,128)} %w_ref.9, f32[2,8,128]{2,1,0:T(8,128)S(1)} %get-tuple-element.44.late_ref, ...), custom_call_target="tpu_custom_call", output_to_operand_aliasing={{}: (4, {})} | custom-call | flops 1000000 | bytes 2000000 | tf_op jit(solution)/shard_map/last_rows/pallas_call | solution.py:379
  67.5 0.0 collective-permute-done.10
  67.5 0.0 collective-permute-done.11
  67.5 2.2 %collective-permute-done.12 = f32[68,128]{1,0:T(8,128)S(1)} collective-permute-done((f32[68,128]{1,0:T(8,128)S(1)}, f32[68,128]{1,0:T(8,128)S(1)}, u32[]{:S(2)}, u32[]{:S(2)}) %collective-permute-start.12) | collective-permute-done | bytes 34848 | tf_op jit(solution)/shard_map/ppermute | solution.py:28
  69.7 0.6 slice_multiply_fusion.1
  70.4 0.6 div.33
  (10 shorter events, 0.1 us)
Async XLA Ops:
  1.6 3.2 %collective-permute-start = (bf16[2,12288]{1,0:T(2,128)(2,1)S(1)}, bf16[2,12288]{1,0:T(2,128)(2,1)S(1)}, u32[]{:S(2)}, u32[]{:S(2)}) collective-permute-start(bf16[2,12288]{1,0:T(2,128)(2,1)S(1)} %slice_bitcast_fusion), channel_id=1, source_target_pairs={{0,1},{1,2},{2,3},{3,4},{4,5},{5,6},{6,7},{8,9},{9,10},{10,11},{11... | collective-permute-start | bytes 147464 | tf_op jit(solution)/shard_map/ppermute | solution.py:23
  4.8 3.9 %copy-start.2 = (bf16[5,128,128]{2,1,0:T(8,128)(2,1)}, bf16[5,128,128]{2,1,0:T(8,128)(2,1)S(1)}, u32[]{:S(2)}) copy-start(bf16[5,128,128]{2,1,0:T(8,128)(2,1)S(1)} %get-tuple-element.29.long_ref) | copy-start | bytes 491524
  4.8 3.9 %copy-start.4 = (bf16[256,128]{1,0:T(8,128)(2,1)}, bf16[256,128]{1,0:T(8,128)(2,1)S(1)}, u32[]{:S(2)}) copy-start(bf16[256,128]{1,0:T(8,128)(2,1)S(1)} %get-tuple-element.30.ahead_ref) | copy-start | bytes 196612
  8.8 11.9 %collective-permute-start.3 = (bf16[128,2048]{1,0:T(8,128)(2,1)S(1)}, bf16[128,2048]{1,0:T(8,128)(2,1)S(1)}, u32[]{:S(2)}, u32[]{:S(2)}) collective-permute-start(bf16[128,2048]{1,0:T(8,128)(2,1)S(1)} %get-tuple-element.32.chip_ref), channel_id=1, source_target_pairs={{0,1},{1,0},{2,3},{3,2},{4,5},{5,4},{6,7},{7,6},{8,9},{9,8},{10,11... | collective-permute-start | bytes 1572872 | tf_op jit(solution)/shard_map/ppermute | solution.py:28
  11.7 9.7 %collective-permute-start.4 = (bf16[128,2048]{1,0:T(8,128)(2,1)S(1)}, bf16[128,2048]{1,0:T(8,128)(2,1)}, u32[]{:S(2)}, u32[]{:S(2)}) collective-permute-start(bf16[128,2048]{1,0:T(8,128)(2,1)S(1)} %get-tuple-element.33.link_ref), channel_id=1, source_target_pairs={{1,2},{3,4},{5,6},{2,1},{4,3},{6,5},{9,10},{11,12},{13,14},{10,9},... | collective-permute-start | bytes 1572872 | tf_op jit(solution)/shard_map/ppermute | solution.py:34
  13.2 8.3 %copy-start.3 = (bf16[5,128,128]{2,1,0:T(8,128)(2,1)S(1)}, bf16[5,128,128]{2,1,0:T(8,128)(2,1)}, u32[]{:S(2)}) copy-start(bf16[5,128,128]{2,1,0:T(8,128)(2,1)} %copy-done.2) | copy-start | bytes 491524
  13.2 8.3 %copy-start.5 = (bf16[256,128]{1,0:T(8,128)(2,1)S(1)}, bf16[256,128]{1,0:T(8,128)(2,1)}, u32[]{:S(2)}) copy-start(bf16[256,128]{1,0:T(8,128)(2,1)} %copy-done.4) | copy-start | bytes 196612
  17.0 18.2 %collective-permute-start.1 = (bf16[128,2048]{1,0:T(8,128)(2,1)S(1)}, bf16[128,2048]{1,0:T(8,128)(2,1)S(1)}, u32[]{:S(2)}, u32[]{:S(2)}) collective-permute-start(bf16[128,2048]{1,0:T(8,128)(2,1)S(1)} %get-tuple-element.27.chip_ref), channel_id=1, source_target_pairs={{0,1},{1,0},{2,3},{3,2},{4,5},{5,4},{6,7},{7,6},{8,9},{9,8},{10,11... | collective-permute-start | bytes 1572872 | tf_op jit(solution)/shard_map/ppermute | solution.py:28
  20.0 15.3 %collective-permute-start.2 = (bf16[128,2048]{1,0:T(8,128)(2,1)S(1)}, bf16[128,2048]{1,0:T(8,128)(2,1)S(1)}, u32[]{:S(2)}, u32[]{:S(2)}) collective-permute-start(bf16[128,2048]{1,0:T(8,128)(2,1)S(1)} %get-tuple-element.28.link_ref), channel_id=1, source_target_pairs={{1,2},{3,4},{5,6},{2,1},{4,3},{6,5},{9,10},{11,12},{13,14},{10,9},... | collective-permute-start | bytes 1572872 | tf_op jit(solution)/shard_map/ppermute | solution.py:34
  20.7 0.8 %copy-start = (bf16[128,2048]{1,0:T(8,128)(2,1)}, bf16[128,2048]{1,0:T(8,128)(2,1)S(1)}, u32[]{:S(2)}) copy-start(bf16[128,2048]{1,0:T(8,128)(2,1)S(1)} %collective-permute-done.3.chip_in_ref) | copy-start | bytes 1572868
  21.5 1.0 %copy-start.1 = (bf16[128,2048]{1,0:T(8,128)(2,1)S(1)}, bf16[128,2048]{1,0:T(8,128)(2,1)}, u32[]{:S(2)}) copy-start(bf16[128,2048]{1,0:T(8,128)(2,1)} %copy-done) | copy-start | bytes 1572868
  48.1 0.6 copy-start.6
  48.8 4.0 %collective-permute-start.6 = (f32[4,68,128]{2,1,0:T(8,128)S(1)}, f32[4,68,128]{2,1,0:T(8,128)S(1)}, u32[]{:S(2)}, u32[]{:S(2)}) collective-permute-start(f32[4,68,128]{2,1,0:T(8,128)S(1)} %fusion.1), channel_id=1, source_target_pairs={{0,1},{1,0},{2,3},{3,2},{4,5},{5,4},{6,7},{7,6},{8,9},{9,8},{10,11... | collective-permute-start | bytes 417800 | tf_op jit(solution)/shard_map/ppermute | solution.py:28
  52.8 5.8 %collective-permute-start.7 = (f32[68,128]{1,0:T(8,128)S(1)}, f32[68,128]{1,0:T(8,128)S(1)}, u32[]{:S(2)}, u32[]{:S(2)}) collective-permute-start(f32[68,128]{1,0:T(8,128)S(1)} %get-tuple-element.50), channel_id=1, source_target_pairs={{0,2},{1,3},{2,0},{3,1},{4,6},{5,7},{6,4},{7,5},{8,10},{9,11},{10,... | collective-permute-start | bytes 104456 | tf_op jit(solution)/shard_map/ppermute | solution.py:28
  54.4 5.5 %collective-permute-start.8 = (f32[68,128]{1,0:T(8,128)S(1)}, f32[68,128]{1,0:T(8,128)S(1)}, u32[]{:S(2)}, u32[]{:S(2)}) collective-permute-start(f32[68,128]{1,0:T(8,128)S(1)} %get-tuple-element.49), channel_id=1, source_target_pairs={{0,4},{1,5},{2,6},{3,7},{4,0},{5,1},{6,2},{7,3},{8,12},{9,13},{10,... | collective-permute-start | bytes 104456 | tf_op jit(solution)/shard_map/ppermute | solution.py:28
  56.0 5.8 %collective-permute-start.9 = (f32[68,128]{1,0:T(8,128)S(1)}, f32[68,128]{1,0:T(8,128)S(1)}, u32[]{:S(2)}, u32[]{:S(2)}) collective-permute-start(f32[68,128]{1,0:T(8,128)S(1)} %get-tuple-element.48), channel_id=1, source_target_pairs={{0,6},{1,7},{2,4},{3,5},{4,2},{5,3},{6,0},{7,1},{8,14},{9,15},{10,... | collective-permute-start | bytes 104456 | tf_op jit(solution)/shard_map/ppermute | solution.py:28
  57.2 8.1 %collective-permute-start.5 = (bf16[3,2,4096]{2,1,0:T(2,128)(2,1)}, bf16[3,2,4096]{2,1,0:T(2,128)(2,1)S(1)}, u32[]{:S(2)}, u32[]{:S(2)}) collective-permute-start(bf16[3,2,4096]{2,1,0:T(2,128)(2,1)} %copy-done.6), channel_id=1, source_target_pairs={{1,0},{2,1},{3,2},{4,3},{5,4},{6,5},{7,6},{9,8},{10,9},{11,10},{12... | collective-permute-start | bytes 147464 | tf_op jit(solution)/shard_map/ppermute | solution.py:23
  61.8 5.7 %collective-permute-start.10 = (f32[68,128]{1,0:T(8,128)S(1)}, f32[68,128]{1,0:T(8,128)S(1)}, u32[]{:S(2)}, u32[]{:S(2)}) collective-permute-start(f32[68,128]{1,0:T(8,128)S(1)} %fusion.5), channel_id=1, source_target_pairs={{0,8},{8,0},{16,24},{24,16},{1,9},{9,1},{17,25},{25,17},{2,10},{10... | collective-permute-start | bytes 104456 | tf_op jit(solution)/shard_map/ppermute | solution.py:28
  63.3 4.2 %collective-permute-start.11 = (f32[68,128]{1,0:T(8,128)S(1)}, f32[68,128]{1,0:T(8,128)S(1)}, u32[]{:S(2)}, u32[]{:S(2)}) collective-permute-start(f32[68,128]{1,0:T(8,128)S(1)} %fusion.5), channel_id=1, source_target_pairs={{0,16},{8,24},{16,0},{24,8},{1,17},{9,25},{17,1},{25,9},{2,18},{10... | collective-permute-start | bytes 104456 | tf_op jit(solution)/shard_map/ppermute | solution.py:28
  64.8 4.9 %collective-permute-start.12 = (f32[68,128]{1,0:T(8,128)S(1)}, f32[68,128]{1,0:T(8,128)S(1)}, u32[]{:S(2)}, u32[]{:S(2)}) collective-permute-start(f32[68,128]{1,0:T(8,128)S(1)} %fusion.5), channel_id=1, source_target_pairs={{0,24},{8,16},{16,8},{24,0},{1,25},{9,17},{17,9},{25,1},{2,26},{10... | collective-permute-start | bytes 104456 | tf_op jit(solution)/shard_map/ppermute | solution.py:28

commit v3 on v2

--- a/solution.py
+++ b/solution.py
@@ -12,9 +12,10 @@
 F32 = jnp.float32
 LANES = 128
 EDGE = 16
-WIDTH = 512
+WIDTH = 1024
+GATE_WIDTH = 2048
+PIECE = 4
 PARTS = 2
-VMEM = 32 * 1024 * 1024
 
 
 def passed_along(value, axis, steps):
@@ -38,7 +39,9 @@
     return pl.BlockSpec(shape, lambda *_: (0,) * len(shape))
 
 
-def call(kernel, name, grid, in_specs, out_specs, out_shape, cost, scratch=(), aliases=None):
+def call(
+    kernel, name, grid, in_specs, out_specs, out_shape, cost, scratch=(), aliases=None, mib=16
+):
     return pl.pallas_call(
         kernel,
         name=name,
@@ -48,7 +51,7 @@
         out_shape=out_shape,
         scratch_shapes=list(scratch),
         input_output_aliases=aliases or {},
-        compiler_params=pltpu.CompilerParams(vmem_limit_bytes=VMEM),
+        compiler_params=pltpu.CompilerParams(vmem_limit_bytes=mib * 1024 * 1024),
         cost_estimate=pl.CostEstimate(flops=cost[0], bytes_accessed=cost[1], transcendentals=0),
     )
 
@@ -73,6 +76,7 @@
     here_row = id_row(here, here >= 0)
     next_row = id_row(here + 1, here < last)
     here_col = jnp.transpose(here_row)
+    prev_col = jnp.transpose(prev_row)
     rows = lax.broadcasted_iota(jnp.int32, (taps, taps), 0)
     cols = lax.broadcasted_iota(jnp.int32, (taps, taps), 1)
 
@@ -80,11 +84,10 @@
         return jnp.where(condition, 1.0, 0.0).astype(BF)
 
     same = here_col == here_row
-    long_ref[0] = put((cols <= rows) & same)
-    long_ref[1] = put((cols > rows) & (here_col == prev_row))
-    long_ref[2] = put((cols >= rows) & same)
-    long_ref[3] = put((cols < rows) & (here_col == next_row))
-    long_ref[4] = put(((cols >= rows) & same) | ((cols < rows) & (here_col == next_row)))
+    long_ref[0] = put((cols >= rows) & same)
+    long_ref[1] = put((cols < rows) & (prev_col == here_row))
+    long_ref[2] = put((cols < rows) & (here_col == next_row))
+    long_ref[3] = put(((cols >= rows) & same) | ((cols < rows) & (here_col == next_row)))
     last_prev = here_col == pltpu.roll(prev_row, 2, 1)
     first_next = here_col == next_row
     for j in (1, 2):
@@ -98,7 +101,7 @@
 
 def prepare(doc_ids, taps):
     shapes = [
-        ((5, taps, taps), BF),
+        ((4, taps, taps), BF),
         ((2 * taps, taps + EDGE), BF),
         ((2 * taps, taps), BF),
         ((2, 8, taps), F32),
@@ -151,7 +154,7 @@
 
 def make_gates(inputs, border, weights, cotangent, back_mask, part, parts):
     rows, model_width = cotangent.shape
-    width = WIDTH
+    width = GATE_WIDTH
     steps = model_width // width
     held = steps // parts
     first = part * held
@@ -174,15 +177,16 @@
             pltpu.VMEM((rows, held * width), BF),
         ],
         (2 * 256 * 256 * 3 * held * width, 9 * rows * held * width * 2),
+        mib=32,
     )(inputs, inputs, inputs, border, weights, cotangent, back_mask)
 
 
 def long_kernel(
-    chip_ref, chip_in_ref, link_ref, link_in_ref, filter_ref, long_ref, back_ref, ahead_ref,
+    chip_in_ref, link_in_ref, filter_ref, long_ref, back_ref, ahead_ref,
     mixed_ref, cot_ref, xq, xk, xv, edge_ref, w_ref, *rest, first, steps, held,
 ):
     out_ref, head_ref, tail_ref, gl_ref, gs_ref, inputs_ref, diag, staged, sems = rest[-9:]
-    rows_here, width = chip_ref.shape
+    rows_here, width = chip_in_ref.shape
     first_core = lax.axis_index("ctx") % 2 == 0
     taps = filter_ref.shape[1]
     subs = width // LANES
@@ -213,11 +217,11 @@
     for u in range(subs):
         ls = slice(u * LANES, (u + 1) * LANES)
         gs = slice(u * per, (u + 1) * per)
-        one_side = jnp.concatenate([chip_ref[:, ls], link_in_ref[:, ls]], axis=0)
-        other_side = jnp.concatenate([link_ref[:, ls], chip_in_ref[:, ls]], axis=0)
-        sources = jnp.where(first_core, one_side, other_side)
-        grads = jnp.where(first_core, other_side, one_side)
-        here = sources[:rows_here]
+        here = mixed_ref[1, :, ls] * mixed_ref[2, :, ls]
+        grad = cot_ref[:, ls] * mixed_ref[0, :, ls]
+        chip_in, link_in = chip_in_ref[:, ls], link_in_ref[:, ls]
+        sources = jnp.concatenate([here, jnp.where(first_core, link_in, chip_in)], axis=0)
+        grads = jnp.concatenate([grad, jnp.where(first_core, chip_in, link_in)], axis=0)
         filters = filter_ref[gs].astype(F32)
         turned = [
             pltpu.roll(
@@ -225,17 +229,23 @@
             ).astype(BF)
             for g in range(per)
         ]
-        upright = [jnp.transpose(turned[g]) for g in range(per)]
-
-        def long_conv(circulants, first_mask, stacked):
-            left = jnp.concatenate(
-                [part * long_ref[first_mask + n] for part in circulants for n in range(2)], axis=1
-            )
-            right = jnp.concatenate([stacked * lane[g] for g in range(per)], axis=0)
-            return jnp.dot(left, right, preferred_element_type=F32).astype(BF)
-
-        long_mix = long_conv(upright, 0, sources)
-        grad_product = long_conv(turned, 2, grads)
+        near = [part * long_ref[0] for part in turned]
+
+        def long_conv(far, stacked, dims):
+            across = jnp.transpose(stacked)
+            parts = []
+            for g in range(per):
+                taken = across[g * share : (g + 1) * share]
+                right = jnp.concatenate([near[g], turned[g] * long_ref[far]], axis=dims)
+                parts.append(
+                    lax.dot_general(
+                        taken, right, (((1,), (dims,)), ((), ())), preferred_element_type=F32
+                    )
+                )
+            return jnp.transpose(jnp.concatenate(parts, axis=0).astype(BF))
+
+        long_mix = long_conv(1, sources, 0)
+        grad_product = long_conv(2, grads, 1)
         out_ref[:, ls] = mixed_ref[0, :, ls] * long_mix
         mixed_grads[0].append(cot_ref[:, ls] * long_mix)
         mixed_grads[1].append(grad_product * mixed_ref[2, :, ls])
@@ -245,7 +255,7 @@
         inner = lax.dot_general(
             spread, grads, (((1,), (1,)), ((), ())), preferred_element_type=F32
         ).reshape(per, taps // 8, 8, 2 * taps)
-        keep = long_ref[4].astype(F32)
+        keep = long_ref[3].astype(F32)
         total = None
         for k in range(taps // 8):
             nearer = (cols >= rows + 8 * k)[None]
@@ -263,7 +273,13 @@
     edge_keep = back_ref[:, taps : taps + 2].astype(F32)
     for b, x_ref in enumerate((xq, xk, xv)):
         mixed_grad = jnp.concatenate(mixed_grads[b], axis=1)
-        head_ref[b] = mixed_grad[:2]
+        first_rows = mixed_grad[:16].astype(F32)
+        for u in range(subs):
+            for r in range(2):
+                at_row = r * PIECE + u % PIECE
+                head_ref[b, u // PIECE, at_row : at_row + 1, :] = first_rows[
+                    r : r + 1, u * LANES : (u + 1) * LANES
+                ]
         both = jnp.dot(ahead_ref[...], mixed_grad, preferred_element_type=F32)
         one, two = both[:rows_here], both[rows_here:]
         at = column(i, b)
@@ -273,7 +289,6 @@
         leaving(i, b).start()
         values = x_ref[...].astype(F32)
         edge = edge_ref[:, at].astype(F32)
-        first_rows = mixed_grad[:16].astype(F32)
         over_edge = (
             None,
             edge_keep[0:1, 1:2] * first_rows[0:1] * edge[1:2],
@@ -285,7 +300,8 @@
             if j:
                 summed = summed + over_edge[j]
             for u in range(subs):
-                gs_ref[b, 0, j * subs + u : j * subs + u + 1, :] = summed[
+                at_row = j * PIECE + u % PIECE
+                gs_ref[b, u // PIECE, at_row : at_row + 1, :] = summed[
                     :, u * LANES : (u + 1) * LANES
                 ]
 
@@ -297,7 +313,7 @@
             leaving(i, b).wait()
 
 
-def make_long(chip, chip_in, link, link_in, filters, masks, mixed, cotangent, inputs, border,
+def make_long(chip_in, link_in, filters, masks, mixed, cotangent, inputs, border,
               weights, part, parts, so_far):
     rows, model_width = cotangent.shape
     groups, taps = filters.shape
@@ -307,14 +323,15 @@
     first = part * held
     subs = width // LANES
     step_groups = groups // steps
+    pieces = model_width // (PIECE * LANES)
     long_masks, back_mask, ahead_mask, _ = masks
     plain = pl.BlockSpec((rows, width), lambda i: (0, i))
     placed = pl.BlockSpec((rows, width), lambda i: (0, first + i))
     anywhere = pl.BlockSpec(memory_space=pl.ANY)
-    operands = [chip, chip_in, link, link_in, filters, long_masks, back_mask, ahead_mask, mixed,
+    operands = [chip_in, link_in, filters, long_masks, back_mask, ahead_mask, mixed,
                 cotangent, inputs, inputs, inputs, border, weights]
     in_specs = (
-        [plain] * 4
+        [plain] * 2
         + [pl.BlockSpec((step_groups, taps), lambda i: (first + i, 0))]
         + [whole(mask.shape) for mask in (long_masks, back_mask, ahead_mask)]
         + [pl.BlockSpec((3, rows, width), lambda i: (0, 0, i)), placed]
@@ -333,18 +350,18 @@
         in_specs,
         [
             placed,
-            pl.BlockSpec((3, 2, width), lambda i: (0, 0, first + i)),
+            pl.BlockSpec((3, subs // PIECE, 2 * PIECE, LANES), lambda i: (0, first + i, 0, 0)),
             pl.BlockSpec((3, 8, width), lambda i: (0, 0, first + i)),
             pl.BlockSpec((step_groups, taps), lambda i: (first + i, 0)),
-            pl.BlockSpec((3, 1, 3 * subs, LANES), lambda i: (0, first + i, 0, 0)),
+            pl.BlockSpec((3, subs // PIECE, 3 * PIECE, LANES), lambda i: (0, first + i, 0, 0)),
             anywhere,
         ],
         [
             jax.ShapeDtypeStruct((rows, model_width), BF),
-            jax.ShapeDtypeStruct((3, 2, model_width), BF),
+            jax.ShapeDtypeStruct((3, pieces, 2 * PIECE, LANES), F32),
             jax.ShapeDtypeStruct((3, 8, model_width), F32),
             jax.ShapeDtypeStruct((groups, taps), F32),
-            jax.ShapeDtypeStruct((3, steps, 3 * subs, LANES), F32),
+            jax.ShapeDtypeStruct((3, pieces, 3 * PIECE, LANES), F32),
             jax.ShapeDtypeStruct((rows, 3 * model_width), BF),
         ],
         (3 * groups * 2 * 128 * 256 * 256 // parts, 24 * 1024 * 1024 // parts),
@@ -354,21 +371,26 @@
             pltpu.SemaphoreType.DMA((2, 3)),
         ],
         aliases,
+        32,
     )(*operands)
 
 
 def last_rows_kernel(tail_ref, ahead_ref, w_ref, late_ref, old_ref, out_ref):
     lines = old_ref.shape[0]
-    width = tail_ref.shape[2]
+    pieces = tail_ref.shape[2] // (PIECE * LANES)
     first_keep, second_keep = late_ref[0, :, 0:1], late_ref[1, :, 0:1]
     next_keep = late_ref[1, :, 1:2]
-    for b in range(3):
-        at = slice(b * width, (b + 1) * width)
-        ahead = ahead_ref[b].astype(F32)
-        first, second = ahead[0:1], ahead[1:2]
+    for n in range(3 * pieces):
+        b, piece = n // pieces, n % pieces
+        first, second = [
+            jnp.concatenate([ahead_ref[n, r * PIECE + u : r * PIECE + u + 1] for u in range(PIECE)], 1)
+            for r in range(2)
+        ]
+        at = slice(n * PIECE * LANES, (n + 1) * PIECE * LANES)
         extra = w_ref[1:2, at] * (first_keep * first)
         extra = extra + w_ref[2:3, at] * (second_keep * first + next_keep * second)
-        ending = (tail_ref[b] + extra).astype(BF)
+        within = slice(piece * PIECE * LANES, (piece + 1) * PIECE * LANES)
+        ending = (tail_ref[b, :, within] + extra).astype(BF)
         out_ref[:, at] = jnp.concatenate([old_ref[: lines // 2, at], ending], axis=0)
 
 
@@ -388,49 +410,90 @@
     )(tail, ahead_rows, weights, late_mask, grad_inputs)
 
 
-def summed_over_windows(value):
+def window_parts(value):
     count = lax.axis_size("dp")
-    if count & (count - 1):
-        return lax.psum(value, "dp")
-    parts = [value] + [swapped(value, "dp", bits) for bits in range(1, count)]
-    while len(parts) > 1:
-        parts = [parts[i] + parts[i + 1] for i in range(0, len(parts), 2)]
-    return parts[0]
-
-
-def owned_sums(short_parts, long_parts):
-    branches, steps, short_rows, lanes = short_parts.shape
+    if count != 4:
+        return [lax.psum(value, "dp")]
+    return [value] + [swapped(value, "dp", bits) for bits in range(1, count)]
+
+
+def from_next_chip(value):
+    count = lax.axis_size("ctx")
+    return lax.ppermute(value, "ctx", [(i, i - 1) for i in range(2, count, 2)])
+
+
+def owned_sums(short_parts, long_parts, head):
+    branches, pieces, short_rows, lanes = short_parts.shape
     groups, taps = long_parts.shape
-    subs = short_rows // 3
+    head_rows = head.shape[2]
     ctx_parts = lax.axis_size("ctx")
-    pieces = branches * steps
-    if ctx_parts != 8 or pieces % ctx_parts or lanes != taps:
-        weight_grad = short_parts.reshape(branches, steps, 3, subs, lanes).transpose(2, 0, 1, 3, 4)
+    total_pieces = branches * pieces
+    head_flat = head.reshape(total_pieces * head_rows, lanes)
+    if ctx_parts != 8 or total_pieces % ctx_parts or lanes != taps:
+        weight_grad = short_parts.reshape(branches, pieces, 3, PIECE, lanes).transpose(2, 0, 1, 3, 4)
         weight_part = lax.psum_scatter(
             weight_grad.reshape(3, -1), "ctx", scatter_dimension=1, tiled=True
         )
         filter_part = lax.psum_scatter(long_parts, "ctx", scatter_dimension=0, tiled=True)
-        return lax.psum((weight_part, filter_part), "dp")
-    held = pieces // ctx_parts
+        weight_total, filter_total = lax.psum((weight_part, filter_part), "dp")
+        return passed_along(head_flat, "ctx", -1), weight_total, filter_total
+    held = total_pieces // ctx_parts
+    chips = ctx_parts // 2
     short_owned = short_parts.reshape(ctx_parts, held * short_rows, lanes)
     long_owned = long_parts.reshape(ctx_parts, groups // ctx_parts, taps)
     joined = jnp.concatenate([short_owned, long_owned], axis=1)
     height = joined.shape[1]
     my_index = lax.axis_index("ctx")
     core, chip = my_index % 2, my_index // 2
-    by_core = joined.reshape(ctx_parts // 2, 2, height, lanes)
+    by_core = joined.reshape(chips, 2, height, lanes)
     kept = lax.dynamic_index_in_dim(by_core, core, 1, keepdims=False)
     given = lax.dynamic_index_in_dim(by_core, 1 - core, 1, keepdims=False)
-    paired = kept + swapped(given, "ctx", 1)
+    message = jnp.concatenate([given.reshape(chips * height, lanes), head_flat], axis=0)
+    answer = swapped(message, "ctx", 1)
+    paired = kept + answer[: chips * height].reshape(chips, height, lanes)
+    partner_head = answer[chips * height :]
     mine = lax.dynamic_index_in_dim(paired, chip, 0, keepdims=False)
+    rounded = paired.astype(BF)
     others = [
-        swapped(lax.dynamic_index_in_dim(paired, chip ^ d, 0, keepdims=False), "ctx", 2 * d)
-        for d in range(1, ctx_parts // 2)
+        swapped(lax.dynamic_index_in_dim(rounded, chip ^ d, 0, keepdims=False), "ctx", 2 * d)
+        for d in range(1, chips)
     ]
+    others = [value.astype(F32) for value in others]
     total = (mine + others[0]) + (others[1] + others[2])
-    total = summed_over_windows(total)
-    short_total = total[: held * short_rows].reshape(held, 3, subs, lanes).transpose(1, 0, 2, 3)
-    return short_total.reshape(3, held * subs * lanes), total[held * short_rows :]
+    next_head = from_next_chip(head_flat.astype(BF)).astype(F32)
+    ahead = jnp.where(core == 0, partner_head, next_head)
+    return ahead, total, None
+
+
+def finish_kernel(*refs, scales):
+    *parts, short_ref, long_ref = refs
+    values = [part[...] for part in parts]
+    while len(values) > 1:
+        values = [values[i] + values[i + 1] for i in range(0, len(values), 2)]
+    total = values[0]
+    held = short_ref.shape[1] // (PIECE * LANES)
+    short_part = total[: held * 3 * PIECE] / scales[0]
+    for piece in range(held):
+        for j in range(3):
+            for u in range(PIECE):
+                row = (piece * 3 + j) * PIECE + u
+                column = (piece * PIECE + u) * LANES
+                short_ref[j : j + 1, column : column + LANES] = short_part[row : row + 1]
+    long_ref[...] = total[held * 3 * PIECE :] / scales[1]
+
+
+def finish(parts, held, scales):
+    height, lanes = parts[0].shape
+    shapes = [(3, held * PIECE * lanes), (height - held * 3 * PIECE, lanes)]
+    return call(
+        functools.partial(finish_kernel, scales=scales),
+        "finish",
+        (),
+        [whole(part.shape) for part in parts],
+        [whole(shape) for shape in shapes],
+        [jax.ShapeDtypeStruct(shape, F32) for shape in shapes],
+        (100000, 400000),
+    )(*parts)
 
 
 def local(projected, doc_ids, short_filter, long_filter, cotangent):
@@ -452,23 +515,28 @@
         mixed, chip, link = make_gates(
             inputs_row, border, short_filter, grad_row, masks[1], part, PARTS
         )
+        link_in = linked(link, "ctx")
         chip_in = swapped(chip, "ctx", 1)
-        link_in = linked(link, "ctx")
-        gated.append((mixed, chip, chip_in, link, link_in))
+        if part + 1 < PARTS:
+            chip_in, link_in = in_hbm(chip_in), in_hbm(link_in)
+        gated.append((mixed, chip_in, link_in))
     done = None
-    for part, (mixed, chip, chip_in, link, link_in) in enumerate(gated):
+    for part, (mixed, chip_in, link_in) in enumerate(gated):
         done = make_long(
-            chip, chip_in, link, link_in, filters, masks, mixed, grad_row, inputs_row, border,
+            chip_in, link_in, filters, masks, mixed, grad_row, inputs_row, border,
             short_filter, part, PARTS, done,
         )
     block_out, head, tail, long_parts, short_parts, grad_inputs = done
-    ahead_rows = passed_along(head, "ctx", -1)
-    grad_inputs = finish_last_rows(grad_inputs, tail, ahead_rows, short_filter, masks[3])
-    weight_total, filter_total = owned_sums(short_parts, long_parts)
     norm_scale = lax.axis_size("dp") * length
-    group_size = model_width // groups
-    grad_short = weight_total / math.sqrt(norm_scale)
-    grad_long = filter_total / math.sqrt(norm_scale * group_size)
+    scales = (math.sqrt(norm_scale), math.sqrt(norm_scale * (model_width // groups)))
+    ahead, total, filter_total = owned_sums(short_parts, long_parts, head)
+    ahead = ahead.reshape(-1, 2 * PIECE, LANES)
+    grad_inputs = finish_last_rows(grad_inputs, tail, ahead, short_filter, masks[3])
+    if filter_total is None:
+        held = 3 * model_width // (PIECE * LANES * lax.axis_size("ctx"))
+        grad_short, grad_long = finish(window_parts(total), held, scales)
+    else:
+        grad_short, grad_long = total / scales[0], filter_total / scales[1]
     return (block_out[None], grad_inputs[None], grad_short, grad_long)
 
 

time: 71.5 us -> 65.3 us (0.913)
  Pallas kernels: 36.2 us -> 31.9 us
  local copies, waits for them, and re-layouts: 4.11 us -> 1.05 us
  waiting for transfers between devices: 6.46 us -> 8.38 us
    pallas_call x2, Pallas kernels: 25.5 us -> 22.9 us  [make_long(): call(functools.partial(long_kernel, first=first, steps=steps, held=held),...]
    unnamed x14 -> x0, local copies, waits for them, and re-layouts: 2.45 us -> none
    pallas_call x2, Pallas kernels: 7.69 us -> 5.44 us  [make_gates(): call(functools.partial(gate_kernel, first=first, steps=steps), 'gates', (...]
    ppermute x9, waiting for transfers between devices: 6.44 us -> 8.37 us  [swapped(): lax.ppermute(value, axis, [(source, source ^ bits) for source in range(co...]
    ppermute x2 -> x1, starting transfers between devices: 3.64 us -> 2.36 us  [passed_along(): lax.ppermute(value, axis, [(source, source + steps) for source in range(i...]
  transfers between devices with their start and end apart: 13 -> 13, of which waited for: 4 -> 4; matrix products, arithmetic and copies ran while one was open for 0% -> 0% of each run, Pallas kernels for 28% -> 26%
where the time goes in v3:
time: 65.3 us; the launch traced here: 65 us
  Pallas kernels  31.9 us (49%)
  starting transfers between devices  22.7 us (35%)
  waiting for transfers between devices  8.38 us (13%)
  local copies, waits for them, and re-layouts  1.05 us (2%)
  between operations  0.82 us (1%)
    pallas_call x2, Pallas kernels, make_long(): call(functools.partial(long_kernel, first=first, steps=steps, held=held),...  22.9 us
    ppermute x9, starting transfers between devices, swapped(): lax.ppermute(value, axis, [(source, source ^ bits) for source in range(co...  17.4 us
    ppermute x9, waiting for transfers between devices, swapped(): lax.ppermute(value, axis, [(source, source ^ bits) for source in range(co...  8.37 us
    pallas_call x2, Pallas kernels, make_gates(): call(functools.partial(gate_kernel, first=first, steps=steps), 'gates', (...  5.44 us
    ppermute x1, starting transfers between devices, passed_along(): lax.ppermute(value, axis, [(source, source + steps) for source in range(i...  2.36 us
    ppermute x2, starting transfers between devices, linked(): return lax.ppermute(value, axis, pairs + [(b, a) for a, b in pairs])  2.32 us
    pallas_call x1, Pallas kernels, finish_last_rows(): call(last_rows_kernel, 'last_rows', (1,), [whole(value.shape) for value i...  2.1 us
  transfers between devices with their start and end apart: 13, of which 4 were waited for; matrix products, arithmetic and copies ran while one was open for 0% of the time, Pallas kernels for 26%

profile of v3, /device:TPU:0, one launch (start us, length us, event | category | flops | bytes accessed | tf_op | source)
XLA Modules:
  0.0 65.0 jit_solution(17349580555246072398)
XLA Ops:
  0.6 1.0 %slice_bitcast_fusion = bf16[2,12288]{1,0:T(2,128)(2,1)S(1)} fusion(bf16[1,128,12288]{2,1,0:T(8,128)(2,1)} %param.5), kind=kLoop, calls=%fused_computation.11 | loop fusion | bytes 98304 | tf_op jit(solution)/shard_map/squeeze | solution.py:507
  1.6 2.4 %collective-permute-start = (bf16[2,12288]{1,0:T(2,128)(2,1)S(1)}, bf16[2,12288]{1,0:T(2,128)(2,1)S(1)}, u32[]{:S(2)}, u32[]{:S(2)}) collective-permute-start(bf16[2,12288]{1,0:T(2,128)(2,1)S(1)} %slice_bitcast_fusion), channel_id=1, source_target_pairs={{0,1},{1,2},{2,3},{3,4},{4,5},{5,6},{6,7},{8,9},{9,10},{10,11},{11... | collective-permute-start | bytes 147464 | tf_op jit(solution)/shard_map/ppermute | solution.py:24
  4.0 0.9 %prepare.1 = (bf16[4,128,128]{2,1,0:T(8,128)(2,1)S(1)}, bf16[256,144]{1,0:T(8,128)(2,1)S(1)}, bf16[256,128]{1,0:T(8,128)(2,1)S(1)}, f32[2,8,128]{2,1,0:T(8,128)S(1)}) custom-call(s32[1,1024]{1,0:T(1,128)} %ids_ref.1), custom_call_target="tpu_custom_call" | custom-call | flops 1000000 | bytes 1000000 | tf_op jit(solution)/shard_map/prepare/pallas_call | solution.py:109
  4.9 0.0 collective-permute-done.edge_ref
  4.9 2.7 %gates.3 = (bf16[3,128,2048]{2,1,0:T(8,128)(2,1)S(1)}, bf16[128,2048]{1,0:T(8,128)(2,1)S(1)}, bf16[128,2048]{1,0:T(8,128)(2,1)S(1)}) custom-call(bf16[128,12288]{1,0:T(8,128)(2,1)} %bitcast.29, bf16[128,12288]{1,0:T(8,128)(2,1)} %bitcast.30, bf16[128,12288]{1,0:T(8,128)(2,1)} %bitcast.31, bf16[2,12288]{1,0:T(2,128)(2,1)S(1)} %collective-permute-done.edge_ref, ...), custom_call_target="tpu_custom_call" | custom-call | flops 805306368 | bytes 4718592 | tf_op jit(solution)/shard_map/gates/pallas_call | solution.py:162
  7.6 3.0 %collective-permute-start.3 = (bf16[128,2048]{1,0:T(8,128)(2,1)S(1)}, bf16[128,2048]{1,0:T(8,128)(2,1)}, u32[]{:S(2)}, u32[]{:S(2)}) collective-permute-start(bf16[128,2048]{1,0:T(8,128)(2,1)S(1)} %get-tuple-element.34), channel_id=1, source_target_pairs={{0,1},{1,0},{2,3},{3,2},{4,5},{5,4},{6,7},{7,6},{8,9},{9,8},{10,11... | collective-permute-start | bytes 1572872 | tf_op jit(solution)/shard_map/ppermute | solution.py:29
  10.6 1.5 %collective-permute-start.4 = (bf16[128,2048]{1,0:T(8,128)(2,1)S(1)}, bf16[128,2048]{1,0:T(8,128)(2,1)}, u32[]{:S(2)}, u32[]{:S(2)}) collective-permute-start(bf16[128,2048]{1,0:T(8,128)(2,1)S(1)} %get-tuple-element.35), channel_id=1, source_target_pairs={{1,2},{3,4},{5,6},{2,1},{4,3},{6,5},{9,10},{11,12},{13,14},{10,9},... | collective-permute-start | bytes 1572872 | tf_op jit(solution)/shard_map/ppermute | solution.py:35
  12.1 2.7 %gates.2 = (bf16[3,128,2048]{2,1,0:T(8,128)(2,1)S(1)}, bf16[128,2048]{1,0:T(8,128)(2,1)S(1)}, bf16[128,2048]{1,0:T(8,128)(2,1)S(1)}) custom-call(bf16[128,12288]{1,0:T(8,128)(2,1)} %bitcast.32, bf16[128,12288]{1,0:T(8,128)(2,1)} %bitcast.33, bf16[128,12288]{1,0:T(8,128)(2,1)} %bitcast.34, bf16[2,12288]{1,0:T(2,128)(2,1)S(1)} %collective-permute-done.edge_ref, ...), custom_call_target="tpu_custom_call" | custom-call | flops 805306368 | bytes 4718592 | tf_op jit(solution)/shard_map/gates/pallas_call | solution.py:162
  14.8 2.9 %collective-permute-start.1 = (bf16[128,2048]{1,0:T(8,128)(2,1)S(1)}, bf16[128,2048]{1,0:T(8,128)(2,1)S(1)}, u32[]{:S(2)}, u32[]{:S(2)}) collective-permute-start(bf16[128,2048]{1,0:T(8,128)(2,1)S(1)} %get-tuple-element.29), channel_id=1, source_target_pairs={{0,1},{1,0},{2,3},{3,2},{4,5},{5,4},{6,7},{7,6},{8,9},{9,8},{10,11... | collective-permute-start | bytes 1572872 | tf_op jit(solution)/shard_map/ppermute | solution.py:29
  17.7 0.9 %collective-permute-start.2 = (bf16[128,2048]{1,0:T(8,128)(2,1)S(1)}, bf16[128,2048]{1,0:T(8,128)(2,1)S(1)}, u32[]{:S(2)}, u32[]{:S(2)}) collective-permute-start(bf16[128,2048]{1,0:T(8,128)(2,1)S(1)} %get-tuple-element.30), channel_id=1, source_target_pairs={{1,2},{3,4},{5,6},{2,1},{4,3},{6,5},{9,10},{11,12},{13,14},{10,9},... | collective-permute-start | bytes 1572872 | tf_op jit(solution)/shard_map/ppermute | solution.py:35
  18.6 0.0 collective-permute-done.3.chip_in_ref
  18.6 0.0 collective-permute-done.4.link_in_ref
  18.6 11.5 %long_parts.2 = (bf16[128,4096]{1,0:T(8,128)(2,1)}, f32[3,8,8,128]{3,2,1,0:T(8,128)S(1)}, f32[3,8,4096]{2,1,0:T(8,128)S(1)}, f32[256,128]{1,0:T(8,128)S(1)}, f32...) custom-call(bf16[128,2048]{1,0:T(8,128)(2,1)} %collective-permute-done.3.chip_in_ref, ...), custom_call_target="tpu_custom_call" | custom-call | flops 6442450944 | bytes 12582912 | tf_op jit(solution)/shard_map/long_parts/pallas_call | solution.py:346
  30.1 0.0 collective-permute-done.1.chip_in_ref
  30.1 0.0 collective-permute-done.2.link_in_ref
  30.1 11.4 %long_parts.3 = (bf16[128,4096]{1,0:T(8,128)(2,1)}, f32[3,8,8,128]{3,2,1,0:T(8,128)S(1)}, f32[3,8,4096]{2,1,0:T(8,128)S(1)}, f32[256,128]{1,0:T(8,128)S(1)}, f32...) custom-call(bf16[128,2048]{1,0:T(8,128)(2,1)S(1)} %collective-permut, ...), custom_call_target="tpu_custom_call", output_to_operand_aliasing={{0}: (13, {}), {1}: (14, {}), {2}: (15, {}), {3}: (16, {}),... | custom-call | flops 6442450944 | bytes 12582912 | tf_op jit(solution)/shard_map/long_parts/pallas_call | solution.py:346
  41.6 3.3 %collective-permute-start.5 = (f32[464,128]{1,0:T(8,128)S(1)}, f32[464,128]{1,0:T(8,128)S(1)}, u32[]{:S(2)}, u32[]{:S(2)}) collective-permute-start(f32[464,128]{1,0:T(8,128)S(1)} %pad_maximum_fusion), channel_id=1, source_target_pairs={{0,1},{1,0},{2,3},{3,2},{4,5},{5,4},{6,7},{7,6},{8,9},{9,8},{10,11... | collective-permute-start | bytes 712712 | tf_op jit(solution)/shard_map/ppermute | solution.py:29
  44.9 1.1 %collective-permute-done.5 = f32[464,128]{1,0:T(8,128)S(1)} collective-permute-done((f32[464,128]{1,0:T(8,128)S(1)}, f32[464,128]{1,0:T(8,128)S(1)}, u32[]{:S(2)}, u32[]{:S(2)}) %collective-permute-start.5) | collective-permute-done | bytes 237600 | tf_op jit(solution)/shard_map/ppermute | solution.py:29
  46.1 2.2 %collective-permute-start.7 = (bf16[68,128]{1,0:T(8,128)(2,1)S(1)}, bf16[68,128]{1,0:T(8,128)(2,1)S(1)}, u32[]{:S(2)}, u32[]{:S(2)}) collective-permute-start(bf16[68,128]{1,0:T(8,128)(2,1)S(1)} %get-tuple-element.54), channel_id=1, source_target_pairs={{0,2},{1,3},{2,0},{3,1},{4,6},{5,7},{6,4},{7,5},{8,10},{9,11},{10,... | collective-permute-start | bytes 52232 | tf_op jit(solution)/shard_map/ppermute | solution.py:29
  48.3 2.5 %collective-permute-start.8 = (bf16[68,128]{1,0:T(8,128)(2,1)S(1)}, bf16[68,128]{1,0:T(8,128)(2,1)S(1)}, u32[]{:S(2)}, u32[]{:S(2)}) collective-permute-start(bf16[68,128]{1,0:T(8,128)(2,1)S(1)} %get-tuple-element.56), channel_id=1, source_target_pairs={{0,4},{1,5},{2,6},{3,7},{4,0},{5,1},{6,2},{7,3},{8,12},{9,13},{10,... | collective-permute-start | bytes 52232 | tf_op jit(solution)/shard_map/ppermute | solution.py:29
  50.7 0.0 collective-permute-start.9
  50.7 0.7 %collective-permute-start.6 = (bf16[192,128]{1,0:T(8,128)(2,1)S(1)}, bf16[192,128]{1,0:T(8,128)(2,1)S(1)}, u32[]{:S(2)}, u32[]{:S(2)}) collective-permute-start(bf16[192,128]{1,0:T(8,128)(2,1)S(1)} %bitcast_convert_fusion), channel_id=1, source_target_pairs={{2,1},{4,3},{6,5},{10,9},{12,11},{14,13},{18,17},{20,19},{22,21},{... | collective-permute-start | bytes 147464 | tf_op jit(solution)/shard_map/ppermute | solution.py:422
  51.4 0.0 collective-permute-done.7
  51.4 1.5 %collective-permute-done.8 = bf16[68,128]{1,0:T(8,128)(2,1)S(1)} collective-permute-done((bf16[68,128]{1,0:T(8,128)(2,1)S(1)}, bf16[68,128]{1,0:T(8,128)(2,1)S(1)}, u32[]{:S(2)}, u32[]{:S(2)}) %collective-permute-start.8) | collective-permute-done | bytes 17440 | tf_op jit(solution)/shard_map/ppermute | solution.py:29
  52.9 3.5 %collective-permute-done.9 = bf16[68,128]{1,0:T(8,128)(2,1)S(1)} collective-permute-done((bf16[68,128]{1,0:T(8,128)(2,1)S(1)}, bf16[68,128]{1,0:T(8,128)(2,1)S(1)}, u32[]{:S(2)}, u32[]{:S(2)}) %collective-permute-start.9) | collective-permute-done | bytes 17440 | tf_op jit(solution)/shard_map/ppermute | solution.py:29
  56.4 1.6 %collective-permute-start.10 = (f32[68,128]{1,0:T(8,128)S(1)}, f32[68,128]{1,0:T(8,128)S(1)}, u32[]{:S(2)}, u32[]{:S(2)}) collective-permute-start(f32[68,128]{1,0:T(8,128)S(1)} %fusion.5.refs_0_), channel_id=1, source_target_pairs={{0,8},{8,0},{16,24},{24,16},{1,9},{9,1},{17,25},{25,17},{2,10},{10... | collective-permute-start | bytes 104456 | tf_op jit(solution)/shard_map/ppermute | solution.py:29
  58.0 1.5 %collective-permute-start.11 = (f32[68,128]{1,0:T(8,128)S(1)}, f32[68,128]{1,0:T(8,128)S(1)}, u32[]{:S(2)}, u32[]{:S(2)}) collective-permute-start(f32[68,128]{1,0:T(8,128)S(1)} %fusion.5.refs_0_), channel_id=1, source_target_pairs={{0,16},{8,24},{16,0},{24,8},{1,17},{9,25},{17,1},{25,9},{2,18},{10... | collective-permute-start | bytes 104456 | tf_op jit(solution)/shard_map/ppermute | solution.py:29
  59.5 0.5 collective-permute-start.12
  60.0 0.0 collective-permute-done.6
  60.0 2.1 %last_rows.1 = bf16[128,12288]{1,0:T(8,128)(2,1)} custom-call(f32[3,8,4096]{2,1,0:T(8,128)S(1)} %get-tuple-element.44.tail_ref, f32[24,8,128]{2,1,0:T(8,128)S(1)} %fusion.4.ahead_ref, f32[3,12288]{1,0:T(4,128)} %w_ref.9, f32[2,8,128]{2,1,0:T(8,128)S(1)} %get-tuple-element.48.late_ref, ...), custom_call_target="tpu_custom_call", output_to_operand_aliasing={{}: (4, {})} | custom-call | flops 1000000 | bytes 2000000 | tf_op jit(solution)/shard_map/last_rows/pallas_call | solution.py:401
  62.1 0.0 collective-permute-done.10.refs_1_
  62.1 0.0 collective-permute-done.11.refs_2_
  62.1 2.3 %collective-permute-done.12.refs_3_ = f32[68,128]{1,0:T(8,128)S(1)} collective-permute-done((f32[68,128]{1,0:T(8,128)S(1)}, f32[68,128]{1,0:T(8,128)S(1)}, u32[]{:S(2)}, u32[]{:S(2)}) %collective-permute-start.12) | collective-permute-done | bytes 34848 | tf_op jit(solution)/shard_map/ppermute | solution.py:29
  64.3 0.6 finish.1
  (11 shorter events, 0.2 us)
Async XLA Ops:
  1.6 3.2 %collective-permute-start = (bf16[2,12288]{1,0:T(2,128)(2,1)S(1)}, bf16[2,12288]{1,0:T(2,128)(2,1)S(1)}, u32[]{:S(2)}, u32[]{:S(2)}) collective-permute-start(bf16[2,12288]{1,0:T(2,128)(2,1)S(1)} %slice_bitcast_fusion), channel_id=1, source_target_pairs={{0,1},{1,2},{2,3},{3,4},{4,5},{5,6},{6,7},{8,9},{9,10},{10,11},{11... | collective-permute-start | bytes 147464 | tf_op jit(solution)/shard_map/ppermute | solution.py:24
  7.6 11.0 %collective-permute-start.3 = (bf16[128,2048]{1,0:T(8,128)(2,1)S(1)}, bf16[128,2048]{1,0:T(8,128)(2,1)}, u32[]{:S(2)}, u32[]{:S(2)}) collective-permute-start(bf16[128,2048]{1,0:T(8,128)(2,1)S(1)} %get-tuple-element.34), channel_id=1, source_target_pairs={{0,1},{1,0},{2,3},{3,2},{4,5},{5,4},{6,7},{7,6},{8,9},{9,8},{10,11... | collective-permute-start | bytes 1572872 | tf_op jit(solution)/shard_map/ppermute | solution.py:29
  10.6 8.0 %collective-permute-start.4 = (bf16[128,2048]{1,0:T(8,128)(2,1)S(1)}, bf16[128,2048]{1,0:T(8,128)(2,1)}, u32[]{:S(2)}, u32[]{:S(2)}) collective-permute-start(bf16[128,2048]{1,0:T(8,128)(2,1)S(1)} %get-tuple-element.35), channel_id=1, source_target_pairs={{1,2},{3,4},{5,6},{2,1},{4,3},{6,5},{9,10},{11,12},{13,14},{10,9},... | collective-permute-start | bytes 1572872 | tf_op jit(solution)/shard_map/ppermute | solution.py:35
  14.8 15.3 %collective-permute-start.1 = (bf16[128,2048]{1,0:T(8,128)(2,1)S(1)}, bf16[128,2048]{1,0:T(8,128)(2,1)S(1)}, u32[]{:S(2)}, u32[]{:S(2)}) collective-permute-start(bf16[128,2048]{1,0:T(8,128)(2,1)S(1)} %get-tuple-element.29), channel_id=1, source_target_pairs={{0,1},{1,0},{2,3},{3,2},{4,5},{5,4},{6,7},{7,6},{8,9},{9,8},{10,11... | collective-permute-start | bytes 1572872 | tf_op jit(solution)/shard_map/ppermute | solution.py:29
  17.7 12.4 %collective-permute-start.2 = (bf16[128,2048]{1,0:T(8,128)(2,1)S(1)}, bf16[128,2048]{1,0:T(8,128)(2,1)S(1)}, u32[]{:S(2)}, u32[]{:S(2)}) collective-permute-start(bf16[128,2048]{1,0:T(8,128)(2,1)S(1)} %get-tuple-element.30), channel_id=1, source_target_pairs={{1,2},{3,4},{5,6},{2,1},{4,3},{6,5},{9,10},{11,12},{13,14},{10,9},... | collective-permute-start | bytes 1572872 | tf_op jit(solution)/shard_map/ppermute | solution.py:35
  41.6 4.4 %collective-permute-start.5 = (f32[464,128]{1,0:T(8,128)S(1)}, f32[464,128]{1,0:T(8,128)S(1)}, u32[]{:S(2)}, u32[]{:S(2)}) collective-permute-start(f32[464,128]{1,0:T(8,128)S(1)} %pad_maximum_fusion), channel_id=1, source_target_pairs={{0,1},{1,0},{2,3},{3,2},{4,5},{5,4},{6,7},{7,6},{8,9},{9,8},{10,11... | collective-permute-start | bytes 712712 | tf_op jit(solution)/shard_map/ppermute | solution.py:29
  46.1 5.3 %collective-permute-start.7 = (bf16[68,128]{1,0:T(8,128)(2,1)S(1)}, bf16[68,128]{1,0:T(8,128)(2,1)S(1)}, u32[]{:S(2)}, u32[]{:S(2)}) collective-permute-start(bf16[68,128]{1,0:T(8,128)(2,1)S(1)} %get-tuple-element.54), channel_id=1, source_target_pairs={{0,2},{1,3},{2,0},{3,1},{4,6},{5,7},{6,4},{7,5},{8,10},{9,11},{10,... | collective-permute-start | bytes 52232 | tf_op jit(solution)/shard_map/ppermute | solution.py:29
  48.3 4.7 %collective-permute-start.8 = (bf16[68,128]{1,0:T(8,128)(2,1)S(1)}, bf16[68,128]{1,0:T(8,128)(2,1)S(1)}, u32[]{:S(2)}, u32[]{:S(2)}) collective-permute-start(bf16[68,128]{1,0:T(8,128)(2,1)S(1)} %get-tuple-element.56), channel_id=1, source_target_pairs={{0,4},{1,5},{2,6},{3,7},{4,0},{5,1},{6,2},{7,3},{8,12},{9,13},{10,... | collective-permute-start | bytes 52232 | tf_op jit(solution)/shard_map/ppermute | solution.py:29
  50.7 5.7 %collective-permute-start.9 = (bf16[68,128]{1,0:T(8,128)(2,1)S(1)}, bf16[68,128]{1,0:T(8,128)(2,1)S(1)}, u32[]{:S(2)}, u32[]{:S(2)}) collective-permute-start(bf16[68,128]{1,0:T(8,128)(2,1)S(1)} %get-tuple-element.55), channel_id=1, source_target_pairs={{0,6},{1,7},{2,4},{3,5},{4,2},{5,3},{6,0},{7,1},{8,14},{9,15},{10,... | collective-permute-start | bytes 52232 | tf_op jit(solution)/shard_map/ppermute | solution.py:29
  50.7 9.2 %collective-permute-start.6 = (bf16[192,128]{1,0:T(8,128)(2,1)S(1)}, bf16[192,128]{1,0:T(8,128)(2,1)S(1)}, u32[]{:S(2)}, u32[]{:S(2)}) collective-permute-start(bf16[192,128]{1,0:T(8,128)(2,1)S(1)} %bitcast_convert_fusion), channel_id=1, source_target_pairs={{2,1},{4,3},{6,5},{10,9},{12,11},{14,13},{18,17},{20,19},{22,21},{... | collective-permute-start | bytes 147464 | tf_op jit(solution)/shard_map/ppermute | solution.py:422
  56.4 5.7 %collective-permute-start.10 = (f32[68,128]{1,0:T(8,128)S(1)}, f32[68,128]{1,0:T(8,128)S(1)}, u32[]{:S(2)}, u32[]{:S(2)}) collective-permute-start(f32[68,128]{1,0:T(8,128)S(1)} %fusion.5.refs_0_), channel_id=1, source_target_pairs={{0,8},{8,0},{16,24},{24,16},{1,9},{9,1},{17,25},{25,17},{2,10},{10... | collective-permute-start | bytes 104456 | tf_op jit(solution)/shard_map/ppermute | solution.py:29
  58.0 4.1 %collective-permute-start.11 = (f32[68,128]{1,0:T(8,128)S(1)}, f32[68,128]{1,0:T(8,128)S(1)}, u32[]{:S(2)}, u32[]{:S(2)}) collective-permute-start(f32[68,128]{1,0:T(8,128)S(1)} %fusion.5.refs_0_), channel_id=1, source_target_pairs={{0,16},{8,24},{16,0},{24,8},{1,17},{9,25},{17,1},{25,9},{2,18},{10... | collective-permute-start | bytes 104456 | tf_op jit(solution)/shard_map/ppermute | solution.py:29
  59.5 4.9 %collective-permute-start.12 = (f32[68,128]{1,0:T(8,128)S(1)}, f32[68,128]{1,0:T(8,128)S(1)}, u32[]{:S(2)}, u32[]{:S(2)}) collective-permute-start(f32[68,128]{1,0:T(8,128)S(1)} %fusion.5.refs_0_), channel_id=1, source_target_pairs={{0,24},{8,16},{16,8},{24,0},{1,25},{9,17},{17,9},{25,1},{2,26},{10... | collective-permute-start | bytes 104456 | tf_op jit(solution)/shard_map/ppermute | solution.py:29

commit v4 on v3

--- a/solution.py
+++ b/solution.py
@@ -61,8 +61,20 @@
 
 
 def prepare_kernel(
-    ids_ref, long_ref, back_ref, ahead_ref, late_ref
+    ids_ref, far_x, far_cot, long_ref, back_ref, ahead_ref, late_ref, near_x, near_cot, sems
 ):
+    held = near_cot.shape[1]
+    copies = [
+        pltpu.make_async_copy(
+            far_x.at[:, b * far_cot.shape[1] : b * far_cot.shape[1] + held],
+            near_x.at[:, b * held : (b + 1) * held],
+            sems.at[b],
+        )
+        for b in range(3)
+    ]
+    copies.append(pltpu.make_async_copy(far_cot.at[:, :held], near_cot, sems.at[3]))
+    for copy in copies:
+        copy.start()
     taps = long_ref.shape[1]
     here = lax.axis_index("ctx")
     last = ids_ref.shape[1] // taps - 1
@@ -97,9 +109,13 @@
         ahead_ref[at, :] = put((cols == rows + j) & same)
         late = jnp.where((cols == rows + j - taps) & first_next, 1.0, 0.0)
         late_ref[j - 1] = late[taps - 8 :]
-
-
-def prepare(doc_ids, taps):
+    for copy in copies:
+        copy.wait()
+
+
+def prepare(doc_ids, taps, inputs, cotangent, held):
+    rows = inputs.shape[0]
+    anywhere = pl.BlockSpec(memory_space=pl.ANY)
     shapes = [
         ((4, taps, taps), BF),
         ((2 * taps, taps + EDGE), BF),
@@ -110,11 +126,13 @@
         prepare_kernel,
         "prepare",
         (),
-        [whole(doc_ids.shape)],
-        [whole(shape) for shape, _ in shapes],
-        [jax.ShapeDtypeStruct(*entry) for entry in shapes],
-        (1000000, 1000000),
-    )(in_hbm(doc_ids))
+        [whole(doc_ids.shape), anywhere, anywhere],
+        [whole(shape) for shape, _ in shapes] + [anywhere, anywhere],
+        [jax.ShapeDtypeStruct(*entry) for entry in shapes]
+        + [pltpu.VMEM((rows, 3 * held), BF), pltpu.VMEM((rows, held), BF)],
+        (1000000, 4000000),
+        [pltpu.SemaphoreType.DMA((4,))],
+    )(in_hbm(doc_ids), in_hbm(inputs), in_hbm(cotangent))
 
 
 def short_sum(weights, values, one, two):
@@ -153,21 +171,24 @@
 
 
 def make_gates(inputs, border, weights, cotangent, back_mask, part, parts):
-    rows, model_width = cotangent.shape
+    rows = cotangent.shape[0]
+    model_width = weights.shape[1] // 3
     width = GATE_WIDTH
     steps = model_width // width
     held = steps // parts
     first = part * held
+    held_steps = cotangent.shape[1] // width
+    held_first = first if held_steps == steps else 0
     plain = pl.BlockSpec((rows, width), lambda i: (0, i))
     return call(
         functools.partial(gate_kernel, first=first, steps=steps),
         "gates",
         (held,),
-        branch_specs(rows, width, first, steps)
+        branch_specs(rows, width, held_first, held_steps)
         + [
             whole(border.shape),
             whole(weights.shape),
-            pl.BlockSpec((rows, width), lambda i: (0, first + i)),
+            pl.BlockSpec((rows, width), lambda i: (0, held_first + i)),
             whole(back_mask.shape),
         ],
         [pl.BlockSpec((3, rows, width), lambda i: (0, 0, i)), plain, plain],
@@ -204,24 +225,27 @@
 
     def leaving(step, b):
         at = lax.rem(step, 2)
-        return pltpu.make_async_copy(
-            staged.at[at, b], inputs_ref.at[:, column(step, b)], sems.at[at, b]
-        )
+        target = out_ref.at[:, column(step, 0)] if b == 3 else inputs_ref.at[:, column(step, b)]
+        return pltpu.make_async_copy(staged.at[at, b], target, sems.at[at, b])
 
     @pl.when(i >= 2)
     def _():
-        for b in range(3):
+        for b in range(4):
             leaving(i - 2, b).wait()
 
-    mixed_grads = [[], [], []]
-    for u in range(subs):
-        ls = slice(u * LANES, (u + 1) * LANES)
-        gs = slice(u * per, (u + 1) * per)
+    def both_sides(ls):
         here = mixed_ref[1, :, ls] * mixed_ref[2, :, ls]
         grad = cot_ref[:, ls] * mixed_ref[0, :, ls]
         chip_in, link_in = chip_in_ref[:, ls], link_in_ref[:, ls]
         sources = jnp.concatenate([here, jnp.where(first_core, link_in, chip_in)], axis=0)
         grads = jnp.concatenate([grad, jnp.where(first_core, chip_in, link_in)], axis=0)
+        return sources, grads
+
+    mixed_grads = [[], [], []]
+    for u in range(subs):
+        ls = slice(u * LANES, (u + 1) * LANES)
+        gs = slice(u * per, (u + 1) * per)
+        sources, grads = both_sides(ls)
         filters = filter_ref[gs].astype(F32)
         turned = [
             pltpu.roll(
@@ -246,30 +270,12 @@
 
         long_mix = long_conv(1, sources, 0)
         grad_product = long_conv(2, grads, 1)
-        out_ref[:, ls] = mixed_ref[0, :, ls] * long_mix
+        staged[slot, 3, :, ls] = mixed_ref[0, :, ls] * long_mix
         mixed_grads[0].append(cot_ref[:, ls] * long_mix)
         mixed_grads[1].append(grad_product * mixed_ref[2, :, ls])
         mixed_grads[2].append(grad_product * mixed_ref[1, :, ls])
 
-        spread = jnp.concatenate([here * lane[g] for g in range(per)], axis=0)
-        inner = lax.dot_general(
-            spread, grads, (((1,), (1,)), ((), ())), preferred_element_type=F32
-        ).reshape(per, taps // 8, 8, 2 * taps)
-        keep = long_ref[3].astype(F32)
-        total = None
-        for k in range(taps // 8):
-            nearer = (cols >= rows + 8 * k)[None]
-            term = jnp.where(nearer, inner[:, k, :, :taps], inner[:, k, :, taps:])
-            term = (term * keep[8 * k : 8 * k + 8][None]).reshape(per * 8, taps)
-            if k:
-                term = pltpu.roll(term, taps - 8 * k, 1)
-            total = term if total is None else total + term
-        diag[u] = total.reshape(per, 8, taps)
-        lined = diag[u, :, 0, :]
-        for r in range(1, 8):
-            lined = lined + pltpu.roll(diag[u, :, r, :], taps - r, 1)
-        gl_ref[gs, :] = lined
-
+    leaving(i, 3).start()
     edge_keep = back_ref[:, taps : taps + 2].astype(F32)
     for b, x_ref in enumerate((xq, xk, xv)):
         mixed_grad = jnp.concatenate(mixed_grads[b], axis=1)
@@ -305,9 +311,33 @@
                     :, u * LANES : (u + 1) * LANES
                 ]
 
+    for u in range(subs):
+        ls = slice(u * LANES, (u + 1) * LANES)
+        gs = slice(u * per, (u + 1) * per)
+        sources, grads = both_sides(ls)
+        here = sources[:rows_here]
+        spread = jnp.concatenate([here * lane[g] for g in range(per)], axis=0)
+        inner = lax.dot_general(
+            spread, grads, (((1,), (1,)), ((), ())), preferred_element_type=F32
+        ).reshape(per, taps // 8, 8, 2 * taps)
+        keep = long_ref[3].astype(F32)
+        total = None
+        for k in range(taps // 8):
+            nearer = (cols >= rows + 8 * k)[None]
+            term = jnp.where(nearer, inner[:, k, :, :taps], inner[:, k, :, taps:])
+            term = (term * keep[8 * k : 8 * k + 8][None]).reshape(per * 8, taps)
+            if k:
+                term = pltpu.roll(term, taps - 8 * k, 1)
+            total = term if total is None else total + term
+        diag[u] = total.reshape(per, 8, taps)
+        lined = diag[u, :, 0, :]
+        for r in range(1, 8):
+            lined = lined + pltpu.roll(diag[u, :, r, :], taps - r, 1)
+        gl_ref[gs, :] = lined
+
     @pl.when(i == held - 1)
     def _():
-        for b in range(3):
+        for b in range(4):
             if held > 1:
                 leaving(i - 1, b).wait()
             leaving(i, b).wait()
@@ -349,7 +379,7 @@
         (held,),
         in_specs,
         [
-            placed,
+            anywhere,
             pl.BlockSpec((3, subs // PIECE, 2 * PIECE, LANES), lambda i: (0, first + i, 0, 0)),
             pl.BlockSpec((3, 8, width), lambda i: (0, 0, first + i)),
             pl.BlockSpec((step_groups, taps), lambda i: (first + i, 0)),
@@ -367,8 +397,8 @@
         (3 * groups * 2 * 128 * 256 * 256 // parts, 24 * 1024 * 1024 // parts),
         [
             pltpu.VMEM((subs, step_groups // subs, 8, taps), F32),
-            pltpu.VMEM((2, 3, rows, width), BF),
-            pltpu.SemaphoreType.DMA((2, 3)),
+            pltpu.VMEM((2, 4, rows, width), BF),
+            pltpu.SemaphoreType.DMA((2, 4)),
         ],
         aliases,
         32,
@@ -506,14 +536,17 @@
     edge = short_taps - 1
     border = passed_along(projected[0, rows - edge :], "ctx", 1)
     filters = in_hbm(long_filter)
-    masks = prepare(doc_ids, long_filter.shape[1])
+    *masks, early_x, early_cot = prepare(
+        doc_ids, long_filter.shape[1], projected[0], grad_row, model_width // PARTS
+    )
     inputs_row, grad_row, short_filter = [
         in_hbm(value) for value in (projected[0], grad_row, short_filter)
     ]
     gated = []
     for part in range(PARTS):
         mixed, chip, link = make_gates(
-            inputs_row, border, short_filter, grad_row, masks[1], part, PARTS
+            inputs_row if part else early_x, border, short_filter,
+            grad_row if part else early_cot, masks[1], part, PARTS,
         )
         link_in = linked(link, "ctx")
         chip_in = swapped(chip, "ctx", 1)

time: 65.3 us -> 63.5 us (0.972)
  starting transfers between devices: 22.7 us -> 21.7 us
    pallas_call x1, Pallas kernels: 0.86 us -> 2.26 us  [prepare(): call(prepare_kernel, 'prepare', (), [whole(doc_ids.shape), anywhere, anyw...]
    pallas_call x2, Pallas kernels: 22.9 us -> 21.7 us  [make_long(): call(functools.partial(long_kernel, first=first, steps=steps, held=held),...]
    ppermute x9, starting transfers between devices: 17.4 us -> 16.4 us  [swapped(): lax.ppermute(value, axis, [(source, source ^ bits) for source in range(co...]
    pallas_call x2, Pallas kernels: 5.44 us -> 4.77 us  [make_gates(): call(functools.partial(gate_kernel, first=first, steps=steps), 'gates', (...]
  transfers between devices with their start and end apart: 13 -> 13, of which waited for: 4 -> 4; matrix products, arithmetic and copies ran while one was open for 0% -> 0% of each run, Pallas kernels for 26% -> 28%
where the time goes in v4:
time: 63.5 us; the launch traced here: 63.1 us
  Pallas kernels  31.4 us (49%)
  starting transfers between devices  21.7 us (34%)
  waiting for transfers between devices  8.06 us (13%)
  local copies, waits for them, and re-layouts  1.05 us (2%)
  between operations  0.82 us (1%)
    pallas_call x2, Pallas kernels, make_long(): call(functools.partial(long_kernel, first=first, steps=steps, held=held),...  21.7 us
    ppermute x9, starting transfers between devices, swapped(): lax.ppermute(value, axis, [(source, source ^ bits) for source in range(co...  16.4 us
    ppermute x9, waiting for transfers between devices, swapped(): lax.ppermute(value, axis, [(source, source ^ bits) for source in range(co...  8.05 us
    pallas_call x2, Pallas kernels, make_gates(): call(functools.partial(gate_kernel, first=first, steps=steps), 'gates', (...  4.77 us
    ppermute x1, starting transfers between devices, passed_along(): lax.ppermute(value, axis, [(source, source + steps) for source in range(i...  2.36 us
    ppermute x2, starting transfers between devices, linked(): return lax.ppermute(value, axis, pairs + [(b, a) for a, b in pairs])  2.32 us
    pallas_call x1, Pallas kernels, prepare(): call(prepare_kernel, 'prepare', (), [whole(doc_ids.shape), anywhere, anyw...  2.26 us
    pallas_call x1, Pallas kernels, finish_last_rows(): call(last_rows_kernel, 'last_rows', (1,), [whole(value.shape) for value i...  2.1 us
  transfers between devices with their start and end apart: 13, of which 4 were waited for; matrix products, arithmetic and copies ran while one was open for 0% of the time, Pallas kernels for 28%

profile of v4, /device:TPU:0, one launch (start us, length us, event | category | flops | bytes accessed | tf_op | source)
XLA Modules:
  0.0 63.1 jit_solution(12776726016996702795)
XLA Ops:
  0.6 1.0 %slice_bitcast_fusion = bf16[2,12288]{1,0:T(2,128)(2,1)S(1)} fusion(bf16[1,128,12288]{2,1,0:T(8,128)(2,1)} %param.5), kind=kLoop, calls=%fused_computation.11 | loop fusion | bytes 98304 | tf_op jit(solution)/shard_map/squeeze | solution.py:537
  1.6 2.4 %collective-permute-start = (bf16[2,12288]{1,0:T(2,128)(2,1)S(1)}, bf16[2,12288]{1,0:T(2,128)(2,1)S(1)}, u32[]{:S(2)}, u32[]{:S(2)}) collective-permute-start(bf16[2,12288]{1,0:T(2,128)(2,1)S(1)} %slice_bitcast_fusion), channel_id=1, source_target_pairs={{0,1},{1,2},{2,3},{3,4},{4,5},{5,6},{6,7},{8,9},{9,10},{10,11},{11... | collective-permute-start | bytes 147464 | tf_op jit(solution)/shard_map/ppermute | solution.py:24
  4.0 2.3 %prepare.1 = (bf16[4,128,128]{2,1,0:T(8,128)(2,1)S(1)}, bf16[256,144]{1,0:T(8,128)(2,1)S(1)}, bf16[256,128]{1,0:T(8,128)(2,1)S(1)}, f32[2,8,128]{2,1,0:T(8,128)S...) custom-call(s32[1,1024]{1,0:T(1,128)} %ids_ref.1, bf16[128,12288]{1,0:T(8,128)(2,1)} %bitcast.29, ...), custom_call_target="tpu_custom_call" | custom-call | flops 1000000 | bytes 4000000 | tf_op jit(solution)/shard_map/prepare/pallas_call | solution.py:125
  6.2 0.0 collective-permute-done.edge_ref
  6.3 2.1 %gates.3 = (bf16[3,128,2048]{2,1,0:T(8,128)(2,1)S(1)}, bf16[128,2048]{1,0:T(8,128)(2,1)S(1)}, bf16[128,2048]{1,0:T(8,128)(2,1)S(1)}) custom-call(bf16[128,6144]{1,0:T(8,128)(2,1)S(1)} %get-tuple-element.36.xq.xk.xv, bf16[128,6144]{1,0:T(8,128)(2,1)S(1)} %get-tuple-element.36.xq.xk.xv, bf16[128,6144]{1,0:T(8,128)(2,1)S(1)} %get-tuple-element.36.xq.xk.xv, ...), custom_call_target="tpu_custom_call" | custom-call | flops 805306368 | bytes 4718592 | tf_op jit(solution)/shard_map/gates/pallas_call | solution.py:183
  8.3 2.8 %collective-permute-start.3 = (bf16[128,2048]{1,0:T(8,128)(2,1)S(1)}, bf16[128,2048]{1,0:T(8,128)(2,1)}, u32[]{:S(2)}, u32[]{:S(2)}) collective-permute-start(bf16[128,2048]{1,0:T(8,128)(2,1)S(1)} %get-tuple-element.38), channel_id=1, source_target_pairs={{0,1},{1,0},{2,3},{3,2},{4,5},{5,4},{6,7},{7,6},{8,9},{9,8},{10,11... | collective-permute-start | bytes 1572872 | tf_op jit(solution)/shard_map/ppermute | solution.py:29
  11.1 1.5 %collective-permute-start.4 = (bf16[128,2048]{1,0:T(8,128)(2,1)S(1)}, bf16[128,2048]{1,0:T(8,128)(2,1)}, u32[]{:S(2)}, u32[]{:S(2)}) collective-permute-start(bf16[128,2048]{1,0:T(8,128)(2,1)S(1)} %get-tuple-element.39), channel_id=1, source_target_pairs={{1,2},{3,4},{5,6},{2,1},{4,3},{6,5},{9,10},{11,12},{13,14},{10,9},... | collective-permute-start | bytes 1572872 | tf_op jit(solution)/shard_map/ppermute | solution.py:35
  12.5 2.7 %gates.2 = (bf16[3,128,2048]{2,1,0:T(8,128)(2,1)S(1)}, bf16[128,2048]{1,0:T(8,128)(2,1)S(1)}, bf16[128,2048]{1,0:T(8,128)(2,1)S(1)}) custom-call(bf16[128,12288]{1,0:T(8,128)(2,1)} %bitcast.30, bf16[128,12288]{1,0:T(8,128)(2,1)} %bitcast.31, bf16[128,12288]{1,0:T(8,128)(2,1)} %bitcast.32, bf16[2,12288]{1,0:T(2,128)(2,1)S(1)} %collective-permute-done.edge_ref, ...), custom_call_target="tpu_custom_call" | custom-call | flops 805306368 | bytes 4718592 | tf_op jit(solution)/shard_map/gates/pallas_call | solution.py:183
  15.3 2.2 %collective-permute-start.1 = (bf16[128,2048]{1,0:T(8,128)(2,1)S(1)}, bf16[128,2048]{1,0:T(8,128)(2,1)S(1)}, u32[]{:S(2)}, u32[]{:S(2)}) collective-permute-start(bf16[128,2048]{1,0:T(8,128)(2,1)S(1)} %get-tuple-element.31), channel_id=1, source_target_pairs={{0,1},{1,0},{2,3},{3,2},{4,5},{5,4},{6,7},{7,6},{8,9},{9,8},{10,11... | collective-permute-start | bytes 1572872 | tf_op jit(solution)/shard_map/ppermute | solution.py:29
  17.5 0.9 %collective-permute-start.2 = (bf16[128,2048]{1,0:T(8,128)(2,1)S(1)}, bf16[128,2048]{1,0:T(8,128)(2,1)S(1)}, u32[]{:S(2)}, u32[]{:S(2)}) collective-permute-start(bf16[128,2048]{1,0:T(8,128)(2,1)S(1)} %get-tuple-element.32), channel_id=1, source_target_pairs={{1,2},{3,4},{5,6},{2,1},{4,3},{6,5},{9,10},{11,12},{13,14},{10,9},... | collective-permute-start | bytes 1572872 | tf_op jit(solution)/shard_map/ppermute | solution.py:35
  18.4 0.0 collective-permute-done.3.chip_in_ref
  18.4 0.0 collective-permute-done.4.link_in_ref
  18.4 10.9 %long_parts.2 = (bf16[128,4096]{1,0:T(8,128)(2,1)}, f32[3,8,8,128]{3,2,1,0:T(8,128)S(1)}, f32[3,8,4096]{2,1,0:T(8,128)S(1)}, f32[256,128]{1,0:T(8,128)S(1)}, f32...) custom-call(bf16[128,2048]{1,0:T(8,128)(2,1)} %collective-permute-done.3.chip_in_ref, ...), custom_call_target="tpu_custom_call" | custom-call | flops 6442450944 | bytes 12582912 | tf_op jit(solution)/shard_map/long_parts/pallas_call | solution.py:376
  29.3 0.0 collective-permute-done.1.chip_in_ref
  29.3 0.0 collective-permute-done.2.link_in_ref
  29.3 10.8 %long_parts.3 = (bf16[128,4096]{1,0:T(8,128)(2,1)}, f32[3,8,8,128]{3,2,1,0:T(8,128)S(1)}, f32[3,8,4096]{2,1,0:T(8,128)S(1)}, f32[256,128]{1,0:T(8,128)S(1)}, f32...) custom-call(bf16[128,2048]{1,0:T(8,128)(2,1)S(1)} %collective-permut, ...), custom_call_target="tpu_custom_call", output_to_operand_aliasing={{0}: (13, {}), {1}: (14, {}), {2}: (15, {}), {3}: (16, {}),... | custom-call | flops 6442450944 | bytes 12582912 | tf_op jit(solution)/shard_map/long_parts/pallas_call | solution.py:376
  40.2 3.3 %collective-permute-start.5 = (f32[464,128]{1,0:T(8,128)S(1)}, f32[464,128]{1,0:T(8,128)S(1)}, u32[]{:S(2)}, u32[]{:S(2)}) collective-permute-start(f32[464,128]{1,0:T(8,128)S(1)} %pad_maximum_fusion), channel_id=1, source_target_pairs={{0,1},{1,0},{2,3},{3,2},{4,5},{5,4},{6,7},{7,6},{8,9},{9,8},{10,11... | collective-permute-start | bytes 712712 | tf_op jit(solution)/shard_map/ppermute | solution.py:29
  43.5 1.1 %collective-permute-done.5 = f32[464,128]{1,0:T(8,128)S(1)} collective-permute-done((f32[464,128]{1,0:T(8,128)S(1)}, f32[464,128]{1,0:T(8,128)S(1)}, u32[]{:S(2)}, u32[]{:S(2)}) %collective-permute-start.5) | collective-permute-done | bytes 237600 | tf_op jit(solution)/shard_map/ppermute | solution.py:29
  44.7 2.0 %collective-permute-start.7 = (bf16[68,128]{1,0:T(8,128)(2,1)S(1)}, bf16[68,128]{1,0:T(8,128)(2,1)S(1)}, u32[]{:S(2)}, u32[]{:S(2)}) collective-permute-start(bf16[68,128]{1,0:T(8,128)(2,1)S(1)} %get-tuple-element.58), channel_id=1, source_target_pairs={{0,2},{1,3},{2,0},{3,1},{4,6},{5,7},{6,4},{7,5},{8,10},{9,11},{10,... | collective-permute-start | bytes 52232 | tf_op jit(solution)/shard_map/ppermute | solution.py:29
  46.7 2.1 %collective-permute-start.8 = (bf16[68,128]{1,0:T(8,128)(2,1)S(1)}, bf16[68,128]{1,0:T(8,128)(2,1)S(1)}, u32[]{:S(2)}, u32[]{:S(2)}) collective-permute-start(bf16[68,128]{1,0:T(8,128)(2,1)S(1)} %get-tuple-element.60), channel_id=1, source_target_pairs={{0,4},{1,5},{2,6},{3,7},{4,0},{5,1},{6,2},{7,3},{8,12},{9,13},{10,... | collective-permute-start | bytes 52232 | tf_op jit(solution)/shard_map/ppermute | solution.py:29
  48.9 0.3 collective-permute-start.9
  49.2 0.7 %collective-permute-start.6 = (bf16[192,128]{1,0:T(8,128)(2,1)S(1)}, bf16[192,128]{1,0:T(8,128)(2,1)S(1)}, u32[]{:S(2)}, u32[]{:S(2)}) collective-permute-start(bf16[192,128]{1,0:T(8,128)(2,1)S(1)} %bitcast_convert_fusion), channel_id=1, source_target_pairs={{2,1},{4,3},{6,5},{10,9},{12,11},{14,13},{18,17},{20,19},{22,21},{... | collective-permute-start | bytes 147464 | tf_op jit(solution)/shard_map/ppermute | solution.py:452
  49.9 0.0 collective-permute-done.7
  49.9 1.5 %collective-permute-done.8 = bf16[68,128]{1,0:T(8,128)(2,1)S(1)} collective-permute-done((bf16[68,128]{1,0:T(8,128)(2,1)S(1)}, bf16[68,128]{1,0:T(8,128)(2,1)S(1)}, u32[]{:S(2)}, u32[]{:S(2)}) %collective-permute-start.8) | collective-permute-done | bytes 17440 | tf_op jit(solution)/shard_map/ppermute | solution.py:29
  51.4 3.1 %collective-permute-done.9 = bf16[68,128]{1,0:T(8,128)(2,1)S(1)} collective-permute-done((bf16[68,128]{1,0:T(8,128)(2,1)S(1)}, bf16[68,128]{1,0:T(8,128)(2,1)S(1)}, u32[]{:S(2)}, u32[]{:S(2)}) %collective-permute-start.9) | collective-permute-done | bytes 17440 | tf_op jit(solution)/shard_map/ppermute | solution.py:29
  54.6 1.6 %collective-permute-start.10 = (f32[68,128]{1,0:T(8,128)S(1)}, f32[68,128]{1,0:T(8,128)S(1)}, u32[]{:S(2)}, u32[]{:S(2)}) collective-permute-start(f32[68,128]{1,0:T(8,128)S(1)} %fusion.5.refs_0_), channel_id=1, source_target_pairs={{0,8},{8,0},{16,24},{24,16},{1,9},{9,1},{17,25},{25,17},{2,10},{10... | collective-permute-start | bytes 104456 | tf_op jit(solution)/shard_map/ppermute | solution.py:29
  56.1 1.5 %collective-permute-start.11 = (f32[68,128]{1,0:T(8,128)S(1)}, f32[68,128]{1,0:T(8,128)S(1)}, u32[]{:S(2)}, u32[]{:S(2)}) collective-permute-start(f32[68,128]{1,0:T(8,128)S(1)} %fusion.5.refs_0_), channel_id=1, source_target_pairs={{0,16},{8,24},{16,0},{24,8},{1,17},{9,25},{17,1},{25,9},{2,18},{10... | collective-permute-start | bytes 104456 | tf_op jit(solution)/shard_map/ppermute | solution.py:29
  57.6 0.5 collective-permute-start.12
  58.1 0.0 collective-permute-done.6
  58.1 2.1 %last_rows.1 = bf16[128,12288]{1,0:T(8,128)(2,1)} custom-call(f32[3,8,4096]{2,1,0:T(8,128)S(1)} %get-tuple-element.48.tail_ref, f32[24,8,128]{2,1,0:T(8,128)S(1)} %fusion.4.ahead_ref, f32[3,12288]{1,0:T(4,128)} %w_ref.9, f32[2,8,128]{2,1,0:T(8,128)S(1)} %get-tuple-element.52.late_ref, ...), custom_call_target="tpu_custom_call", output_to_operand_aliasing={{}: (4, {})} | custom-call | flops 1000000 | bytes 2000000 | tf_op jit(solution)/shard_map/last_rows/pallas_call | solution.py:431
  60.2 0.0 collective-permute-done.10.refs_1_
  60.2 0.0 collective-permute-done.11.refs_2_
  60.3 2.3 %collective-permute-done.12.refs_3_ = f32[68,128]{1,0:T(8,128)S(1)} collective-permute-done((f32[68,128]{1,0:T(8,128)S(1)}, f32[68,128]{1,0:T(8,128)S(1)}, u32[]{:S(2)}, u32[]{:S(2)}) %collective-permute-start.12) | collective-permute-done | bytes 34848 | tf_op jit(solution)/shard_map/ppermute | solution.py:29
  62.5 0.6 finish.1
  (11 shorter events, 0.2 us)
Async XLA Ops:
  1.6 4.6 %collective-permute-start = (bf16[2,12288]{1,0:T(2,128)(2,1)S(1)}, bf16[2,12288]{1,0:T(2,128)(2,1)S(1)}, u32[]{:S(2)}, u32[]{:S(2)}) collective-permute-start(bf16[2,12288]{1,0:T(2,128)(2,1)S(1)} %slice_bitcast_fusion), channel_id=1, source_target_pairs={{0,1},{1,2},{2,3},{3,4},{4,5},{5,6},{6,7},{8,9},{9,10},{10,11},{11... | collective-permute-start | bytes 147464 | tf_op jit(solution)/shard_map/ppermute | solution.py:24
  8.3 10.1 %collective-permute-start.3 = (bf16[128,2048]{1,0:T(8,128)(2,1)S(1)}, bf16[128,2048]{1,0:T(8,128)(2,1)}, u32[]{:S(2)}, u32[]{:S(2)}) collective-permute-start(bf16[128,2048]{1,0:T(8,128)(2,1)S(1)} %get-tuple-element.38), channel_id=1, source_target_pairs={{0,1},{1,0},{2,3},{3,2},{4,5},{5,4},{6,7},{7,6},{8,9},{9,8},{10,11... | collective-permute-start | bytes 1572872 | tf_op jit(solution)/shard_map/ppermute | solution.py:29
  11.1 7.3 %collective-permute-start.4 = (bf16[128,2048]{1,0:T(8,128)(2,1)S(1)}, bf16[128,2048]{1,0:T(8,128)(2,1)}, u32[]{:S(2)}, u32[]{:S(2)}) collective-permute-start(bf16[128,2048]{1,0:T(8,128)(2,1)S(1)} %get-tuple-element.39), channel_id=1, source_target_pairs={{1,2},{3,4},{5,6},{2,1},{4,3},{6,5},{9,10},{11,12},{13,14},{10,9},... | collective-permute-start | bytes 1572872 | tf_op jit(solution)/shard_map/ppermute | solution.py:35
  15.3 14.0 %collective-permute-start.1 = (bf16[128,2048]{1,0:T(8,128)(2,1)S(1)}, bf16[128,2048]{1,0:T(8,128)(2,1)S(1)}, u32[]{:S(2)}, u32[]{:S(2)}) collective-permute-start(bf16[128,2048]{1,0:T(8,128)(2,1)S(1)} %get-tuple-element.31), channel_id=1, source_target_pairs={{0,1},{1,0},{2,3},{3,2},{4,5},{5,4},{6,7},{7,6},{8,9},{9,8},{10,11... | collective-permute-start | bytes 1572872 | tf_op jit(solution)/shard_map/ppermute | solution.py:29
  17.5 11.8 %collective-permute-start.2 = (bf16[128,2048]{1,0:T(8,128)(2,1)S(1)}, bf16[128,2048]{1,0:T(8,128)(2,1)S(1)}, u32[]{:S(2)}, u32[]{:S(2)}) collective-permute-start(bf16[128,2048]{1,0:T(8,128)(2,1)S(1)} %get-tuple-element.32), channel_id=1, source_target_pairs={{1,2},{3,4},{5,6},{2,1},{4,3},{6,5},{9,10},{11,12},{13,14},{10,9},... | collective-permute-start | bytes 1572872 | tf_op jit(solution)/shard_map/ppermute | solution.py:35
  40.2 4.5 %collective-permute-start.5 = (f32[464,128]{1,0:T(8,128)S(1)}, f32[464,128]{1,0:T(8,128)S(1)}, u32[]{:S(2)}, u32[]{:S(2)}) collective-permute-start(f32[464,128]{1,0:T(8,128)S(1)} %pad_maximum_fusion), channel_id=1, source_target_pairs={{0,1},{1,0},{2,3},{3,2},{4,5},{5,4},{6,7},{7,6},{8,9},{9,8},{10,11... | collective-permute-start | bytes 712712 | tf_op jit(solution)/shard_map/ppermute | solution.py:29
  44.7 5.1 %collective-permute-start.7 = (bf16[68,128]{1,0:T(8,128)(2,1)S(1)}, bf16[68,128]{1,0:T(8,128)(2,1)S(1)}, u32[]{:S(2)}, u32[]{:S(2)}) collective-permute-start(bf16[68,128]{1,0:T(8,128)(2,1)S(1)} %get-tuple-element.58), channel_id=1, source_target_pairs={{0,2},{1,3},{2,0},{3,1},{4,6},{5,7},{6,4},{7,5},{8,10},{9,11},{10,... | collective-permute-start | bytes 52232 | tf_op jit(solution)/shard_map/ppermute | solution.py:29
  46.7 4.7 %collective-permute-start.8 = (bf16[68,128]{1,0:T(8,128)(2,1)S(1)}, bf16[68,128]{1,0:T(8,128)(2,1)S(1)}, u32[]{:S(2)}, u32[]{:S(2)}) collective-permute-start(bf16[68,128]{1,0:T(8,128)(2,1)S(1)} %get-tuple-element.60), channel_id=1, source_target_pairs={{0,4},{1,5},{2,6},{3,7},{4,0},{5,1},{6,2},{7,3},{8,12},{9,13},{10,... | collective-permute-start | bytes 52232 | tf_op jit(solution)/shard_map/ppermute | solution.py:29
  48.9 5.7 %collective-permute-start.9 = (bf16[68,128]{1,0:T(8,128)(2,1)S(1)}, bf16[68,128]{1,0:T(8,128)(2,1)S(1)}, u32[]{:S(2)}, u32[]{:S(2)}) collective-permute-start(bf16[68,128]{1,0:T(8,128)(2,1)S(1)} %get-tuple-element.59), channel_id=1, source_target_pairs={{0,6},{1,7},{2,4},{3,5},{4,2},{5,3},{6,0},{7,1},{8,14},{9,15},{10,... | collective-permute-start | bytes 52232 | tf_op jit(solution)/shard_map/ppermute | solution.py:29
  49.2 8.9 %collective-permute-start.6 = (bf16[192,128]{1,0:T(8,128)(2,1)S(1)}, bf16[192,128]{1,0:T(8,128)(2,1)S(1)}, u32[]{:S(2)}, u32[]{:S(2)}) collective-permute-start(bf16[192,128]{1,0:T(8,128)(2,1)S(1)} %bitcast_convert_fusion), channel_id=1, source_target_pairs={{2,1},{4,3},{6,5},{10,9},{12,11},{14,13},{18,17},{20,19},{22,21},{... | collective-permute-start | bytes 147464 | tf_op jit(solution)/shard_map/ppermute | solution.py:452
  54.6 5.7 %collective-permute-start.10 = (f32[68,128]{1,0:T(8,128)S(1)}, f32[68,128]{1,0:T(8,128)S(1)}, u32[]{:S(2)}, u32[]{:S(2)}) collective-permute-start(f32[68,128]{1,0:T(8,128)S(1)} %fusion.5.refs_0_), channel_id=1, source_target_pairs={{0,8},{8,0},{16,24},{24,16},{1,9},{9,1},{17,25},{25,17},{2,10},{10... | collective-permute-start | bytes 104456 | tf_op jit(solution)/shard_map/ppermute | solution.py:29
  56.1 4.1 %collective-permute-start.11 = (f32[68,128]{1,0:T(8,128)S(1)}, f32[68,128]{1,0:T(8,128)S(1)}, u32[]{:S(2)}, u32[]{:S(2)}) collective-permute-start(f32[68,128]{1,0:T(8,128)S(1)} %fusion.5.refs_0_), channel_id=1, source_target_pairs={{0,16},{8,24},{16,0},{24,8},{1,17},{9,25},{17,1},{25,9},{2,18},{10... | collective-permute-start | bytes 104456 | tf_op jit(solution)/shard_map/ppermute | solution.py:29
  57.6 4.9 %collective-permute-start.12 = (f32[68,128]{1,0:T(8,128)S(1)}, f32[68,128]{1,0:T(8,128)S(1)}, u32[]{:S(2)}, u32[]{:S(2)}) collective-permute-start(f32[68,128]{1,0:T(8,128)S(1)} %fusion.5.refs_0_), channel_id=1, source_target_pairs={{0,24},{8,16},{16,8},{24,0},{1,25},{9,17},{17,9},{25,1},{2,26},{10... | collective-permute-start | bytes 104456 | tf_op jit(solution)/shard_map/ppermute | solution.py:29

commit v5 on v4

--- a/solution.py
+++ b/solution.py
@@ -61,7 +61,8 @@
 
 
 def prepare_kernel(
-    ids_ref, far_x, far_cot, long_ref, back_ref, ahead_ref, late_ref, near_x, near_cot, sems
+    ids_ref, far_x, far_cot, far_w, long_ref, back_ref, ahead_ref, late_ref,
+    near_x, near_cot, near_w, sems,
 ):
     held = near_cot.shape[1]
     copies = [
@@ -73,6 +74,7 @@
         for b in range(3)
     ]
     copies.append(pltpu.make_async_copy(far_cot.at[:, :held], near_cot, sems.at[3]))
+    copies.append(pltpu.make_async_copy(far_w, near_w, sems.at[4]))
     for copy in copies:
         copy.start()
     taps = long_ref.shape[1]
@@ -113,7 +115,7 @@
         copy.wait()
 
 
-def prepare(doc_ids, taps, inputs, cotangent, held):
+def prepare(doc_ids, taps, inputs, cotangent, weights, held):
     rows = inputs.shape[0]
     anywhere = pl.BlockSpec(memory_space=pl.ANY)
     shapes = [
@@ -126,13 +128,14 @@
         prepare_kernel,
         "prepare",
         (),
-        [whole(doc_ids.shape), anywhere, anywhere],
-        [whole(shape) for shape, _ in shapes] + [anywhere, anywhere],
+        [whole(doc_ids.shape), anywhere, anywhere, anywhere],
+        [whole(shape) for shape, _ in shapes] + [anywhere, anywhere, anywhere],
         [jax.ShapeDtypeStruct(*entry) for entry in shapes]
-        + [pltpu.VMEM((rows, 3 * held), BF), pltpu.VMEM((rows, held), BF)],
+        + [pltpu.VMEM((rows, 3 * held), BF), pltpu.VMEM((rows, held), BF)]
+        + [pltpu.VMEM(weights.shape, F32)],
         (1000000, 4000000),
-        [pltpu.SemaphoreType.DMA((4,))],
-    )(in_hbm(doc_ids), in_hbm(inputs), in_hbm(cotangent))
+        [pltpu.SemaphoreType.DMA((5,))],
+    )(in_hbm(doc_ids), in_hbm(inputs), in_hbm(cotangent), in_hbm(weights))
 
 
 def short_sum(weights, values, one, two):
@@ -536,8 +539,8 @@
     edge = short_taps - 1
     border = passed_along(projected[0, rows - edge :], "ctx", 1)
     filters = in_hbm(long_filter)
-    *masks, early_x, early_cot = prepare(
-        doc_ids, long_filter.shape[1], projected[0], grad_row, model_width // PARTS
+    *masks, early_x, early_cot, early_w = prepare(
+        doc_ids, long_filter.shape[1], projected[0], grad_row, short_filter, model_width // PARTS
     )
     inputs_row, grad_row, short_filter = [
         in_hbm(value) for value in (projected[0], grad_row, short_filter)
@@ -545,7 +548,7 @@
     gated = []
     for part in range(PARTS):
         mixed, chip, link = make_gates(
-            inputs_row if part else early_x, border, short_filter,
+            inputs_row if part else early_x, border, early_w,
             grad_row if part else early_cot, masks[1], part, PARTS,
         )
         link_in = linked(link, "ctx")
@@ -557,14 +560,14 @@
     for part, (mixed, chip_in, link_in) in enumerate(gated):
         done = make_long(
             chip_in, link_in, filters, masks, mixed, grad_row, inputs_row, border,
-            short_filter, part, PARTS, done,
+            early_w, part, PARTS, done,
         )
     block_out, head, tail, long_parts, short_parts, grad_inputs = done
     norm_scale = lax.axis_size("dp") * length
     scales = (math.sqrt(norm_scale), math.sqrt(norm_scale * (model_width // groups)))
     ahead, total, filter_total = owned_sums(short_parts, long_parts, head)
     ahead = ahead.reshape(-1, 2 * PIECE, LANES)
-    grad_inputs = finish_last_rows(grad_inputs, tail, ahead, short_filter, masks[3])
+    grad_inputs = finish_last_rows(grad_inputs, tail, ahead, early_w, masks[3])
     if filter_total is None:
         held = 3 * model_width // (PIECE * LANES * lax.axis_size("ctx"))
         grad_short, grad_long = finish(window_parts(total), held, scales)

time: 63.5 us -> 62.4 us (0.983)
  Pallas kernels: 31.4 us -> 30.3 us
    pallas_call x2, Pallas kernels: 4.77 us -> 3.81 us  [make_gates(): call(functools.partial(gate_kernel, first=first, steps=steps), 'gates', (...]
  transfers between devices with their start and end apart: 13 -> 13, of which waited for: 4 -> 4; matrix products, arithmetic and copies ran while one was open for 0% -> 0% of each run, Pallas kernels for 28% -> 29%
where the time goes in v5:
time: 62.4 us; the launch traced here: 62.1 us
  Pallas kernels  30.3 us (49%)
  starting transfers between devices  21.7 us (35%)
  waiting for transfers between devices  8.11 us (13%)
  local copies, waits for them, and re-layouts  1.05 us (2%)
  between operations  0.82 us (1%)
    pallas_call x2, Pallas kernels, make_long(): call(functools.partial(long_kernel, first=first, steps=steps, held=held),...  21.5 us
    ppermute x9, starting transfers between devices, swapped(): lax.ppermute(value, axis, [(source, source ^ bits) for source in range(co...  16.4 us
    ppermute x9, waiting for transfers between devices, swapped(): lax.ppermute(value, axis, [(source, source ^ bits) for source in range(co...  8.1 us
    pallas_call x2, Pallas kernels, make_gates(): call(functools.partial(gate_kernel, first=first, steps=steps), 'gates', (...  3.81 us
    ppermute x1, starting transfers between devices, passed_along(): lax.ppermute(value, axis, [(source, source + steps) for source in range(i...  2.36 us
    pallas_call x1, Pallas kernels, prepare(): call(prepare_kernel, 'prepare', (), [whole(doc_ids.shape), anywhere, anyw...  2.32 us
    ppermute x2, starting transfers between devices, linked(): return lax.ppermute(value, axis, pairs + [(b, a) for a, b in pairs])  2.32 us
    pallas_call x1, Pallas kernels, finish_last_rows(): call(last_rows_kernel, 'last_rows', (1,), [whole(value.shape) for value i...  1.99 us
  transfers between devices with their start and end apart: 13, of which 4 were waited for; matrix products, arithmetic and copies ran while one was open for 0% of the time, Pallas kernels for 29%

profile of v5, /device:TPU:0, one launch (start us, length us, event | category | flops | bytes accessed | tf_op | source)
XLA Modules:
  0.0 62.1 jit_solution(14282120997886253396)
XLA Ops:
  0.6 1.0 %slice_bitcast_fusion = bf16[2,12288]{1,0:T(2,128)(2,1)S(1)} fusion(bf16[1,128,12288]{2,1,0:T(8,128)(2,1)} %param.5), kind=kLoop, calls=%fused_computation.11 | loop fusion | bytes 98304 | tf_op jit(solution)/shard_map/squeeze | solution.py:540
  1.6 2.4 %collective-permute-start = (bf16[2,12288]{1,0:T(2,128)(2,1)S(1)}, bf16[2,12288]{1,0:T(2,128)(2,1)S(1)}, u32[]{:S(2)}, u32[]{:S(2)}) collective-permute-start(bf16[2,12288]{1,0:T(2,128)(2,1)S(1)} %slice_bitcast_fusion), channel_id=1, source_target_pairs={{0,1},{1,2},{2,3},{3,4},{4,5},{5,6},{6,7},{8,9},{9,10},{10,11},{11... | collective-permute-start | bytes 147464 | tf_op jit(solution)/shard_map/ppermute | solution.py:24
  4.0 2.3 %prepare.1 = (bf16[4,128,128]{2,1,0:T(8,128)(2,1)S(1)}, bf16[256,144]{1,0:T(8,128)(2,1)S(1)}, bf16[256,128]{1,0:T(8,128)(2,1)S(1)}, f32[2,8,128]{2,1,0:T(8,128)S...) custom-call(s32[1,1024]{1,0:T(1,128)} %ids_ref.1, ...), custom_call_target="tpu_custom_call" | custom-call | flops 1000000 | bytes 4000000 | tf_op jit(solution)/shard_map/prepare/pallas_call | solution.py:127
  6.3 0.0 collective-permute-done.edge_ref
  6.3 1.2 %gates.3 = (bf16[3,128,2048]{2,1,0:T(8,128)(2,1)S(1)}, bf16[128,2048]{1,0:T(8,128)(2,1)S(1)}, bf16[128,2048]{1,0:T(8,128)(2,1)S(1)}) custom-call(bf16[128,6144]{1,0:T(8,128)(2,1)S(1)} %get-tuple-element.38.xq.xk.xv, bf16[128,6144]{1,0:T(8,128)(2,1)S(1)} %get-tuple-element.38.xq.xk.xv, bf16[128,6144]{1,0:T(8,128)(2,1)S(1)} %get-tuple-element.38.xq.xk.xv, ...), custom_call_target="tpu_custom_call" | custom-call | flops 805306368 | bytes 4718592 | tf_op jit(solution)/shard_map/gates/pallas_call | solution.py:186
  7.5 2.7 %collective-permute-start.3 = (bf16[128,2048]{1,0:T(8,128)(2,1)S(1)}, bf16[128,2048]{1,0:T(8,128)(2,1)}, u32[]{:S(2)}, u32[]{:S(2)}) collective-permute-start(bf16[128,2048]{1,0:T(8,128)(2,1)S(1)} %get-tuple-element.40), channel_id=1, source_target_pairs={{0,1},{1,0},{2,3},{3,2},{4,5},{5,4},{6,7},{7,6},{8,9},{9,8},{10,11... | collective-permute-start | bytes 1572872 | tf_op jit(solution)/shard_map/ppermute | solution.py:29
  10.2 1.5 %collective-permute-start.4 = (bf16[128,2048]{1,0:T(8,128)(2,1)S(1)}, bf16[128,2048]{1,0:T(8,128)(2,1)}, u32[]{:S(2)}, u32[]{:S(2)}) collective-permute-start(bf16[128,2048]{1,0:T(8,128)(2,1)S(1)} %get-tuple-element.41), channel_id=1, source_target_pairs={{1,2},{3,4},{5,6},{2,1},{4,3},{6,5},{9,10},{11,12},{13,14},{10,9},... | collective-permute-start | bytes 1572872 | tf_op jit(solution)/shard_map/ppermute | solution.py:35
  11.7 2.7 %gates.2 = (bf16[3,128,2048]{2,1,0:T(8,128)(2,1)S(1)}, bf16[128,2048]{1,0:T(8,128)(2,1)S(1)}, bf16[128,2048]{1,0:T(8,128)(2,1)S(1)}) custom-call(bf16[128,12288]{1,0:T(8,128)(2,1)} %bitcast.30, bf16[128,12288]{1,0:T(8,128)(2,1)} %bitcast.31, bf16[128,12288]{1,0:T(8,128)(2,1)} %bitcast.32, bf16[2,12288]{1,0:T(2,128)(2,1)S(1)} %collective-permute-done.edge_ref, ...), custom_call_target="tpu_custom_call" | custom-call | flops 805306368 | bytes 4718592 | tf_op jit(solution)/shard_map/gates/pallas_call | solution.py:186
  14.3 2.2 %collective-permute-start.1 = (bf16[128,2048]{1,0:T(8,128)(2,1)S(1)}, bf16[128,2048]{1,0:T(8,128)(2,1)S(1)}, u32[]{:S(2)}, u32[]{:S(2)}) collective-permute-start(bf16[128,2048]{1,0:T(8,128)(2,1)S(1)} %get-tuple-element.33), channel_id=1, source_target_pairs={{0,1},{1,0},{2,3},{3,2},{4,5},{5,4},{6,7},{7,6},{8,9},{9,8},{10,11... | collective-permute-start | bytes 1572872 | tf_op jit(solution)/shard_map/ppermute | solution.py:29
  16.6 0.9 %collective-permute-start.2 = (bf16[128,2048]{1,0:T(8,128)(2,1)S(1)}, bf16[128,2048]{1,0:T(8,128)(2,1)S(1)}, u32[]{:S(2)}, u32[]{:S(2)}) collective-permute-start(bf16[128,2048]{1,0:T(8,128)(2,1)S(1)} %get-tuple-element.34), channel_id=1, source_target_pairs={{1,2},{3,4},{5,6},{2,1},{4,3},{6,5},{9,10},{11,12},{13,14},{10,9},... | collective-permute-start | bytes 1572872 | tf_op jit(solution)/shard_map/ppermute | solution.py:35
  17.5 0.0 collective-permute-done.3.chip_in_ref
  17.5 0.0 collective-permute-done.4.link_in_ref
  17.5 10.8 %long_parts.2 = (bf16[128,4096]{1,0:T(8,128)(2,1)}, f32[3,8,8,128]{3,2,1,0:T(8,128)S(1)}, f32[3,8,4096]{2,1,0:T(8,128)S(1)}, f32[256,128]{1,0:T(8,128)S(1)}, f32...) custom-call(bf16[128,2048]{1,0:T(8,128)(2,1)} %collective-permute-done.3.chip_in_ref, ...), custom_call_target="tpu_custom_call" | custom-call | flops 6442450944 | bytes 12582912 | tf_op jit(solution)/shard_map/long_parts/pallas_call | solution.py:379
  28.3 0.0 collective-permute-done.1.chip_in_ref
  28.3 0.0 collective-permute-done.2.link_in_ref
  28.3 10.7 %long_parts.3 = (bf16[128,4096]{1,0:T(8,128)(2,1)}, f32[3,8,8,128]{3,2,1,0:T(8,128)S(1)}, f32[3,8,4096]{2,1,0:T(8,128)S(1)}, f32[256,128]{1,0:T(8,128)S(1)}, f32...) custom-call(bf16[128,2048]{1,0:T(8,128)(2,1)S(1)} %collective-permut, ...), custom_call_target="tpu_custom_call", output_to_operand_aliasing={{0}: (13, {}), {1}: (14, {}), {2}: (15, {}), {3}: (16, {}),... | custom-call | flops 6442450944 | bytes 12582912 | tf_op jit(solution)/shard_map/long_parts/pallas_call | solution.py:379
  39.1 3.4 %collective-permute-start.5 = (f32[464,128]{1,0:T(8,128)S(1)}, f32[464,128]{1,0:T(8,128)S(1)}, u32[]{:S(2)}, u32[]{:S(2)}) collective-permute-start(f32[464,128]{1,0:T(8,128)S(1)} %pad_maximum_fusion), channel_id=1, source_target_pairs={{0,1},{1,0},{2,3},{3,2},{4,5},{5,4},{6,7},{7,6},{8,9},{9,8},{10,11... | collective-permute-start | bytes 712712 | tf_op jit(solution)/shard_map/ppermute | solution.py:29
  42.5 1.1 %collective-permute-done.5 = f32[464,128]{1,0:T(8,128)S(1)} collective-permute-done((f32[464,128]{1,0:T(8,128)S(1)}, f32[464,128]{1,0:T(8,128)S(1)}, u32[]{:S(2)}, u32[]{:S(2)}) %collective-permute-start.5) | collective-permute-done | bytes 237600 | tf_op jit(solution)/shard_map/ppermute | solution.py:29
  43.7 2.0 %collective-permute-start.7 = (bf16[68,128]{1,0:T(8,128)(2,1)S(1)}, bf16[68,128]{1,0:T(8,128)(2,1)S(1)}, u32[]{:S(2)}, u32[]{:S(2)}) collective-permute-start(bf16[68,128]{1,0:T(8,128)(2,1)S(1)} %get-tuple-element.60), channel_id=1, source_target_pairs={{0,2},{1,3},{2,0},{3,1},{4,6},{5,7},{6,4},{7,5},{8,10},{9,11},{10,... | collective-permute-start | bytes 52232 | tf_op jit(solution)/shard_map/ppermute | solution.py:29
  45.7 2.1 %collective-permute-start.8 = (bf16[68,128]{1,0:T(8,128)(2,1)S(1)}, bf16[68,128]{1,0:T(8,128)(2,1)S(1)}, u32[]{:S(2)}, u32[]{:S(2)}) collective-permute-start(bf16[68,128]{1,0:T(8,128)(2,1)S(1)} %get-tuple-element.62), channel_id=1, source_target_pairs={{0,4},{1,5},{2,6},{3,7},{4,0},{5,1},{6,2},{7,3},{8,12},{9,13},{10,... | collective-permute-start | bytes 52232 | tf_op jit(solution)/shard_map/ppermute | solution.py:29
  47.8 0.4 collective-permute-start.9
  48.2 0.7 %collective-permute-start.6 = (bf16[192,128]{1,0:T(8,128)(2,1)S(1)}, bf16[192,128]{1,0:T(8,128)(2,1)S(1)}, u32[]{:S(2)}, u32[]{:S(2)}) collective-permute-start(bf16[192,128]{1,0:T(8,128)(2,1)S(1)} %bitcast_convert_fusion), channel_id=1, source_target_pairs={{2,1},{4,3},{6,5},{10,9},{12,11},{14,13},{18,17},{20,19},{22,21},{... | collective-permute-start | bytes 147464 | tf_op jit(solution)/shard_map/ppermute | solution.py:455
  48.9 0.0 collective-permute-done.7
  48.9 1.5 %collective-permute-done.8 = bf16[68,128]{1,0:T(8,128)(2,1)S(1)} collective-permute-done((bf16[68,128]{1,0:T(8,128)(2,1)S(1)}, bf16[68,128]{1,0:T(8,128)(2,1)S(1)}, u32[]{:S(2)}, u32[]{:S(2)}) %collective-permute-start.8) | collective-permute-done | bytes 17440 | tf_op jit(solution)/shard_map/ppermute | solution.py:29
  50.4 3.1 %collective-permute-done.9 = bf16[68,128]{1,0:T(8,128)(2,1)S(1)} collective-permute-done((bf16[68,128]{1,0:T(8,128)(2,1)S(1)}, bf16[68,128]{1,0:T(8,128)(2,1)S(1)}, u32[]{:S(2)}, u32[]{:S(2)}) %collective-permute-start.9) | collective-permute-done | bytes 17440 | tf_op jit(solution)/shard_map/ppermute | solution.py:29
  53.5 1.6 %collective-permute-start.10 = (f32[68,128]{1,0:T(8,128)S(1)}, f32[68,128]{1,0:T(8,128)S(1)}, u32[]{:S(2)}, u32[]{:S(2)}) collective-permute-start(f32[68,128]{1,0:T(8,128)S(1)} %fusion.5.refs_0_), channel_id=1, source_target_pairs={{0,8},{8,0},{16,24},{24,16},{1,9},{9,1},{17,25},{25,17},{2,10},{10... | collective-permute-start | bytes 104456 | tf_op jit(solution)/shard_map/ppermute | solution.py:29
  55.1 1.5 %collective-permute-start.11 = (f32[68,128]{1,0:T(8,128)S(1)}, f32[68,128]{1,0:T(8,128)S(1)}, u32[]{:S(2)}, u32[]{:S(2)}) collective-permute-start(f32[68,128]{1,0:T(8,128)S(1)} %fusion.5.refs_0_), channel_id=1, source_target_pairs={{0,16},{8,24},{16,0},{24,8},{1,17},{9,25},{17,1},{25,9},{2,18},{10... | collective-permute-start | bytes 104456 | tf_op jit(solution)/shard_map/ppermute | solution.py:29
  56.6 0.5 collective-permute-start.12
  57.1 0.0 collective-permute-done.6
  57.1 2.0 %last_rows.1 = bf16[128,12288]{1,0:T(8,128)(2,1)} custom-call(f32[3,8,4096]{2,1,0:T(8,128)S(1)} %get-tuple-element.50.tail_ref, f32[24,8,128]{2,1,0:T(8,128)S(1)} %fusion.4.ahead_ref, f32[3,12288]{1,0:T(4,128)S(1)} %get-tuple-element.31.w_ref, f32[2,8,128]{2,1,0:T(8,128)S(1)} %get-tuple-element.54.late_ref, ...), custom_call_target="tpu_custom_call", output_to_operand_aliasing={{}: (4, {})} | custom-call | flops 1000000 | bytes 2000000 | tf_op jit(solution)/shard_map/last_rows/pallas_call | solution.py:434
  59.1 0.0 collective-permute-done.10.refs_1_
  59.1 0.0 collective-permute-done.11.refs_2_
  59.1 2.4 %collective-permute-done.12.refs_3_ = f32[68,128]{1,0:T(8,128)S(1)} collective-permute-done((f32[68,128]{1,0:T(8,128)S(1)}, f32[68,128]{1,0:T(8,128)S(1)}, u32[]{:S(2)}, u32[]{:S(2)}) %collective-permute-start.12) | collective-permute-done | bytes 34848 | tf_op jit(solution)/shard_map/ppermute | solution.py:29
  61.4 0.6 %finish.1 = (f32[3,1536]{1,0:T(4,128)}, f32[32,128]{1,0:T(8,128)}) custom-call(f32[68,128]{1,0:T(8,128)S(1)} %fusion.5.refs_0_, f32[68,128]{1,0:T(8,128)S(1)} %collective-permute-done.10.refs_1_, f32[68,128]{1,0:T(8,128)S(1)} %collective-permute-done.11.refs_2_, f32[68,128]{1,0:T(8,128)S(1)} %collective-permute-done.12.refs_3_), custom_call_target="tpu_custom_call" | custom-call | flops 100000 | bytes 400000 | tf_op jit(solution)/shard_map/finish/pallas_call | solution.py:521
  (11 shorter events, 0.2 us)
Async XLA Ops:
  1.6 4.7 %collective-permute-start = (bf16[2,12288]{1,0:T(2,128)(2,1)S(1)}, bf16[2,12288]{1,0:T(2,128)(2,1)S(1)}, u32[]{:S(2)}, u32[]{:S(2)}) collective-permute-start(bf16[2,12288]{1,0:T(2,128)(2,1)S(1)} %slice_bitcast_fusion), channel_id=1, source_target_pairs={{0,1},{1,2},{2,3},{3,4},{4,5},{5,6},{6,7},{8,9},{9,10},{10,11},{11... | collective-permute-start | bytes 147464 | tf_op jit(solution)/shard_map/ppermute | solution.py:24
  7.5 10.0 %collective-permute-start.3 = (bf16[128,2048]{1,0:T(8,128)(2,1)S(1)}, bf16[128,2048]{1,0:T(8,128)(2,1)}, u32[]{:S(2)}, u32[]{:S(2)}) collective-permute-start(bf16[128,2048]{1,0:T(8,128)(2,1)S(1)} %get-tuple-element.40), channel_id=1, source_target_pairs={{0,1},{1,0},{2,3},{3,2},{4,5},{5,4},{6,7},{7,6},{8,9},{9,8},{10,11... | collective-permute-start | bytes 1572872 | tf_op jit(solution)/shard_map/ppermute | solution.py:29
  10.2 7.2 %collective-permute-start.4 = (bf16[128,2048]{1,0:T(8,128)(2,1)S(1)}, bf16[128,2048]{1,0:T(8,128)(2,1)}, u32[]{:S(2)}, u32[]{:S(2)}) collective-permute-start(bf16[128,2048]{1,0:T(8,128)(2,1)S(1)} %get-tuple-element.41), channel_id=1, source_target_pairs={{1,2},{3,4},{5,6},{2,1},{4,3},{6,5},{9,10},{11,12},{13,14},{10,9},... | collective-permute-start | bytes 1572872 | tf_op jit(solution)/shard_map/ppermute | solution.py:35
  14.3 13.9 %collective-permute-start.1 = (bf16[128,2048]{1,0:T(8,128)(2,1)S(1)}, bf16[128,2048]{1,0:T(8,128)(2,1)S(1)}, u32[]{:S(2)}, u32[]{:S(2)}) collective-permute-start(bf16[128,2048]{1,0:T(8,128)(2,1)S(1)} %get-tuple-element.33), channel_id=1, source_target_pairs={{0,1},{1,0},{2,3},{3,2},{4,5},{5,4},{6,7},{7,6},{8,9},{9,8},{10,11... | collective-permute-start | bytes 1572872 | tf_op jit(solution)/shard_map/ppermute | solution.py:29
  16.6 11.7 %collective-permute-start.2 = (bf16[128,2048]{1,0:T(8,128)(2,1)S(1)}, bf16[128,2048]{1,0:T(8,128)(2,1)S(1)}, u32[]{:S(2)}, u32[]{:S(2)}) collective-permute-start(bf16[128,2048]{1,0:T(8,128)(2,1)S(1)} %get-tuple-element.34), channel_id=1, source_target_pairs={{1,2},{3,4},{5,6},{2,1},{4,3},{6,5},{9,10},{11,12},{13,14},{10,9},... | collective-permute-start | bytes 1572872 | tf_op jit(solution)/shard_map/ppermute | solution.py:35
  39.1 4.5 %collective-permute-start.5 = (f32[464,128]{1,0:T(8,128)S(1)}, f32[464,128]{1,0:T(8,128)S(1)}, u32[]{:S(2)}, u32[]{:S(2)}) collective-permute-start(f32[464,128]{1,0:T(8,128)S(1)} %pad_maximum_fusion), channel_id=1, source_target_pairs={{0,1},{1,0},{2,3},{3,2},{4,5},{5,4},{6,7},{7,6},{8,9},{9,8},{10,11... | collective-permute-start | bytes 712712 | tf_op jit(solution)/shard_map/ppermute | solution.py:29
  43.7 5.1 %collective-permute-start.7 = (bf16[68,128]{1,0:T(8,128)(2,1)S(1)}, bf16[68,128]{1,0:T(8,128)(2,1)S(1)}, u32[]{:S(2)}, u32[]{:S(2)}) collective-permute-start(bf16[68,128]{1,0:T(8,128)(2,1)S(1)} %get-tuple-element.60), channel_id=1, source_target_pairs={{0,2},{1,3},{2,0},{3,1},{4,6},{5,7},{6,4},{7,5},{8,10},{9,11},{10,... | collective-permute-start | bytes 52232 | tf_op jit(solution)/shard_map/ppermute | solution.py:29
  45.7 4.7 %collective-permute-start.8 = (bf16[68,128]{1,0:T(8,128)(2,1)S(1)}, bf16[68,128]{1,0:T(8,128)(2,1)S(1)}, u32[]{:S(2)}, u32[]{:S(2)}) collective-permute-start(bf16[68,128]{1,0:T(8,128)(2,1)S(1)} %get-tuple-element.62), channel_id=1, source_target_pairs={{0,4},{1,5},{2,6},{3,7},{4,0},{5,1},{6,2},{7,3},{8,12},{9,13},{10,... | collective-permute-start | bytes 52232 | tf_op jit(solution)/shard_map/ppermute | solution.py:29
  47.8 5.7 %collective-permute-start.9 = (bf16[68,128]{1,0:T(8,128)(2,1)S(1)}, bf16[68,128]{1,0:T(8,128)(2,1)S(1)}, u32[]{:S(2)}, u32[]{:S(2)}) collective-permute-start(bf16[68,128]{1,0:T(8,128)(2,1)S(1)} %get-tuple-element.61), channel_id=1, source_target_pairs={{0,6},{1,7},{2,4},{3,5},{4,2},{5,3},{6,0},{7,1},{8,14},{9,15},{10,... | collective-permute-start | bytes 52232 | tf_op jit(solution)/shard_map/ppermute | solution.py:29
  48.2 8.8 %collective-permute-start.6 = (bf16[192,128]{1,0:T(8,128)(2,1)S(1)}, bf16[192,128]{1,0:T(8,128)(2,1)S(1)}, u32[]{:S(2)}, u32[]{:S(2)}) collective-permute-start(bf16[192,128]{1,0:T(8,128)(2,1)S(1)} %bitcast_convert_fusion), channel_id=1, source_target_pairs={{2,1},{4,3},{6,5},{10,9},{12,11},{14,13},{18,17},{20,19},{22,21},{... | collective-permute-start | bytes 147464 | tf_op jit(solution)/shard_map/ppermute | solution.py:455
  53.5 5.6 %collective-permute-start.10 = (f32[68,128]{1,0:T(8,128)S(1)}, f32[68,128]{1,0:T(8,128)S(1)}, u32[]{:S(2)}, u32[]{:S(2)}) collective-permute-start(f32[68,128]{1,0:T(8,128)S(1)} %fusion.5.refs_0_), channel_id=1, source_target_pairs={{0,8},{8,0},{16,24},{24,16},{1,9},{9,1},{17,25},{25,17},{2,10},{10... | collective-permute-start | bytes 104456 | tf_op jit(solution)/shard_map/ppermute | solution.py:29
  55.1 4.0 %collective-permute-start.11 = (f32[68,128]{1,0:T(8,128)S(1)}, f32[68,128]{1,0:T(8,128)S(1)}, u32[]{:S(2)}, u32[]{:S(2)}) collective-permute-start(f32[68,128]{1,0:T(8,128)S(1)} %fusion.5.refs_0_), channel_id=1, source_target_pairs={{0,16},{8,24},{16,0},{24,8},{1,17},{9,25},{17,1},{25,9},{2,18},{10... | collective-permute-start | bytes 104456 | tf_op jit(solution)/shard_map/ppermute | solution.py:29
  56.6 4.9 %collective-permute-start.12 = (f32[68,128]{1,0:T(8,128)S(1)}, f32[68,128]{1,0:T(8,128)S(1)}, u32[]{:S(2)}, u32[]{:S(2)}) collective-permute-start(f32[68,128]{1,0:T(8,128)S(1)} %fusion.5.refs_0_), channel_id=1, source_target_pairs={{0,24},{8,16},{16,8},{24,0},{1,25},{9,17},{17,9},{25,1},{2,26},{10... | collective-permute-start | bytes 104456 | tf_op jit(solution)/shard_map/ppermute | solution.py:29
